TPU v7x, 32 devices: a whole 2x2x4 slice. The times are simulated.
32 devices in a mesh: rows: 4 (over z), cols: 8 (over y, x, core).
Axes of the slice: x: 2, y: 2, z: 4, core: 2. Of those that a mesh axis runs over, the one named last changes fastest.
Arguments:
- tokens: bfloat16 [32, 256, 192], P('rows', 'cols'), may hold values from -60 to 60
- region_ids: int32 [32, 256], P('rows', 'cols'), may hold values from 0 to 2
- upper_rim: bfloat16 [4, 256, 192], P(None, 'cols'), may hold values from -60 to 60
- upper_ids: int32 [4, 256], P(None, 'cols'), may hold values from 0 to 2
- lower_rim: bfloat16 [4, 256, 192], P(None, 'cols'), may hold values from -60 to 60
- lower_ids: int32 [4, 256], P(None, 'cols'), may hold values from 0 to 2
- cotangent: bfloat16 [32, 256, 192], P('rows', 'cols'), may hold values from -6 to 6
- qkv_weight: bfloat16 [2, 192, 576], replicated, may hold values from -0.4375 to 0.4375
- proj_weight: bfloat16 [2, 192, 192], replicated, may hold values from -0.4375 to 0.4375
- inner_weight: bfloat16 [2, 192, 768], replicated, may hold values from -0.4375 to 0.4375
- outer_weight: bfloat16 [2, 768, 192], replicated, may hold values from -0.21875 to 0.21875
- bias_table: float32 [2, 225, 6], replicated, may hold values from -4 to 400
Outputs:
- token_grad: bfloat16 [32, 256, 192], P('rows', 'cols')
- qkv_grad: float32 [2, 192, 576], P(None, 'rows', 'cols')
- proj_grad: float32 [2, 192, 192], P(None, 'rows', 'cols')
- inner_grad: float32 [2, 192, 768], P(None, 'rows', 'cols')
- outer_grad: float32 [2, 768, 192], P(None, 'rows', 'cols')
- table_grad: float32 [2, 225, 6], replicated
All inputs are finite; a program needn't handle non-finite values.
Results may differ from a plain program's by a relative error of at most 0.03.
Values may be sent and summed in bfloat16 or wider, within the bound.
No kernel may reach another device: no remote copies, remote signals or barrier semaphores. Data moves between devices by JAX's collectives and lax.ppermute only.
A program may use at most 64 MiB of HBM per device.

v0:
```python
import functools
import math

import jax
import jax.numpy as jnp
from jax import lax
from jax.experimental import pallas as pl
from jax.experimental.pallas import tpu as pltpu
from jax.sharding import PartitionSpec as P

WIN = 8
HALF = 4
TOK = WIN * WIN
SPAN = 2 * WIN - 1
LANES = 128
EPS = 1e-05
MASKED = -1000000000.0
F32 = jnp.float32
BF16 = jnp.bfloat16
VMEM_LIMIT = 40 * 1024 * 1024


def nn(left, right):
    return lax.dot_general(left, right, (((1,), (0,)), ((), ())), preferred_element_type=F32)


def nt(left, right):
    return lax.dot_general(left, right, (((1,), (1,)), ((), ())), preferred_element_type=F32)


def tn(left, right):
    return lax.dot_general(left, right, (((0,), (0,)), ((), ())), preferred_element_type=F32)


def iota(shape, dim):
    return lax.broadcasted_iota(jnp.int32, shape, dim)


def ones_where(condition):
    return jnp.where(condition, 1.0, 0.0).astype(BF16)


def norm(values):
    shifted = values - jnp.mean(values, axis=-1, keepdims=True)
    inverse = lax.rsqrt(jnp.mean(shifted * shifted, axis=-1, keepdims=True) + EPS)
    return shifted * inverse, inverse


def norm_back(unit, inverse, grad):
    mean_grad = jnp.mean(grad, axis=-1, keepdims=True)
    mean_unit = jnp.mean(grad * unit, axis=-1, keepdims=True)
    return inverse * (grad - mean_grad - unit * mean_unit)


def to_windows(grid):
    rows, cols, channels = grid.shape
    return jnp.concatenate(
        [
            grid[a : a + WIN, b : b + WIN].reshape(TOK, channels)
            for a in range(0, rows, WIN)
            for b in range(0, cols, WIN)
        ],
        axis=0,
    )


def from_windows(framed, rows, cols):
    per_band = cols // WIN
    bands = []
    for a in range(rows // WIN):
        pieces = [
            framed[(a * per_band + b) * TOK : (a * per_band + b + 1) * TOK].reshape(WIN, WIN, -1)
            for b in range(per_band)
        ]
        bands.append(jnp.concatenate(pieces, axis=1))
    return jnp.concatenate(bands, axis=0) if len(bands) > 1 else bands[0]


def lane_tiles(channels, size):
    tiles = []
    for start in range(0, channels, LANES):
        width = min(LANES, channels - start)
        tiles.append((start, width, start // size * TOK, (start + width) // size * TOK))
    return tiles


def spread(part, size):
    lane = iota((1, part.shape[1]), 1)
    copies = [
        part * ones_where((lane >= first) & (lane < first + size))
        for first in range(0, part.shape[1], size)
    ]
    return jnp.concatenate(copies, axis=0)


def collect(stacked, size):
    width = stacked.shape[1]
    heads = width // size
    lane = iota((TOK, width), 1)
    total = stacked[(heads - 1) * TOK :]
    for head in reversed(range(heads - 1)):
        total = jnp.where(lane < (head + 1) * size, stacked[head * TOK : (head + 1) * TOK], total)
    return total


def attend(query, key, value, bias, same, size):
    scale = size ** (-0.5)
    tiles = lane_tiles(query.shape[1], size)
    parts = []
    for start, width, first, last in tiles:
        scores = nt(key[:, start : start + width], spread(query[:, start : start + width], size))
        for at in range(first, last, LANES):
            part = scores[:, at - first : at - first + LANES] * scale + bias[:, at : at + LANES]
            part = jnp.where(same, part, MASKED)
            exponent = jnp.exp(part - jnp.max(part, axis=0, keepdims=True))
            parts.append(exponent * (1.0 / jnp.sum(exponent, axis=0, keepdims=True)))
    probs = jnp.concatenate(parts, axis=1)
    low = probs.astype(BF16)
    mix = [
        collect(tn(low[:, first:last], value[:, start : start + width]), size)
        for start, width, first, last in tiles
    ]
    return probs, jnp.concatenate(mix, axis=1).astype(BF16)


def attend_back(query, key, value, probs, grad_mix, size):
    scale = size ** (-0.5)
    grads = ([], [], [])
    terms = []
    for start, width, first, last in lane_tiles(query.shape[1], size):
        part = slice(start, start + width)
        grad_heads = spread(grad_mix[:, part], size)
        chance = probs[:, first:last]
        grad_probs = nt(value[:, part], grad_heads)
        term = chance * (grad_probs - jnp.sum(grad_probs * chance, axis=0, keepdims=True))
        low = term.astype(BF16)
        grads[0].append(collect(tn(low, key[:, part]), size) * scale)
        grads[1].append(nn(low, spread(query[:, part], size)) * scale)
        grads[2].append(nn(chance.astype(BF16), grad_heads))
        terms.append(term)
    return [jnp.concatenate(g, axis=1).astype(BF16) for g in grads], jnp.concatenate(terms, axis=1)


def same_region(ids):
    rows, cols = ids.shape
    masks = []
    row = iota((TOK, cols), 0)
    col = iota((TOK, cols), 1)
    lift = ones_where(iota((TOK, WIN), 0) // WIN == iota((TOK, WIN), 1))
    ones = jnp.ones((cols, LANES), BF16)
    for a in range(0, rows, WIN):
        band = ids[a : a + WIN].astype(BF16)
        lifted = nn(lift, band)
        for b in range(0, cols, WIN):
            picked = jnp.where(col == b + (row & (WIN - 1)), lifted, 0.0).astype(BF16)
            down = nn(picked, ones)
            tiled = nn(
                band,
                ones_where(iota((cols, LANES), 0) == b + (iota((cols, LANES), 1) & (WIN - 1))),
            )
            own = iota((WIN, LANES), 0) == ((iota((WIN, LANES), 1) // WIN) & (WIN - 1))
            across = jnp.sum(jnp.where(own, tiled, 0.0), axis=0, keepdims=True)
            masks.append(down == across)
    return masks


def split(values, count):
    parts = []
    for _ in range(count):
        low = values.astype(BF16)
        parts.append(low)
        values = values - low.astype(F32)
    return parts


def offset_rows(length):
    place = iota((length, 2 * LANES), 0)
    row = (place * 4370) >> 16
    return ones_where(iota((length, 2 * LANES), 1) == 2 * WIN * row + place - SPAN * row)


def offset_places():
    lane = iota((2 * LANES, WIN * LANES), 1)
    row = ((lane >> 3) & (WIN - 1)) - (lane >> 7) + WIN - 1
    return ones_where(iota((2 * LANES, WIN * LANES), 0) == 2 * WIN * row + (lane & (WIN - 1)))


def expand_bias(table):
    length, heads = table.shape
    onehot = offset_rows(length)
    rows = sum(tn(part, onehot) for part in split(table, 3))
    base = jnp.concatenate(
        [jnp.broadcast_to(rows[h : h + 1], (WIN, 2 * LANES)) for h in range(heads)], axis=0
    )
    place = iota(base.shape, 0) & (WIN - 1)
    rolled = base
    for c in range(WIN - 1):
        rolled = jnp.where(place == c, pltpu.roll(base, c + 2 * LANES - WIN + 1, 1), rolled)
    places = offset_places()
    spreaded = sum(nn(part, places) for part in split(rolled, 3))
    left = iota((WIN, LANES), 1) < TOK
    columns = []
    for h in range(0, heads, 2):
        pieces = [
            jnp.where(
                left,
                spreaded[h * WIN : (h + 1) * WIN, r * LANES : (r + 1) * LANES],
                spreaded[(h + 1) * WIN : (h + 2) * WIN, r * LANES : (r + 1) * LANES],
            )
            for r in range(WIN)
        ]
        columns.append(jnp.concatenate(pieces, axis=0))
    return jnp.concatenate(columns, axis=1)


def fold_bias(grad):
    heads = grad.shape[1] // TOK
    left = iota((WIN, LANES), 1) < TOK
    rows = []
    for h in range(heads):
        at = h // 2 * LANES
        pieces = []
        for r in range(WIN):
            piece = grad[r * WIN : (r + 1) * WIN, at : at + LANES]
            pieces.append(jnp.where(left, piece, 0.0) if h % 2 == 0 else jnp.where(left, 0.0, piece))
        rows.append(jnp.concatenate(pieces, axis=1))
    stacked = jnp.concatenate(rows, axis=0)
    places = offset_places()
    folded = sum(nt(part, places) for part in split(stacked, 3))
    place = iota(folded.shape, 0) & (WIN - 1)
    rolled = folded
    for c in range(WIN - 1):
        rolled = jnp.where(place == c, pltpu.roll(folded, WIN - 1 - c, 1), rolled)
    sums = [
        jnp.sum(rolled[h * WIN : (h + 1) * WIN], axis=0, keepdims=True) for h in range(heads)
    ]
    sums.append(jnp.zeros((WIN - heads, 2 * LANES), F32))
    return jnp.concatenate(sums, axis=0)


def table_rows(table, width):
    parts = [part.astype(F32) for part in split(table, 2)]
    if width == LANES:
        return jnp.concatenate([p[:, a : a + LANES] for p in parts for a in (0, LANES)], axis=0)
    pad = jnp.zeros((WIN, width - 2 * LANES), F32)
    return jnp.concatenate([jnp.concatenate([p, pad], axis=1) for p in parts], axis=0)


def rows_table(rows):
    if rows.shape[1] == LANES:
        rows = jnp.concatenate(
            [
                jnp.concatenate([rows[:WIN], rows[WIN : 2 * WIN]], axis=1),
                jnp.concatenate([rows[2 * WIN : 3 * WIN], rows[3 * WIN :]], axis=1),
            ],
            axis=0,
        )
    return rows[:WIN, : 2 * LANES] + rows[WIN : 2 * WIN, : 2 * LANES]


def halved(blocks, bit, table, send_ref, keep_ref):
    tail = table_rows(table, blocks[0].shape[1])
    low = bit == 0
    send = [jnp.where(low, blocks[i + 1], blocks[i]) for i in range(0, len(blocks), 2)]
    keep = [jnp.where(low, blocks[i], blocks[i + 1]) for i in range(0, len(blocks), 2)]
    send_ref[...] = jnp.concatenate(send + [tail], axis=0).astype(BF16)
    keep_ref[...] = jnp.concatenate(keep + [tail], axis=0).astype(BF16)


def pack_terms(qkv, inner, proj, outer, count):
    blocks = []
    for c in range(count):
        parts = []
        for term in (qkv, inner, proj):
            size = term.shape[0] // count
            parts.append(term[c * size : (c + 1) * size])
        block = jnp.concatenate(parts, axis=0)
        half = block.shape[0] // 2
        block = jnp.concatenate([block[:half], block[half:]], axis=1)
        size = outer.shape[0] // count
        wide = outer[c * size : (c + 1) * size]
        parts = [wide[:, a : a + block.shape[1]] for a in range(0, wide.shape[1], block.shape[1])]
        blocks.append(jnp.concatenate([block] + parts, axis=0))
    return blocks


def row_blocks(block, half, channels, hidden, count):
    low = block[:half]
    size = (block.shape[0] - half) * block.shape[1] // hidden
    wide = jnp.concatenate(
        [block[half + a : half + a + size] for a in range(0, block.shape[0] - half, size)], axis=1
    )
    thin = channels // count
    broad = hidden // count
    blocks = []
    for r in range(count):
        pair = jnp.concatenate(
            [
                low[:, r * thin : (r + 1) * thin],
                low[:, channels + r * thin : channels + (r + 1) * thin],
            ],
            axis=1,
        )
        parts = [
            wide[:, r * broad + a : r * broad + a + 2 * thin] for a in range(0, broad, 2 * thin)
        ]
        out = jnp.concatenate([pair] + parts, axis=0)
        blocks.append(
            jnp.concatenate([out, jnp.zeros((out.shape[0], LANES - 2 * thin), F32)], axis=1)
        )
    return blocks


def first_kernel(
    tokens,
    ids,
    cotangent,
    qkv_w,
    proj_w,
    inner_w,
    outer_w,
    table,
    first_out,
    up,
    down,
    query_out,
    key_out,
    value_out,
    probs_out,
    mix_out,
    middle_out,
    pre_out,
    act_out,
    edge,
):
    rows, cols, channels = tokens.shape
    heads = table.shape[2]
    size = channels // heads
    count = rows * cols
    surface = to_windows(tokens[...].astype(F32))
    normed = norm(surface)[0].astype(BF16)
    bias = expand_bias(table[0])
    masks = same_region(ids[...].astype(F32))
    query, key, value = (
        nn(normed, qkv_w[0, :, i * channels : (i + 1) * channels]).astype(BF16) for i in range(3)
    )
    query_out[...] = query
    key_out[...] = key
    value_out[...] = value
    mixes = []
    for w in range(count // TOK):
        at = slice(w * TOK, (w + 1) * TOK)
        probs, mix = attend(query[at], key[at], value[at], bias, masks[w], size)
        probs_out[w] = probs
        mixes.append(mix)
    mix = jnp.concatenate(mixes, axis=0)
    mix_out[...] = mix
    middle = (surface + nn(mix, proj_w[0])).astype(BF16)
    middle_out[...] = middle
    normed = norm(middle.astype(F32))[0].astype(BF16)
    outs = []
    for at in range(0, count, 2 * TOK):
        pre = nn(normed[at : at + 2 * TOK], inner_w[0])
        pre_out[at : at + 2 * TOK] = pre
        act = (0.5 * pre * (1.0 + lax.erf(pre * math.sqrt(0.5)))).astype(BF16)
        act_out[at : at + 2 * TOK] = act
        outs.append(nn(act, outer_w[0]))
    result = (middle.astype(F32) + jnp.concatenate(outs, axis=0)).astype(BF16).astype(F32)
    grid = from_windows(result, rows, cols)
    first_out[...] = grid.astype(BF16)
    grads = cotangent[...].astype(F32)
    marks = ids[...].astype(F32)
    for ref, start in ((up, 0), (down, rows - HALF)):
        edge[...] = jnp.zeros(edge.shape, F32)
        for i in range(HALF):
            edge[i * cols : (i + 1) * cols, :channels] = grid[start + i]
            edge[i * cols : (i + 1) * cols, channels:] = grads[start + i]
        edge[HALF * cols : HALF * cols + HALF, :cols] = marks[start : start + HALF]
        ref[...] = edge[...].astype(BF16)


def edge_kernel(
    first_out,
    cotangent,
    ids,
    upper_rim,
    upper_ids,
    lower_rim,
    lower_ids,
    from_up,
    from_down,
    up,
    down,
    to_left,
    to_right,
    ext_ids,
    edge,
    marks,
):
    rows, cols, channels = first_out.shape
    index = lax.axis_index("rows")
    at_top = index == 0
    at_bottom = index == lax.axis_size("rows") - 1
    grid = first_out[...].astype(F32)
    grads = cotangent[...].astype(F32)
    marks[HALF : HALF + rows, :] = ids[...].astype(F32)
    bands = []
    for at_end, rim, rim_ids, source, target, place in (
        (at_top, upper_rim, upper_ids, from_up, up, 0),
        (at_bottom, lower_rim, lower_ids, from_down, down, HALF + rows),
    ):
        got = source[...].astype(F32)
        wide = HALF * cols
        tokens = jnp.where(at_end, rim[...].astype(F32).reshape(wide, channels), got[:wide, :channels])
        rest = jnp.where(at_end, 0.0, got[:wide, channels:])
        band = jnp.concatenate([tokens, rest], axis=1)
        target[...] = band.astype(BF16)
        marks[place : place + HALF, :] = jnp.where(
            at_end, rim_ids[...].astype(F32), got[wide : wide + HALF, :cols]
        )
        bands.append(band)
    ext_ids[...] = marks[...]
    total = rows + 2 * HALF
    for ref, start in ((to_left, 0), (to_right, cols - HALF)):
        edge[...] = jnp.zeros(edge.shape, F32)
        for i in range(total):
            here = slice(i * HALF, (i + 1) * HALF)
            if HALF <= i < HALF + rows:
                edge[here, :channels] = grid[i - HALF, start : start + HALF]
                edge[here, channels:] = grads[i - HALF, start : start + HALF]
            else:
                band, row = (bands[0], i) if i < HALF else (bands[1], i - HALF - rows)
                edge[here, :] = band[row * cols + start : row * cols + start + HALF]
        edge[total * HALF : total * HALF + total, :cols] = marks[...]
        ref[...] = edge[...].astype(BF16)


def side_kernel(table, pre, bias, slope, keeps):
    bias[...] = expand_bias(table[1])
    count = pre.shape[0]
    for at in range(0, count, TOK):
        x = pre[at : at + TOK]
        slope[at : at + TOK] = 0.5 * (1.0 + lax.erf(x * math.sqrt(0.5))) + x * (
            jnp.exp(-0.5 * x * x) * (1.0 / math.sqrt(2.0 * math.pi))
        )


def own_windows(rows, cols, channels, low, high):
    per_band = (cols + 2 * HALF) // WIN
    masks = []
    for a in range((rows + 2 * HALF) // WIN):
        for b in range(per_band):
            token = iota((TOK, channels), 0)
            row = a * WIN + (token >> 3)
            col = b * WIN + (token & (WIN - 1))
            masks.append((row >= low) & (row < high) & (col >= HALF) & (col < HALF + cols))
    return jnp.concatenate([ones_where(mask) for mask in masks], axis=0)


def second_kernel(
    first_out,
    cotangent,
    up,
    down,
    left,
    right,
    ext_ids,
    bias_ref,
    qkv_w,
    proj_w,
    inner_w,
    outer_w,
    grad_out,
    send,
    keep,
    xs,
    cs,
    probs_s,
):
    rows, cols, channels = first_out.shape
    total, wide = rows + 2 * HALF, cols + 2 * HALF
    width = bias_ref.shape[1]
    size = channels // (width // TOK)
    hidden = inner_w.shape[2]
    for ref, source, at in ((xs, first_out, 0), (cs, cotangent, channels)):
        part = slice(at, at + channels)
        ref[HALF : HALF + rows, HALF : HALF + cols, :] = source[...].astype(F32)
        for edge, place in ((up, 0), (down, HALF + rows)):
            band = edge[...].astype(F32)[:, part]
            for i in range(HALF):
                ref[place + i, HALF : HALF + cols, :] = band[i * cols : (i + 1) * cols]
        for edge, place in ((left, 0), (right, HALF + cols)):
            band = edge[...].astype(F32)[:, part]
            for i in range(total):
                ref[i, place : place + HALF, :] = band[i * HALF : (i + 1) * HALF]
    tail = slice(total * HALF, total * HALF + total)
    source_col = iota((cols, wide), 0)
    target_col = iota((cols, wide), 1)
    marks = sum(
        nn(values.astype(BF16), ones_where(target_col == source_col + shift))
        for values, shift in (
            (left[...].astype(F32)[tail, :cols], HALF - cols),
            (ext_ids[...], HALF),
            (right[...].astype(F32)[tail, :cols], HALF + cols),
        )
    )
    masks = same_region(marks)
    bias = bias_ref[...]
    surface = to_windows(xs[...])
    grad = to_windows(cs[...]).astype(BF16)
    count = surface.shape[0]
    unit_one, inverse_one = norm(surface)
    normed_one = unit_one.astype(BF16)
    weights = [qkv_w[1, :, i * channels : (i + 1) * channels] for i in range(3)]
    query, key, value = (nn(normed_one, w).astype(BF16) for w in weights)
    mixes = []
    for w in range(count // TOK):
        at = slice(w * TOK, (w + 1) * TOK)
        probs, mix = attend(query[at], key[at], value[at], bias, masks[w], size)
        probs_s[w] = probs
        mixes.append(mix)
    mix = jnp.concatenate(mixes, axis=0)
    middle = (surface + nn(mix, proj_w[1])).astype(BF16).astype(F32)
    unit_two, inverse_two = norm(middle)
    normed_two = unit_two.astype(BF16)
    acts, grad_pres, grad_norms = [], [], []
    for at in range(0, count, 2 * TOK):
        here = slice(at, at + 2 * TOK)
        pre = nn(normed_two[here], inner_w[1])
        cdf = 0.5 * (1.0 + lax.erf(pre * math.sqrt(0.5)))
        acts.append((pre * cdf).astype(BF16))
        slope = cdf + pre * (jnp.exp(-0.5 * pre * pre) * (1.0 / math.sqrt(2.0 * math.pi)))
        grad_pre = (slope * nt(grad[here], outer_w[1])).astype(BF16)
        grad_pres.append(grad_pre)
        grad_norms.append(nt(grad_pre, inner_w[1]))
    act = jnp.concatenate(acts, axis=0)
    grad_pre = jnp.concatenate(grad_pres, axis=0)
    grad_norm = jnp.concatenate(grad_norms, axis=0)
    grad_middle = (grad.astype(F32) + norm_back(unit_two, inverse_two, grad_norm)).astype(BF16)
    index = lax.axis_index("rows")
    last = lax.axis_size("rows") - 1
    per_band = wide // WIN
    raw = nt(grad_middle, proj_w[1])
    grad_mixes = []
    for w in range(count // TOK):
        row = w // per_band * WIN + (iota((TOK, channels), 0) >> 3)
        low = jnp.where(index == 0, HALF, 0)
        high = jnp.where(index == last, HALF + rows, total)
        part = jnp.where((row >= low) & (row < high), raw[w * TOK : (w + 1) * TOK], 0.0)
        grad_mixes.append(part.astype(BF16))
    grads = ([], [], [])
    bias_sum = jnp.zeros((TOK, width), F32)
    for w in range(count // TOK):
        at = slice(w * TOK, (w + 1) * TOK)
        parts, term = attend_back(query[at], key[at], value[at], probs_s[w], grad_mixes[w], size)
        for total_list, part in zip(grads, parts):
            total_list.append(part)
        lane = iota((1, width), 1)
        row = w // per_band * WIN + ((lane >> 3) & (WIN - 1))
        col = w % per_band * WIN + (lane & (WIN - 1))
        own = (row >= HALF) & (row < HALF + rows) & (col >= HALF) & (col < HALF + cols)
        bias_sum = bias_sum + term * jnp.where(own, 1.0, 0.0)
    grads = [jnp.concatenate(g, axis=0) for g in grads]
    grad_norm = sum(nt(g, w) for g, w in zip(grads, weights))
    grad_surface = grad_middle.astype(F32) + norm_back(unit_one, inverse_one, grad_norm)
    xs[...] = from_windows(grad_surface, total, wide)
    grad_out[...] = to_windows(xs[HALF : HALF + rows, HALF : HALF + cols, :]).astype(BF16)
    own = own_windows(rows, cols, channels, HALF, HALF + rows)
    low = jnp.where(index == 0, 0, HALF)
    high = jnp.where(index == last, total, HALF + rows)
    normed_one = normed_one * own_windows(rows, cols, channels, low, high)
    blocks = pack_terms(
        jnp.concatenate([tn(g, normed_one) for g in grads], axis=0),
        tn(grad_pre, normed_two * own),
        tn(grad_middle, mix * own),
        tn(grad * own, act),
        lax.axis_size("cols"),
    )
    halved(blocks, lax.axis_index("cols") & 1, fold_bias(bias_sum), send, keep)


def third_kernel(
    tokens,
    grad_ref,
    query,
    key,
    value,
    probs_ref,
    mix,
    middle_ref,
    act,
    slope,
    qkv_w,
    proj_w,
    inner_w,
    outer_w,
    token_grad,
    send,
    keep,
):
    rows, cols, channels = tokens.shape
    width = probs_ref.shape[2]
    size = channels // (width // TOK)
    count = rows * cols
    grad = grad_ref[...]
    unit_one, inverse_one = norm(to_windows(tokens[...].astype(F32)))
    normed_one = unit_one.astype(BF16)
    unit_two, inverse_two = norm(middle_ref[...].astype(F32))
    normed_two = unit_two.astype(BF16)
    grad_pres, grad_norms = [], []
    for at in range(0, count, 2 * TOK):
        here = slice(at, at + 2 * TOK)
        grad_pre = (slope[here] * nt(grad[here], outer_w[0])).astype(BF16)
        grad_pres.append(grad_pre)
        grad_norms.append(nt(grad_pre, inner_w[0]))
    grad_pre = jnp.concatenate(grad_pres, axis=0)
    grad_norm = jnp.concatenate(grad_norms, axis=0)
    grad_middle = (grad.astype(F32) + norm_back(unit_two, inverse_two, grad_norm)).astype(BF16)
    grad_mix = nt(grad_middle, proj_w[0]).astype(BF16)
    grads = ([], [], [])
    bias_sum = jnp.zeros((TOK, width), F32)
    for w in range(count // TOK):
        at = slice(w * TOK, (w + 1) * TOK)
        parts, term = attend_back(query[at], key[at], value[at], probs_ref[w], grad_mix[at], size)
        for total_list, part in zip(grads, parts):
            total_list.append(part)
        bias_sum = bias_sum + term
    grads = [jnp.concatenate(g, axis=0) for g in grads]
    weights = [qkv_w[0, :, i * channels : (i + 1) * channels] for i in range(3)]
    grad_norm = sum(nt(g, w) for g, w in zip(grads, weights))
    grad_surface = grad_middle.astype(F32) + norm_back(unit_one, inverse_one, grad_norm)
    token_grad[...] = from_windows(grad_surface, rows, cols).astype(BF16)
    blocks = pack_terms(
        jnp.concatenate([tn(g, normed_one) for g in grads], axis=0),
        tn(grad_pre, normed_two),
        tn(grad_middle, mix[...]),
        tn(grad, act[...]),
        lax.axis_size("cols"),
    )
    halved(blocks, lax.axis_index("cols") & 1, fold_bias(bias_sum), send, keep)


def summed(keep, got, tail):
    both = keep[...].astype(F32) + got[...].astype(F32)
    edge = both.shape[0] - tail
    return both[:edge], rows_table(both[edge:])


def cols_kernel(count, bit, keep_in, got, send, keep):
    both, table = summed(keep_in, got, 2 * WIN)
    rows = both.shape[0] // count
    blocks = [both[i * rows : (i + 1) * rows] for i in range(count)]
    halved(blocks, (lax.axis_index("cols") >> bit) & 1, table, send, keep)


def turn_kernel(half, channels, hidden, keep_in, got, send, keep):
    both, table = summed(keep_in, got, 2 * WIN)
    blocks = row_blocks(both, half, channels, hidden, lax.axis_size("rows"))
    halved(blocks, lax.axis_index("rows") & 1, table, send, keep)


def rows_kernel(count, bit, keep_in, got, send, keep):
    both, table = summed(keep_in, got, 4 * WIN)
    rows = both.shape[0] // count
    blocks = [both[i * rows : (i + 1) * rows] for i in range(count)]
    halved(blocks, (lax.axis_index("rows") >> bit) & 1, table, send, keep)


def last_kernel(
    sizes, scale, keep_one, got_one, keep_two, got_two, qkv, proj, inner, outer, table
):
    (qkv_cols, inner_cols, proj_cols), thin, broad = sizes
    for b, (keep, got) in enumerate(((keep_one, got_one), (keep_two, got_two))):
        both, sums = summed(keep, got, 4 * WIN)
        both = both * scale
        half = (qkv_cols + inner_cols + proj_cols) // 2
        low = jnp.concatenate([both[:half, :thin], both[:half, thin : 2 * thin]], axis=0)
        qkv[b] = low[:qkv_cols].T
        inner[b] = low[qkv_cols : qkv_cols + inner_cols].T
        proj[b] = low[qkv_cols + inner_cols :].T
        wide = jnp.concatenate(
            [
                both[half + i * proj_cols : half + (i + 1) * proj_cols, : 2 * thin]
                for i in range(broad // (2 * thin))
            ],
            axis=1,
        )
        outer[b] = wide.T
        heads = table.shape[2]
        onehot = offset_rows(table.shape[1])
        table[b] = sum(nt(onehot, part) for part in split(sums * scale, 3))[:, :heads]


def call(kernel, outs, scratch, *operands):
    return pl.pallas_call(
        kernel,
        out_shape=[jax.ShapeDtypeStruct(shape, kind) for shape, kind in outs],
        scratch_shapes=scratch,
        compiler_params=pltpu.CompilerParams(vmem_limit_bytes=VMEM_LIMIT),
    )(*operands)


def flip(values, axis, bit):
    count = lax.axis_size(axis)
    return lax.ppermute(values, axis, [(i, i ^ (1 << bit)) for i in range(count)])


def ring(values, axis, step, periodic):
    count = lax.axis_size(axis)
    pairs = [(i, (i + step) % count) for i in range(count) if periodic or 0 <= i + step < count]
    return lax.ppermute(values, axis, pairs)


def reduce_terms(send, keep, channels, hidden, half):
    col_count = lax.axis_size("cols")
    row_count = lax.axis_size("rows")
    got = flip(send, "cols", 0)
    left = col_count // 2
    bit = 1
    tail = 2 * WIN
    rows = (keep.shape[0] - tail) // left
    while left > 1:
        shape = ((left // 2 * rows + tail, keep.shape[1]), BF16)
        send, keep = call(functools.partial(cols_kernel, left, bit), [shape, shape], [], keep, got)
        got = flip(send, "cols", bit)
        left //= 2
        bit += 1
    thin = channels // row_count
    broad = hidden // row_count
    rows = half + (rows - half) * keep.shape[1] // hidden * (broad // (2 * thin))
    tail = 4 * WIN
    left = row_count
    shape = ((left // 2 * rows + tail, LANES), BF16)
    send, keep = call(
        functools.partial(turn_kernel, half, channels, hidden), [shape, shape], [], keep, got
    )
    got = flip(send, "rows", 0)
    left //= 2
    bit = 1
    while left > 1:
        shape = ((left // 2 * rows + tail, LANES), BF16)
        send, keep = call(functools.partial(rows_kernel, left, bit), [shape, shape], [], keep, got)
        got = flip(send, "rows", bit)
        left //= 2
        bit += 1
    return keep, got


def local(
    tokens,
    region_ids,
    upper_rim,
    upper_ids,
    lower_rim,
    lower_ids,
    cotangent,
    qkv_weight,
    proj_weight,
    inner_weight,
    outer_weight,
    bias_table,
):
    rows, cols, channels = tokens.shape
    hidden = inner_weight.shape[2]
    length, heads = bias_table.shape[1:]
    col_count = lax.axis_size("cols")
    row_count = lax.axis_size("rows")
    count = rows * cols
    width = heads * TOK
    total = rows + 2 * HALF
    flat = ((count, channels), BF16)
    band = (HALF * cols + 2 * WIN, 2 * channels)
    first_out, up, down, query, key, value, probs, mix, middle, pre, act = call(
        first_kernel,
        [
            ((rows, cols, channels), BF16),
            (band, BF16),
            (band, BF16),
            flat,
            flat,
            flat,
            ((count // TOK, TOK, width), F32),
            flat,
            flat,
            ((count, hidden), F32),
            ((count, hidden), BF16),
        ],
        [pltpu.VMEM(band, F32)],
        tokens,
        region_ids,
        cotangent,
        qkv_weight,
        proj_weight,
        inner_weight,
        outer_weight,
        bias_table,
    )
    from_up = ring(down, "rows", 1, False)
    from_down = ring(up, "rows", -1, False)
    bias, slope = call(
        lambda t, p, b, s: side_kernel(t, p, b, s, None),
        [((TOK, width), F32), ((count, hidden), F32)],
        [],
        bias_table,
        pre,
    )
    strip = (total * HALF + total, 2 * channels)
    up, down, to_left, to_right, ext_ids = call(
        edge_kernel,
        [
            ((HALF * cols, 2 * channels), BF16),
            ((HALF * cols, 2 * channels), BF16),
            (strip, BF16),
            (strip, BF16),
            ((total, cols), F32),
        ],
        [pltpu.VMEM(strip, F32), pltpu.VMEM((total, cols), F32)],
        first_out,
        cotangent,
        region_ids,
        upper_rim,
        upper_ids,
        lower_rim,
        lower_ids,
        from_up,
        from_down,
    )
    left = ring(to_right, "cols", 1, True)
    right = ring(to_left, "cols", -1, True)
    half = (4 * channels + hidden) // col_count // 2
    block_rows = half + channels // col_count * hidden // (2 * channels)
    packed = ((col_count // 2 * block_rows + 2 * WIN, 2 * channels), BF16)
    grid = (total, cols + 2 * HALF, channels)
    grad_first, send_two, keep_two = call(
        second_kernel,
        [flat, packed, packed],
        [
            pltpu.VMEM(grid, F32),
            pltpu.VMEM(grid, F32),
            pltpu.VMEM((grid[0] * grid[1] // TOK, TOK, width), F32),
        ],
        first_out,
        cotangent,
        up,
        down,
        left,
        right,
        ext_ids,
        bias,
        qkv_weight,
        proj_weight,
        inner_weight,
        outer_weight,
    )
    token_grad, send_one, keep_one = call(
        third_kernel,
        [((rows, cols, channels), BF16), packed, packed],
        [],
        tokens,
        grad_first,
        query,
        key,
        value,
        probs,
        mix,
        middle,
        act,
        slope,
        qkv_weight,
        proj_weight,
        inner_weight,
        outer_weight,
    )
    keep_two, got_two = reduce_terms(send_two, keep_two, channels, hidden, half)
    keep_one, got_one = reduce_terms(send_one, keep_one, channels, hidden, half)
    thin = channels // row_count
    broad = hidden // row_count
    sizes = (
        (3 * channels // col_count, hidden // col_count, channels // col_count),
        thin,
        broad,
    )
    qkv_grad, proj_grad, inner_grad, outer_grad, table_grad = call(
        functools.partial(last_kernel, sizes, 1.0 / (row_count * col_count)),
        [
            ((2, thin, sizes[0][0]), F32),
            ((2, thin, sizes[0][2]), F32),
            ((2, thin, sizes[0][1]), F32),
            ((2, broad, sizes[0][2]), F32),
            ((2, length, heads), F32),
        ],
        [],
        keep_one,
        got_one,
        keep_two,
        got_two,
    )
    return token_grad, qkv_grad, proj_grad, inner_grad, outer_grad, table_grad


def solution(mesh):
    return jax.shard_map(
        local,
        mesh=mesh,
        in_specs=(
            P("rows", "cols", None),
            P("rows", "cols"),
            P(None, "cols", None),
            P(None, "cols"),
            P(None, "cols", None),
            P(None, "cols"),
            P("rows", "cols", None),
            P(),
            P(),
            P(),
            P(),
            P(),
        ),
        out_specs=(
            P("rows", "cols", None),
            P(None, "rows", "cols"),
            P(None, "rows", "cols"),
            P(None, "rows", "cols"),
            P(None, "rows", "cols"),
            P(),
        ),
        check_vma=False,
    )
```

profile of v0, /device:TPU:0, one launch (start us, length us, event | category | flops | bytes accessed | tf_op | source)
XLA Modules:
  0.0 71.9 jit_solution(8831211311977336060)
XLA Ops:
  0.7 1.4 %copy.18.outer_w = bf16[2,768,192]{2,1,0:T(8,128)(2,1)S(1)} copy(bf16[2,768,192]{1,2,0:T(8,128)(2,1)} %param.22) | data formatting | bytes 1179648 | tf_op args[10]
  2.3 0.7 %copy-done.2 = bf16[2,192,192]{2,1,0:T(8,128)(2,1)S(1)} copy-done((bf16[2,192,192]{2,1,0:T(8,128)(2,1)S(1)}, bf16[2,192,192]{2,1,0:T(8,128)(2,1)}, u32[]{:S(2)}) %copy-start.2) | copy-done | bytes 147480
  3.1 2.8 %shard_map.163 = (bf16[8,32,192]{2,1,0:T(8,128)(2,1)S(1)}, bf16[144,384]{1,0:T(8,128)(2,1)S(1)}, bf16[144,384]{1,0:T(8,128)(2,1)S(1)}, bf16[256,192]{1,0:T(8,128...) custom-call(bf16[8,32,192]{2,1,0:T(8,128)(2,1)S(1)} %copy-done.4, ...), custom_call_target="tpu_custom_call" | custom-call | tf_op jit(solution)/shard_map/pallas_call | solution.py:695
  5.9 4.9 %collective-permute-start = (bf16[144,384]{1,0:T(8,128)(2,1)S(1)}, bf16[144,384]{1,0:T(8,128)(2,1)S(1)}, u32[]{:S(2)}, u32[]{:S(2)}) collective-permute-start(bf16[144,384]{1,0:T(8,128)(2,1)S(1)} %get-tuple-element.52), channel_id=1, source_target_pairs={{0,8},{8,16},{16,24},{1,9},{9,17},{17,25},{2,10},{10,18},{18,26},{... | collective-permute-start | bytes 331784 | tf_op jit(solution)/shard_map/ppermute | solution.py:711
  10.9 1.3 %collective-permute-start.1 = (bf16[144,384]{1,0:T(8,128)(2,1)S(1)}, bf16[144,384]{1,0:T(8,128)(2,1)S(1)}, u32[]{:S(2)}, u32[]{:S(2)}) collective-permute-start(bf16[144,384]{1,0:T(8,128)(2,1)S(1)} %get-tuple-element.53), channel_id=1, source_target_pairs={{8,0},{16,8},{24,16},{9,1},{17,9},{25,17},{10,2},{18,10},{26,18},{... | collective-permute-start | bytes 331784 | tf_op jit(solution)/shard_map/ppermute | solution.py:711
  12.2 1.0 %collective-permute-done.from_up = bf16[144,384]{1,0:T(8,128)(2,1)S(1)} collective-permute-done((bf16[144,384]{1,0:T(8,128)(2,1)S(1)}, bf16[144,384]{1,0:T(8,128)(2,1)S(1)}, u32[]{:S(2)}, u32[]{:S(2)}) %collective-permute-start) | collective-permute-done | bytes 110624 | tf_op jit(solution)/shard_map/ppermute | solution.py:711
  13.2 4.3 %collective-permute-done.1.from_down = bf16[144,384]{1,0:T(8,128)(2,1)S(1)} collective-permute-done((bf16[144,384]{1,0:T(8,128)(2,1)S(1)}, bf16[144,384]{1,0:T(8,128)(2,1)S(1)}, u32[]{:S(2)}, u32[]{:S(2)}) %collective-permute-start.1) | collective-permute-done | bytes 110624 | tf_op jit(solution)/shard_map/ppermute | solution.py:711
  17.5 0.2 shard_map.164
  17.7 2.6 %collective-permute-start.3 = (bf16[80,384]{1,0:T(8,128)(2,1)S(1)}, bf16[80,384]{1,0:T(8,128)(2,1)S(1)}, u32[]{:S(2)}, u32[]{:S(2)}) collective-permute-start(bf16[80,384]{1,0:T(8,128)(2,1)S(1)} %get-tuple-element.57), channel_id=1, source_target_pairs={{0,7},{1,0},{2,1},{3,2},{4,3},{5,4},{6,5},{7,6},{8,15},{9,8},{10,9... | collective-permute-start | bytes 184328 | tf_op jit(solution)/shard_map/ppermute | solution.py:711
  20.4 1.0 %shard_map.165 = (f32[64,384]{1,0:T(8,128)S(1)}, f32[256,768]{1,0:T(8,128)S(1)}) custom-call(f32[2,225,6]{2,1,0:T(8,128)S(1)} %copy.19.table.t, f32[256,768]{1,0:T(8,128)S(1)} %get-tuple-element.59.p), custom_call_target="tpu_custom_call" | custom-call | tf_op jit(solution)/shard_map/pallas_call | solution.py:695
  21.4 0.9 %collective-permute-done.2.left = bf16[80,384]{1,0:T(8,128)(2,1)S(1)} collective-permute-done((bf16[80,384]{1,0:T(8,128)(2,1)S(1)}, bf16[80,384]{1,0:T(8,128)(2,1)S(1)}, u32[]{:S(2)}, u32[]{:S(2)}) %collective-permute-start.2) | collective-permute-done | bytes 61472 | tf_op jit(solution)/shard_map/ppermute | solution.py:711
  22.3 11.9 %shard_map.166 = (bf16[256,192]{1,0:T(8,128)(2,1)S(1)}, bf16[592,384]{1,0:T(8,128)(2,1)S(1)}, bf16[592,384]{1,0:T(8,128)(2,1)S(1)}) custom-call(bf16[8,32,192]{2,1,0:T(8,128)(2,1)S(1)} %get-tuple-element.51.first_out, bf16[8,32,192]{2,1,0:T(8,128)(2,1)S(1)} %copy-done.3, bf16[128,384]{1,0:T(8,128)(2,1)S(1)} %get-tuple-element.54.up, ...), custom_call_target="tpu_custom_call" | custom-call | tf_op jit(solution)/shard_map/pallas_call | solution.py:695
  34.2 0.8 %collective-permute-start.9 = (bf16[592,384]{1,0:T(8,128)(2,1)S(1)}, bf16[592,384]{1,0:T(8,128)(2,1)S(1)}, u32[]{:S(2)}, u32[]{:S(2)}) collective-permute-start(bf16[592,384]{1,0:T(8,128)(2,1)S(1)} %get-tuple-element.82), channel_id=1, source_target_pairs={{0,1},{1,0},{2,3},{3,2},{4,5},{5,4},{6,7},{7,6},{8,9},{9,8},{10,11... | collective-permute-start | bytes 1363976 | tf_op jit(solution)/shard_map/ppermute | solution.py:705
  35.0 4.4 %shard_map.167 = (bf16[8,32,192]{2,1,0:T(8,128)(2,1)}, bf16[592,384]{1,0:T(8,128)(2,1)S(1)}, bf16[592,384]{1,0:T(8,128)(2,1)S(1)}) custom-call(bf16[8,32,192]{2,1,0:T(8,128)(2,1)S(1)} %copy-done.4, bf16[256,192]{1,0:T(8,128)(2,1)S(1)} %get-tuple-element.61.grad_ref, bf16[256,192]{1,0:T(8,128)(2,1)S(1)} %get-tuple-element.62.query, ...), custom_call_target="tpu_custom_call" | custom-call | tf_op jit(solution)/shard_map/pallas_call | solution.py:695
  39.6 2.5 %collective-permute-start.10 = (bf16[304,384]{1,0:T(8,128)(2,1)S(1)}, bf16[304,384]{1,0:T(8,128)(2,1)S(1)}, u32[]{:S(2)}, u32[]{:S(2)}) collective-permute-start(bf16[304,384]{1,0:T(8,128)(2,1)S(1)} %get-tuple-element.84), channel_id=1, source_target_pairs={{0,2},{1,3},{2,0},{3,1},{4,6},{5,7},{6,4},{7,5},{8,10},{9,11},{10,... | collective-permute-start | bytes 700424 | tf_op jit(solution)/shard_map/ppermute | solution.py:705
  42.2 1.6 %collective-permute-start.5 = (bf16[304,384]{1,0:T(8,128)(2,1)S(1)}, bf16[304,384]{1,0:T(8,128)(2,1)S(1)}, u32[]{:S(2)}, u32[]{:S(2)}) collective-permute-start(bf16[304,384]{1,0:T(8,128)(2,1)S(1)} %get-tuple-element.74), channel_id=1, source_target_pairs={{0,2},{1,3},{2,0},{3,1},{4,6},{5,7},{6,4},{7,5},{8,10},{9,11},{10,... | collective-permute-start | bytes 700424 | tf_op jit(solution)/shard_map/ppermute | solution.py:705
  43.8 4.8 %collective-permute-done.10.got = bf16[304,384]{1,0:T(8,128)(2,1)S(1)} collective-permute-done((bf16[304,384]{1,0:T(8,128)(2,1)S(1)}, bf16[304,384]{1,0:T(8,128)(2,1)S(1)}, u32[]{:S(2)}, u32[]{:S(2)}) %collective-permute-start.10) | collective-permute-done | bytes 233504 | tf_op jit(solution)/shard_map/ppermute | solution.py:705
  48.7 1.1 %collective-permute-start.11 = (bf16[160,384]{1,0:T(8,128)(2,1)S(1)}, bf16[160,384]{1,0:T(8,128)(2,1)S(1)}, u32[]{:S(2)}, u32[]{:S(2)}) collective-permute-start(bf16[160,384]{1,0:T(8,128)(2,1)S(1)} %get-tuple-element.86), channel_id=1, source_target_pairs={{0,4},{1,5},{2,6},{3,7},{4,0},{5,1},{6,2},{7,3},{8,12},{9,13},{10,... | collective-permute-start | bytes 368648 | tf_op jit(solution)/shard_map/ppermute | solution.py:705
  49.8 3.6 %collective-permute-done.5.got = bf16[304,384]{1,0:T(8,128)(2,1)S(1)} collective-permute-done((bf16[304,384]{1,0:T(8,128)(2,1)S(1)}, bf16[304,384]{1,0:T(8,128)(2,1)S(1)}, u32[]{:S(2)}, u32[]{:S(2)}) %collective-permute-start.5) | collective-permute-done | bytes 233504 | tf_op jit(solution)/shard_map/ppermute | solution.py:705
  53.5 0.9 %collective-permute-start.6 = (bf16[160,384]{1,0:T(8,128)(2,1)S(1)}, bf16[160,384]{1,0:T(8,128)(2,1)S(1)}, u32[]{:S(2)}, u32[]{:S(2)}) collective-permute-start(bf16[160,384]{1,0:T(8,128)(2,1)S(1)} %get-tuple-element.76), channel_id=1, source_target_pairs={{0,4},{1,5},{2,6},{3,7},{4,0},{5,1},{6,2},{7,3},{8,12},{9,13},{10,... | collective-permute-start | bytes 368648 | tf_op jit(solution)/shard_map/ppermute | solution.py:705
  54.6 1.6 %collective-permute-start.12 = (bf16[320,128]{1,0:T(8,128)(2,1)S(1)}, bf16[320,128]{1,0:T(8,128)(2,1)S(1)}, u32[]{:S(2)}, u32[]{:S(2)}) collective-permute-start(bf16[320,128]{1,0:T(8,128)(2,1)S(1)} %get-tuple-element.88), channel_id=1, source_target_pairs={{0,8},{8,0},{16,24},{24,16},{1,9},{9,1},{17,25},{25,17},{2,10},{10... | collective-permute-start | bytes 245768 | tf_op jit(solution)/shard_map/ppermute | solution.py:705
  56.2 2.5 %collective-permute-done.6.got = bf16[160,384]{1,0:T(8,128)(2,1)S(1)} collective-permute-done((bf16[160,384]{1,0:T(8,128)(2,1)S(1)}, bf16[160,384]{1,0:T(8,128)(2,1)S(1)}, u32[]{:S(2)}, u32[]{:S(2)}) %collective-permute-start.6) | collective-permute-done | bytes 122912 | tf_op jit(solution)/shard_map/ppermute | solution.py:705
  58.8 1.6 %collective-permute-start.7 = (bf16[320,128]{1,0:T(8,128)(2,1)S(1)}, bf16[320,128]{1,0:T(8,128)(2,1)S(1)}, u32[]{:S(2)}, u32[]{:S(2)}) collective-permute-start(bf16[320,128]{1,0:T(8,128)(2,1)S(1)} %get-tuple-element.78), channel_id=1, source_target_pairs={{0,8},{8,0},{16,24},{24,16},{1,9},{9,1},{17,25},{25,17},{2,10},{10... | collective-permute-start | bytes 245768 | tf_op jit(solution)/shard_map/ppermute | solution.py:705
  60.5 1.3 %collective-permute-start.13 = (bf16[176,128]{1,0:T(8,128)(2,1)S(1)}, bf16[176,128]{1,0:T(8,128)(2,1)S(1)}, u32[]{:S(2)}, u32[]{:S(2)}) collective-permute-start(bf16[176,128]{1,0:T(8,128)(2,1)S(1)} %get-tuple-element.90), channel_id=1, source_target_pairs={{0,16},{8,24},{16,0},{24,8},{1,17},{9,25},{17,1},{25,9},{2,18},{10... | collective-permute-start | bytes 135176 | tf_op jit(solution)/shard_map/ppermute | solution.py:705
  61.8 2.1 %collective-permute-done.7.got = bf16[320,128]{1,0:T(8,128)(2,1)S(1)} collective-permute-done((bf16[320,128]{1,0:T(8,128)(2,1)S(1)}, bf16[320,128]{1,0:T(8,128)(2,1)S(1)}, u32[]{:S(2)}, u32[]{:S(2)}) %collective-permute-start.7) | collective-permute-done | bytes 81952 | tf_op jit(solution)/shard_map/ppermute | solution.py:705
  63.9 2.2 %collective-permute-start.8 = (bf16[176,128]{1,0:T(8,128)(2,1)S(1)}, bf16[176,128]{1,0:T(8,128)(2,1)S(1)}, u32[]{:S(2)}, u32[]{:S(2)}) collective-permute-start(bf16[176,128]{1,0:T(8,128)(2,1)S(1)} %get-tuple-element.80), channel_id=1, source_target_pairs={{0,16},{8,24},{16,0},{24,8},{1,17},{9,25},{17,1},{25,9},{2,18},{10... | collective-permute-start | bytes 135176 | tf_op jit(solution)/shard_map/ppermute | solution.py:705
  66.0 0.7 %collective-permute-done.13.got_two = bf16[176,128]{1,0:T(8,128)(2,1)S(1)} collective-permute-done((bf16[176,128]{1,0:T(8,128)(2,1)S(1)}, bf16[176,128]{1,0:T(8,128)(2,1)S(1)}, u32[]{:S(2)}, u32[]{:S(2)}) %collective-permute-start.13) | collective-permute-done | bytes 45088 | tf_op jit(solution)/shard_map/ppermute | solution.py:705
  66.8 2.1 %collective-permute-done.8.got_one = bf16[176,128]{1,0:T(8,128)(2,1)S(1)} collective-permute-done((bf16[176,128]{1,0:T(8,128)(2,1)S(1)}, bf16[176,128]{1,0:T(8,128)(2,1)S(1)}, u32[]{:S(2)}, u32[]{:S(2)}) %collective-permute-start.8) | collective-permute-done | bytes 45088 | tf_op jit(solution)/shard_map/ppermute | solution.py:705
  68.9 0.9 %shard_map.176 = (f32[2,48,72]{2,1,0:T(8,128)}, f32[2,48,24]{2,1,0:T(8,128)S(1)}, f32[2,48,96]{2,1,0:T(8,128)}, f32[2,192,24]{2,1,0:T(8,128)S(1)}, f32[2,225,6]{2,1,0:T(8,128)S(1)}) custom-call(bf16[176,128]{1,0:T(8,128)(2,1)S(1)} %get-tuple-element.79.keep_one, bf16[176,128]{1,0:T(8,128)(2,1)S(1)} %collective-permute-done.8.got_one, ...), custom_call_target="tpu_custom_call" | custom-call | tf_op jit(solution)/shard_map/pallas_call | solution.py:695
  69.7 0.7 %copy.24 = f32[2,192,24]{1,2,0:T(8,128)} copy(f32[2,192,24]{2,1,0:T(8,128)S(1)} %get-tuple-element.100) | data formatting | bytes 73728
  70.5 0.7 copy.23
  71.2 0.7 copy.25
  (37 shorter events, 1.1 us)
Async XLA Ops:
  0.6 1.5 %copy-start.10 = (f32[2,225,6]{1,0,2:T(2,128)S(1)}, f32[2,225,6]{1,0,2:T(2,128)}, u32[]{:S(2)}) copy-start(f32[2,225,6]{1,0,2:T(2,128)} %param.23) | copy-start | bytes 32404
  0.6 1.7 %copy-start.1 = (bf16[2,192,576]{2,1,0:T(8,128)(2,1)S(1)}, bf16[2,192,576]{2,1,0:T(8,128)(2,1)}, u32[]{:S(2)}) copy-start(bf16[2,192,576]{2,1,0:T(8,128)(2,1)} %qkv_w.5) | copy-start | bytes 1327108
  0.7 1.7 %copy-start = (bf16[2,192,768]{2,1,0:T(8,128)(2,1)S(1)}, bf16[2,192,768]{2,1,0:T(8,128)(2,1)}, u32[]{:S(2)}) copy-start(bf16[2,192,768]{2,1,0:T(8,128)(2,1)} %inner_w.5) | copy-start | bytes 1769476
  0.7 1.7 %copy-start.3 = (bf16[8,32,192]{2,1,0:T(8,128)(2,1)S(1)}, bf16[8,32,192]{2,1,0:T(8,128)(2,1)}, u32[]{:S(2)}) copy-start(bf16[8,32,192]{2,1,0:T(8,128)(2,1)} %cotangent.5) | copy-start | bytes 294916
  0.7 1.7 %copy-start.4 = (bf16[8,32,192]{2,1,0:T(8,128)(2,1)S(1)}, bf16[8,32,192]{2,1,0:T(8,128)(2,1)}, u32[]{:S(2)}) copy-start(bf16[8,32,192]{2,1,0:T(8,128)(2,1)} %tokens.3) | copy-start | bytes 294916
  2.1 0.9 %copy-start.2 = (bf16[2,192,192]{2,1,0:T(8,128)(2,1)S(1)}, bf16[2,192,192]{2,1,0:T(8,128)(2,1)}, u32[]{:S(2)}) copy-start(bf16[2,192,192]{2,1,0:T(8,128)(2,1)} %proj_w.5) | copy-start | bytes 442372
  2.1 0.9 %copy-start.7 = (s32[8,32]{1,0:T(8,128)S(1)}, s32[8,32]{1,0:T(8,128)}, u32[]{:S(2)}) copy-start(s32[8,32]{1,0:T(8,128)} %ids.3) | copy-start | bytes 3076
  3.1 14.4 %copy-start.5 = (bf16[4,32,192]{2,1,0:T(8,128)(2,1)S(1)}, bf16[4,32,192]{2,1,0:T(8,128)(2,1)}, u32[]{:S(2)}) copy-start(bf16[4,32,192]{2,1,0:T(8,128)(2,1)} %upper_rim.1) | copy-start | bytes 147460
  3.1 14.4 %copy-start.6 = (bf16[4,32,192]{2,1,0:T(8,128)(2,1)S(1)}, bf16[4,32,192]{2,1,0:T(8,128)(2,1)}, u32[]{:S(2)}) copy-start(bf16[4,32,192]{2,1,0:T(8,128)(2,1)} %lower_rim.1) | copy-start | bytes 147460
  5.9 11.6 %copy-start.9 = (s32[4,32]{1,0:T(4,128)S(1)}, s32[4,32]{1,0:T(4,128)}, u32[]{:S(2)}) copy-start(s32[4,32]{1,0:T(4,128)} %lower_ids.1) | copy-start | bytes 1540
  5.9 11.6 %copy-start.8 = (s32[4,32]{1,0:T(4,128)S(1)}, s32[4,32]{1,0:T(4,128)}, u32[]{:S(2)}) copy-start(s32[4,32]{1,0:T(4,128)} %upper_ids.1) | copy-start | bytes 1540
  5.9 7.2 %collective-permute-start = (bf16[144,384]{1,0:T(8,128)(2,1)S(1)}, bf16[144,384]{1,0:T(8,128)(2,1)S(1)}, u32[]{:S(2)}, u32[]{:S(2)}) collective-permute-start(bf16[144,384]{1,0:T(8,128)(2,1)S(1)} %get-tuple-element.52), channel_id=1, source_target_pairs={{0,8},{8,16},{16,24},{1,9},{9,17},{17,25},{2,10},{10,18},{18,26},{... | collective-permute-start | bytes 331784 | tf_op jit(solution)/shard_map/ppermute | solution.py:711
  10.9 6.6 %collective-permute-start.1 = (bf16[144,384]{1,0:T(8,128)(2,1)S(1)}, bf16[144,384]{1,0:T(8,128)(2,1)S(1)}, u32[]{:S(2)}, u32[]{:S(2)}) collective-permute-start(bf16[144,384]{1,0:T(8,128)(2,1)S(1)} %get-tuple-element.53), channel_id=1, source_target_pairs={{8,0},{16,8},{24,16},{9,1},{17,9},{25,17},{10,2},{18,10},{26,18},{... | collective-permute-start | bytes 331784 | tf_op jit(solution)/shard_map/ppermute | solution.py:711
  17.7 4.6 %collective-permute-start.2 = (bf16[80,384]{1,0:T(8,128)(2,1)S(1)}, bf16[80,384]{1,0:T(8,128)(2,1)S(1)}, u32[]{:S(2)}, u32[]{:S(2)}) collective-permute-start(bf16[80,384]{1,0:T(8,128)(2,1)S(1)} %get-tuple-element.56), channel_id=1, source_target_pairs={{0,1},{1,2},{2,3},{3,4},{4,5},{5,6},{6,7},{7,0},{8,9},{9,10},{10,1... | collective-permute-start | bytes 184328 | tf_op jit(solution)/shard_map/ppermute | solution.py:711
  17.7 4.5 %collective-permute-start.3 = (bf16[80,384]{1,0:T(8,128)(2,1)S(1)}, bf16[80,384]{1,0:T(8,128)(2,1)S(1)}, u32[]{:S(2)}, u32[]{:S(2)}) collective-permute-start(bf16[80,384]{1,0:T(8,128)(2,1)S(1)} %get-tuple-element.57), channel_id=1, source_target_pairs={{0,7},{1,0},{2,1},{3,2},{4,3},{5,4},{6,5},{7,6},{8,15},{9,8},{10,9... | collective-permute-start | bytes 184328 | tf_op jit(solution)/shard_map/ppermute | solution.py:711
  34.2 5.2 %collective-permute-start.9 = (bf16[592,384]{1,0:T(8,128)(2,1)S(1)}, bf16[592,384]{1,0:T(8,128)(2,1)S(1)}, u32[]{:S(2)}, u32[]{:S(2)}) collective-permute-start(bf16[592,384]{1,0:T(8,128)(2,1)S(1)} %get-tuple-element.82), channel_id=1, source_target_pairs={{0,1},{1,0},{2,3},{3,2},{4,5},{5,4},{6,7},{7,6},{8,9},{9,8},{10,11... | collective-permute-start | bytes 1363976 | tf_op jit(solution)/shard_map/ppermute | solution.py:705
  39.4 2.6 %collective-permute-start.4 = (bf16[592,384]{1,0:T(8,128)(2,1)S(1)}, bf16[592,384]{1,0:T(8,128)(2,1)S(1)}, u32[]{:S(2)}, u32[]{:S(2)}) collective-permute-start(bf16[592,384]{1,0:T(8,128)(2,1)S(1)} %get-tuple-element.72), channel_id=1, source_target_pairs={{0,1},{1,0},{2,3},{3,2},{4,5},{5,4},{6,7},{7,6},{8,9},{9,8},{10,11... | collective-permute-start | bytes 1363976 | tf_op jit(solution)/shard_map/ppermute | solution.py:705
  39.6 9.0 %collective-permute-start.10 = (bf16[304,384]{1,0:T(8,128)(2,1)S(1)}, bf16[304,384]{1,0:T(8,128)(2,1)S(1)}, u32[]{:S(2)}, u32[]{:S(2)}) collective-permute-start(bf16[304,384]{1,0:T(8,128)(2,1)S(1)} %get-tuple-element.84), channel_id=1, source_target_pairs={{0,2},{1,3},{2,0},{3,1},{4,6},{5,7},{6,4},{7,5},{8,10},{9,11},{10,... | collective-permute-start | bytes 700424 | tf_op jit(solution)/shard_map/ppermute | solution.py:705
  42.2 11.2 %collective-permute-start.5 = (bf16[304,384]{1,0:T(8,128)(2,1)S(1)}, bf16[304,384]{1,0:T(8,128)(2,1)S(1)}, u32[]{:S(2)}, u32[]{:S(2)}) collective-permute-start(bf16[304,384]{1,0:T(8,128)(2,1)S(1)} %get-tuple-element.74), channel_id=1, source_target_pairs={{0,2},{1,3},{2,0},{3,1},{4,6},{5,7},{6,4},{7,5},{8,10},{9,11},{10,... | collective-permute-start | bytes 700424 | tf_op jit(solution)/shard_map/ppermute | solution.py:705
  48.7 5.8 %collective-permute-start.11 = (bf16[160,384]{1,0:T(8,128)(2,1)S(1)}, bf16[160,384]{1,0:T(8,128)(2,1)S(1)}, u32[]{:S(2)}, u32[]{:S(2)}) collective-permute-start(bf16[160,384]{1,0:T(8,128)(2,1)S(1)} %get-tuple-element.86), channel_id=1, source_target_pairs={{0,4},{1,5},{2,6},{3,7},{4,0},{5,1},{6,2},{7,3},{8,12},{9,13},{10,... | collective-permute-start | bytes 368648 | tf_op jit(solution)/shard_map/ppermute | solution.py:705
  53.5 5.2 %collective-permute-start.6 = (bf16[160,384]{1,0:T(8,128)(2,1)S(1)}, bf16[160,384]{1,0:T(8,128)(2,1)S(1)}, u32[]{:S(2)}, u32[]{:S(2)}) collective-permute-start(bf16[160,384]{1,0:T(8,128)(2,1)S(1)} %get-tuple-element.76), channel_id=1, source_target_pairs={{0,4},{1,5},{2,6},{3,7},{4,0},{5,1},{6,2},{7,3},{8,12},{9,13},{10,... | collective-permute-start | bytes 368648 | tf_op jit(solution)/shard_map/ppermute | solution.py:705
  54.6 5.9 %collective-permute-start.12 = (bf16[320,128]{1,0:T(8,128)(2,1)S(1)}, bf16[320,128]{1,0:T(8,128)(2,1)S(1)}, u32[]{:S(2)}, u32[]{:S(2)}) collective-permute-start(bf16[320,128]{1,0:T(8,128)(2,1)S(1)} %get-tuple-element.88), channel_id=1, source_target_pairs={{0,8},{8,0},{16,24},{24,16},{1,9},{9,1},{17,25},{25,17},{2,10},{10... | collective-permute-start | bytes 245768 | tf_op jit(solution)/shard_map/ppermute | solution.py:705
  58.8 5.0 %collective-permute-start.7 = (bf16[320,128]{1,0:T(8,128)(2,1)S(1)}, bf16[320,128]{1,0:T(8,128)(2,1)S(1)}, u32[]{:S(2)}, u32[]{:S(2)}) collective-permute-start(bf16[320,128]{1,0:T(8,128)(2,1)S(1)} %get-tuple-element.78), channel_id=1, source_target_pairs={{0,8},{8,0},{16,24},{24,16},{1,9},{9,1},{17,25},{25,17},{2,10},{10... | collective-permute-start | bytes 245768 | tf_op jit(solution)/shard_map/ppermute | solution.py:705
  60.5 6.3 %collective-permute-start.13 = (bf16[176,128]{1,0:T(8,128)(2,1)S(1)}, bf16[176,128]{1,0:T(8,128)(2,1)S(1)}, u32[]{:S(2)}, u32[]{:S(2)}) collective-permute-start(bf16[176,128]{1,0:T(8,128)(2,1)S(1)} %get-tuple-element.90), channel_id=1, source_target_pairs={{0,16},{8,24},{16,0},{24,8},{1,17},{9,25},{17,1},{25,9},{2,18},{10... | collective-permute-start | bytes 135176 | tf_op jit(solution)/shard_map/ppermute | solution.py:705
  63.9 5.0 %collective-permute-start.8 = (bf16[176,128]{1,0:T(8,128)(2,1)S(1)}, bf16[176,128]{1,0:T(8,128)(2,1)S(1)}, u32[]{:S(2)}, u32[]{:S(2)}) collective-permute-start(bf16[176,128]{1,0:T(8,128)(2,1)S(1)} %get-tuple-element.80), channel_id=1, source_target_pairs={{0,16},{8,24},{16,0},{24,8},{1,17},{9,25},{17,1},{25,9},{2,18},{10... | collective-permute-start | bytes 135176 | tf_op jit(solution)/shard_map/ppermute | solution.py:705
where the time goes:
time: 72.1 us; the launch traced here: 71.9 us
  starting transfers between devices  22.6 us (31%)
  Pallas kernels  22 us (31%)
  waiting for transfers between devices  21.9 us (30%)
  local copies, waits for them, and re-layouts  4.46 us (6%)
  between operations  0.87 us (1%)
    pallas_call x14, Pallas kernels, call(): pl.pallas_call(kernel, out_shape=[jax.ShapeDtypeStruct(shape, kind) for s...  22 us
    ppermute x10, waiting for transfers between devices, flip(): return lax.ppermute(values, axis, [(i, i ^ 1 << bit) for i in range(count)])  15.7 us
    ppermute x10, starting transfers between devices, flip(): return lax.ppermute(values, axis, [(i, i ^ 1 << bit) for i in range(count)])  13.7 us
    ppermute x4, starting transfers between devices, ring(): return lax.ppermute(values, axis, pairs)  8.91 us
    ppermute x4, waiting for transfers between devices, ring(): return lax.ppermute(values, axis, pairs)  6.21 us
    unnamed x27, local copies, waits for them, and re-layouts  4.46 us
  transfers between devices with their start and end apart: 14, of which 9 were waited for; matrix products, arithmetic and copies ran while one was open for 0% of the time, Pallas kernels for 9%

commit v1 on v0

v1 whole, which is shorter than its diff:
```python
import functools
import math

import jax
import jax.numpy as jnp
from jax import lax
from jax.experimental import pallas as pl
from jax.experimental.pallas import tpu as pltpu
from jax.sharding import PartitionSpec as P

WIN = 8
HALF = 4
TOK = WIN * WIN
SPAN = 2 * WIN - 1
LANES = 128
EPS = 1e-05
MASKED = -1000000000.0
F32 = jnp.float32
BF16 = jnp.bfloat16
ARRIVAL = (0, 3, 2, 1)
ORDERED = (0, 3, 2, 1)
VMEM_LIMIT = 40 * 1024 * 1024


def nn(left, right):
    return lax.dot_general(left, right, (((1,), (0,)), ((), ())), preferred_element_type=F32)


def nt(left, right):
    return lax.dot_general(left, right, (((1,), (1,)), ((), ())), preferred_element_type=F32)


def tn(left, right):
    return lax.dot_general(left, right, (((0,), (0,)), ((), ())), preferred_element_type=F32)


def iota(shape, dim):
    return lax.broadcasted_iota(jnp.int32, shape, dim)


def ones_where(condition):
    return jnp.where(condition, 1.0, 0.0).astype(BF16)


def norm(values):
    shifted = values - jnp.mean(values, axis=-1, keepdims=True)
    inverse = lax.rsqrt(jnp.mean(shifted * shifted, axis=-1, keepdims=True) + EPS)
    return shifted * inverse, inverse


def norm_back(unit, inverse, grad):
    mean_grad = jnp.mean(grad, axis=-1, keepdims=True)
    mean_unit = jnp.mean(grad * unit, axis=-1, keepdims=True)
    return inverse * (grad - mean_grad - unit * mean_unit)


def to_windows(grid):
    rows, cols, channels = grid.shape
    return jnp.concatenate(
        [
            grid[a : a + WIN, b : b + WIN].reshape(TOK, channels)
            for a in range(0, rows, WIN)
            for b in range(0, cols, WIN)
        ],
        axis=0,
    )


def from_windows(framed, rows, cols):
    per_band = cols // WIN
    bands = []
    for a in range(rows // WIN):
        pieces = [
            framed[(a * per_band + b) * TOK : (a * per_band + b + 1) * TOK].reshape(WIN, WIN, -1)
            for b in range(per_band)
        ]
        bands.append(jnp.concatenate(pieces, axis=1))
    return jnp.concatenate(bands, axis=0) if len(bands) > 1 else bands[0]


def lane_tiles(channels, size):
    tiles = []
    for start in range(0, channels, LANES):
        width = min(LANES, channels - start)
        tiles.append((start, width, start // size * TOK, (start + width) // size * TOK))
    return tiles


def spread(part, size):
    lane = iota((1, part.shape[1]), 1)
    copies = [
        part * ones_where((lane >= first) & (lane < first + size))
        for first in range(0, part.shape[1], size)
    ]
    return jnp.concatenate(copies, axis=0)


def paired(stacks, sides, size):
    both = []
    for n, part in enumerate(stacks):
        zeros = jnp.zeros(part.shape, part.dtype)
        both.append(jnp.concatenate([part, zeros] if n == 0 else [zeros, part], axis=0))
    wide = nn(sides, jnp.concatenate(both, axis=1))
    left = iota((size, LANES), 1) < TOK
    half = stacks[0].shape[1]
    rows = []
    for h in range(sides.shape[0] // size):
        at = h // 2 * LANES
        own = slice(h * size, (h + 1) * size)
        first = wide[own, at : at + LANES]
        second = wide[own, half + at : half + at + LANES]
        if h % 2 == 0:
            rows.append(jnp.where(left, first, pltpu.roll(second, TOK, 1)))
        else:
            rows.append(jnp.where(left, pltpu.roll(first, TOK, 1), second))
    return jnp.concatenate(rows, axis=0)


def pair_up(stacks, sides, size):
    channels = sides.shape[0]
    return jnp.concatenate(
        [
            paired([stack[:, first:last] for stack in stacks], sides[start : start + width], size)
            for start, width, first, last in lane_tiles(channels, size)
        ],
        axis=0,
    )


def attend(query, key, bias, same, size):
    scale = size ** (-0.5)
    parts = []
    for start, width, first, last in lane_tiles(query.shape[1], size):
        scores = nt(key[:, start : start + width], spread(query[:, start : start + width], size))
        for at in range(first, last, LANES):
            part = scores[:, at - first : at - first + LANES] * scale + bias[:, at : at + LANES]
            part = jnp.where(same, part, MASKED)
            exponent = jnp.exp(part - jnp.max(part, axis=0, keepdims=True))
            parts.append(exponent * (1.0 / jnp.sum(exponent, axis=0, keepdims=True)))
    return jnp.concatenate(parts, axis=1)


def attend_all(query, key, value_t, bias, masks, size, probs_ref):
    mixes = []
    for w in range(0, len(masks), 2):
        lows = []
        for v in (w, w + 1):
            at = slice(v * TOK, (v + 1) * TOK)
            probs = attend(query[at], key[at], bias, masks[v], size)
            probs_ref[v] = probs
            lows.append(probs.astype(BF16))
        mixes.append(pair_up(lows, value_t[:, w * TOK : (w + 2) * TOK], size).astype(BF16))
    return jnp.concatenate(mixes, axis=1)


def attend_back(query, value, probs, grad_mix, size):
    scale = size ** (-0.5)
    keys, values = [], []
    terms = []
    for start, width, first, last in lane_tiles(query.shape[1], size):
        part = slice(start, start + width)
        grad_heads = spread(grad_mix[:, part], size)
        chance = probs[:, first:last]
        grad_probs = nt(value[:, part], grad_heads)
        term = chance * (grad_probs - jnp.sum(grad_probs * chance, axis=0, keepdims=True))
        keys.append(nn(term.astype(BF16), spread(query[:, part], size)) * scale)
        values.append(nn(chance.astype(BF16), grad_heads))
        terms.append(term)
    return (
        jnp.concatenate(keys, axis=1).astype(BF16),
        jnp.concatenate(values, axis=1).astype(BF16),
        jnp.concatenate(terms, axis=1),
    )


def attend_all_back(query, key_t, value, probs_ref, grad_mixes, size, weigh):
    scale = size ** (-0.5)
    queries, keys, values = [], [], []
    bias_sum = None
    for w in range(0, len(grad_mixes), 2):
        lows = []
        for v in (w, w + 1):
            at = slice(v * TOK, (v + 1) * TOK)
            key, val, term = attend_back(query[at], value[at], probs_ref[v], grad_mixes[v], size)
            keys.append(key)
            values.append(val)
            lows.append(term.astype(BF16))
            term = weigh(v, term)
            bias_sum = term if bias_sum is None else bias_sum + term
        part = pair_up(lows, key_t[:, w * TOK : (w + 2) * TOK], size)
        queries.append((part * scale).astype(BF16))
    return (
        jnp.concatenate(queries, axis=1),
        jnp.concatenate(keys, axis=0),
        jnp.concatenate(values, axis=0),
        bias_sum,
    )


def same_region(ids):
    rows, cols = ids.shape
    masks = []
    row = iota((TOK, cols), 0)
    col = iota((TOK, cols), 1)
    lift = ones_where(iota((TOK, WIN), 0) // WIN == iota((TOK, WIN), 1))
    ones = jnp.ones((cols, LANES), BF16)
    for a in range(0, rows, WIN):
        band = ids[a : a + WIN].astype(BF16)
        lifted = nn(lift, band)
        for b in range(0, cols, WIN):
            picked = jnp.where(col == b + (row & (WIN - 1)), lifted, 0.0).astype(BF16)
            down = nn(picked, ones)
            tiled = nn(
                band,
                ones_where(iota((cols, LANES), 0) == b + (iota((cols, LANES), 1) & (WIN - 1))),
            )
            own = iota((WIN, LANES), 0) == ((iota((WIN, LANES), 1) // WIN) & (WIN - 1))
            across = jnp.sum(jnp.where(own, tiled, 0.0), axis=0, keepdims=True)
            masks.append(down == across)
    return masks


def split(values, count):
    parts = []
    for _ in range(count):
        low = values.astype(BF16)
        parts.append(low)
        values = values - low.astype(F32)
    return parts


def offset_rows(length):
    place = iota((length, 2 * LANES), 0)
    row = (place * 4370) >> 16
    return ones_where(iota((length, 2 * LANES), 1) == 2 * WIN * row + place - SPAN * row)


def offset_places():
    lane = iota((2 * LANES, WIN * LANES), 1)
    row = ((lane >> 3) & (WIN - 1)) - (lane >> 7) + WIN - 1
    return ones_where(iota((2 * LANES, WIN * LANES), 0) == 2 * WIN * row + (lane & (WIN - 1)))


def expand_bias(table):
    heads, length = table.shape
    onehot = offset_rows(length)
    rows = sum(nn(part, onehot) for part in split(table, 3))
    base = jnp.concatenate(
        [jnp.broadcast_to(rows[h : h + 1], (WIN, 2 * LANES)) for h in range(heads)], axis=0
    )
    place = iota(base.shape, 0) & (WIN - 1)
    rolled = base
    for c in range(WIN - 1):
        rolled = jnp.where(place == c, pltpu.roll(base, c + 2 * LANES - WIN + 1, 1), rolled)
    places = offset_places()
    spreaded = sum(nn(part, places) for part in split(rolled, 3))
    left = iota((WIN, LANES), 1) < TOK
    columns = []
    for h in range(0, heads, 2):
        pieces = [
            jnp.where(
                left,
                spreaded[h * WIN : (h + 1) * WIN, r * LANES : (r + 1) * LANES],
                spreaded[(h + 1) * WIN : (h + 2) * WIN, r * LANES : (r + 1) * LANES],
            )
            for r in range(WIN)
        ]
        columns.append(jnp.concatenate(pieces, axis=0))
    return jnp.concatenate(columns, axis=1)


def fold_bias(grad):
    heads = grad.shape[1] // TOK
    left = iota((WIN, LANES), 1) < TOK
    rows = []
    for h in range(heads):
        at = h // 2 * LANES
        pieces = []
        for r in range(WIN):
            piece = grad[r * WIN : (r + 1) * WIN, at : at + LANES]
            pieces.append(jnp.where(left, piece, 0.0) if h % 2 == 0 else jnp.where(left, 0.0, piece))
        rows.append(jnp.concatenate(pieces, axis=1))
    stacked = jnp.concatenate(rows, axis=0)
    places = offset_places()
    folded = sum(nt(part, places) for part in split(stacked, 3))
    place = iota(folded.shape, 0) & (WIN - 1)
    rolled = folded
    for c in range(WIN - 1):
        rolled = jnp.where(place == c, pltpu.roll(folded, WIN - 1 - c, 1), rolled)
    sums = [
        jnp.sum(rolled[h * WIN : (h + 1) * WIN], axis=0, keepdims=True) for h in range(heads)
    ]
    sums.append(jnp.zeros((WIN - heads, 2 * LANES), F32))
    return jnp.concatenate(sums, axis=0)


def table_rows(table, width):
    if width == LANES:
        return jnp.concatenate([table[:, :LANES], table[:, LANES:]], axis=0)
    return jnp.concatenate([table, jnp.zeros((WIN, width - 2 * LANES), F32)], axis=1)


def rows_table(rows):
    if rows.shape[1] == LANES:
        return jnp.concatenate([rows[:WIN], rows[WIN:]], axis=1)
    return rows[:WIN, : 2 * LANES]


def sort_by(blocks, place, ways):
    bit = 1
    while bit < ways:
        low = (place & bit) == 0
        blocks = [
            jnp.where(low, blocks[i], blocks[i ^ bit]) for i in range(len(blocks))
        ]
        bit *= 2
    return [blocks[i::ways] for i in range(ways)]


def tree_sum(values):
    while len(values) > 1:
        values = [values[i] + values[i + 1] for i in range(0, len(values), 2)]
    return values[0]


def write_parts(parts, tails, refs):
    for ref, part in zip(refs, parts):
        ref[...] = jnp.concatenate(part + tails, axis=0).astype(BF16)


def table_tail(tables, width):
    rows = jnp.concatenate([table_rows(table, width) for table in tables], axis=0)
    pad = -rows.shape[0] % (2 * WIN)
    if pad:
        rows = jnp.concatenate([rows, jnp.zeros((pad, width), F32)], axis=0)
    return rows


def narrow_units(terms, count):
    units = []
    for c in range(count):
        parts = []
        for term in terms:
            size = term.shape[0] // count
            parts.append(term[c * size : (c + 1) * size])
        block = jnp.concatenate(parts, axis=0) if len(parts) > 1 else parts[0]
        half = block.shape[0] // 2
        units.append(jnp.concatenate([block[:half], block[half:]], axis=1))
    return units


def wide_units(outer, width, count):
    units = []
    size = outer.shape[0] // count
    for c in range(count):
        wide = outer[c * size : (c + 1) * size]
        units.append(
            jnp.concatenate([wide[:, a : a + width] for a in range(0, wide.shape[1], width)], axis=0)
        )
    return units


def joined(*units):
    return [jnp.concatenate(parts, axis=0) for parts in zip(*units)]


def row_pieces(block, wide, channels, hidden, count):
    thin = channels // count
    broad = hidden // count
    if wide:
        size = block.shape[0] * block.shape[1] // hidden
        full = jnp.concatenate(
            [block[a : a + size] for a in range(0, block.shape[0], size)], axis=1
        )
        return [
            jnp.concatenate(
                [full[:, r * broad + a : r * broad + a + 2 * thin] for a in range(0, broad, 2 * thin)],
                axis=0,
            )
            for r in range(count)
        ]
    return [
        jnp.concatenate(
            [
                block[:, r * thin : (r + 1) * thin],
                block[:, channels + r * thin : channels + (r + 1) * thin],
            ],
            axis=1,
        )
        for r in range(count)
    ]


def bias_kernel(table, first, second):
    first[...] = expand_bias(table[:, 0])
    second[...] = expand_bias(table[:, 1])


def first_kernel(
    tokens,
    ids,
    cotangent,
    qkv_w,
    proj_w,
    inner_w,
    outer_w,
    bias_ref,
    first_out,
    near,
    far,
    query_out,
    key_out,
    value_out,
    probs_out,
    mix_out,
    middle_out,
    pre_out,
    act_out,
    edge,
):
    rows, cols, channels = tokens.shape
    size = channels // (bias_ref.shape[1] // TOK)
    count = rows * cols
    surface = to_windows(tokens[...].astype(F32))
    normed = norm(surface)[0].astype(BF16)
    bias = bias_ref[...]
    masks = same_region(ids[...].astype(F32))
    query, key, value = (
        nn(normed, qkv_w[0, :, i * channels : (i + 1) * channels]).astype(BF16) for i in range(3)
    )
    query_out[...] = query
    key_out[...] = key
    value_out[...] = value
    mix_t = attend_all(query, key, value.T, bias, masks, size, probs_out)
    mix_out[...] = mix_t
    middle = (surface + tn(mix_t, proj_w[0])).astype(BF16)
    middle_out[...] = middle
    normed = norm(middle.astype(F32))[0].astype(BF16)
    outs = []
    for at in range(0, count, 2 * TOK):
        pre = nn(normed[at : at + 2 * TOK], inner_w[0])
        pre_out[at : at + 2 * TOK] = pre
        act = (0.5 * pre * (1.0 + lax.erf(pre * math.sqrt(0.5)))).astype(BF16)
        act_out[at : at + 2 * TOK] = act
        outs.append(nt(act, outer_w[0]))
    result = (middle.astype(F32) + jnp.concatenate(outs, axis=0)).astype(BF16).astype(F32)
    grid = from_windows(result, rows, cols)
    first_out[...] = grid.astype(BF16)
    grads = cotangent[...].astype(F32)
    marks = ids[...].astype(F32)
    even = (lax.axis_index("rows") & 1) == 0
    for ref, down in ((near, even), (far, jnp.logical_not(even))):
        edge[...] = jnp.zeros(edge.shape, F32)
        for i in range(HALF):
            low = rows - HALF + i
            here = slice(i * cols, (i + 1) * cols)
            edge[here, :channels] = jnp.where(down, grid[low], grid[i])
            edge[here, channels:] = jnp.where(down, grads[low], grads[i])
        edge[HALF * cols : HALF * cols + HALF, :cols] = jnp.where(
            down, marks[rows - HALF :], marks[:HALF]
        )
        ref[...] = edge[...].astype(BF16)


def edge_kernel(
    first_out,
    cotangent,
    ids,
    upper_rim,
    upper_ids,
    lower_rim,
    lower_ids,
    from_near,
    from_far,
    up,
    down,
    near,
    far,
    ext_ids,
    edge,
    marks,
):
    rows, cols, channels = first_out.shape
    index = lax.axis_index("rows")
    at_top = index == 0
    at_bottom = index == lax.axis_size("rows") - 1
    grid = first_out[...].astype(F32)
    grads = cotangent[...].astype(F32)
    marks[HALF : HALF + rows, :] = ids[...].astype(F32)
    bands = []
    even = (index & 1) == 0
    got_near = from_near[...].astype(F32)
    got_far = from_far[...].astype(F32)
    for at_end, rim, rim_ids, got, target, place in (
        (at_top, upper_rim, upper_ids, jnp.where(even, got_far, got_near), up, 0),
        (at_bottom, lower_rim, lower_ids, jnp.where(even, got_near, got_far), down, HALF + rows),
    ):
        wide = HALF * cols
        tokens = jnp.where(at_end, rim[...].astype(F32).reshape(wide, channels), got[:wide, :channels])
        rest = jnp.where(at_end, 0.0, got[:wide, channels:])
        band = jnp.concatenate([tokens, rest], axis=1)
        target[...] = band.astype(BF16)
        marks[place : place + HALF, :] = jnp.where(
            at_end, rim_ids[...].astype(F32), got[wide : wide + HALF, :cols]
        )
        bands.append(band)
    ext_ids[...] = marks[...]
    total = rows + 2 * HALF
    even = (lax.axis_index("cols") & 1) == 0
    last = cols - HALF
    for ref, right in ((near, even), (far, jnp.logical_not(even))):
        edge[...] = jnp.zeros(edge.shape, F32)
        for i in range(total):
            here = slice(i * HALF, (i + 1) * HALF)
            if HALF <= i < HALF + rows:
                for values, part in ((grid, slice(0, channels)), (grads, slice(channels, None))):
                    row = values[i - HALF]
                    edge[here, part] = jnp.where(right, row[last:], row[:HALF])
            else:
                band, row = (bands[0], i) if i < HALF else (bands[1], i - HALF - rows)
                row = band[row * cols : (row + 1) * cols]
                edge[here, :] = jnp.where(right, row[last:], row[:HALF])
        edge[total * HALF : total * HALF + total, :cols] = marks[...]
        ref[...] = edge[...].astype(BF16)


def side_kernel(pre, key, slope, key_t):
    key_t[...] = key[...].T
    for at in range(0, pre.shape[0], TOK):
        x = pre[at : at + TOK]
        slope[at : at + TOK] = 0.5 * (1.0 + lax.erf(x * math.sqrt(0.5))) + x * (
            jnp.exp(-0.5 * x * x) * (1.0 / math.sqrt(2.0 * math.pi))
        )


def own_windows(rows, cols, channels, low, high):
    per_band = (cols + 2 * HALF) // WIN
    masks = []
    for a in range((rows + 2 * HALF) // WIN):
        for b in range(per_band):
            token = iota((TOK, channels), 0)
            row = a * WIN + (token >> 3)
            col = b * WIN + (token & (WIN - 1))
            masks.append((row >= low) & (row < high) & (col >= HALF) & (col < HALF + cols))
    return jnp.concatenate([ones_where(mask) for mask in masks], axis=0)


def second_kernel(
    first_out,
    cotangent,
    up,
    down,
    near,
    far,
    ext_ids,
    bias_ref,
    qkv_w,
    proj_w,
    inner_w,
    outer_w,
    grad_out,
    keep,
    send,
    xs,
    cs,
    probs_s,
):
    rows, cols, channels = first_out.shape
    total, wide = rows + 2 * HALF, cols + 2 * HALF
    width = bias_ref.shape[1]
    size = channels // (width // TOK)
    even = (lax.axis_index("cols") & 1) == 0
    got_near = near[...].astype(F32)
    got_far = far[...].astype(F32)
    left = jnp.where(even, got_far, got_near)
    right = jnp.where(even, got_near, got_far)
    for ref, source, at in ((xs, first_out, 0), (cs, cotangent, channels)):
        part = slice(at, at + channels)
        ref[HALF : HALF + rows, HALF : HALF + cols, :] = source[...].astype(F32)
        for edge, place in ((up, 0), (down, HALF + rows)):
            band = edge[...].astype(F32)[:, part]
            for i in range(HALF):
                ref[place + i, HALF : HALF + cols, :] = band[i * cols : (i + 1) * cols]
        for edge, place in ((left, 0), (right, HALF + cols)):
            band = edge[:, part]
            for i in range(total):
                ref[i, place : place + HALF, :] = band[i * HALF : (i + 1) * HALF]
    tail = slice(total * HALF, total * HALF + total)
    source_col = iota((cols, wide), 0)
    target_col = iota((cols, wide), 1)
    marks = sum(
        nn(values.astype(BF16), ones_where(target_col == source_col + shift))
        for values, shift in (
            (left[tail, :cols], HALF - cols),
            (ext_ids[...], HALF),
            (right[tail, :cols], HALF + cols),
        )
    )
    masks = same_region(marks)
    bias = bias_ref[...]
    surface = to_windows(xs[...])
    grad = to_windows(cs[...]).astype(BF16)
    count = surface.shape[0]
    unit_one, inverse_one = norm(surface)
    normed_one = unit_one.astype(BF16)
    weights = [qkv_w[1, :, i * channels : (i + 1) * channels] for i in range(3)]
    query, key, value = (nn(normed_one, w).astype(BF16) for w in weights)
    key_t, value_t = (nt(w.T, normed_one).astype(BF16) for w in weights[1:])
    mix_t = attend_all(query, key, value_t, bias, masks, size, probs_s)
    middle = (surface + tn(mix_t, proj_w[1])).astype(BF16).astype(F32)
    unit_two, inverse_two = norm(middle)
    normed_two = unit_two.astype(BF16)
    acts, grad_pres, grad_norms = [], [], []
    for at in range(0, count, 2 * TOK):
        here = slice(at, at + 2 * TOK)
        pre = nn(normed_two[here], inner_w[1])
        cdf = 0.5 * (1.0 + lax.erf(pre * math.sqrt(0.5)))
        acts.append((pre * cdf).astype(BF16))
        slope = cdf + pre * (jnp.exp(-0.5 * pre * pre) * (1.0 / math.sqrt(2.0 * math.pi)))
        grad_pre = (slope * nn(grad[here], outer_w[1])).astype(BF16)
        grad_pres.append(grad_pre)
        grad_norms.append(nt(grad_pre, inner_w[1]))
    act = jnp.concatenate(acts, axis=0)
    grad_pre = jnp.concatenate(grad_pres, axis=0)
    grad_norm = jnp.concatenate(grad_norms, axis=0)
    grad_middle = (grad.astype(F32) + norm_back(unit_two, inverse_two, grad_norm)).astype(BF16)
    index = lax.axis_index("rows")
    last = lax.axis_size("rows") - 1
    per_band = wide // WIN
    raw = nt(grad_middle, proj_w[1])
    grad_mixes = []
    for w in range(count // TOK):
        row = w // per_band * WIN + (iota((TOK, channels), 0) >> 3)
        low = jnp.where(index == 0, HALF, 0)
        high = jnp.where(index == last, HALF + rows, total)
        part = jnp.where((row >= low) & (row < high), raw[w * TOK : (w + 1) * TOK], 0.0)
        grad_mixes.append(part.astype(BF16))

    def weigh(w, term):
        lane = iota((1, width), 1)
        row = w // per_band * WIN + ((lane >> 3) & (WIN - 1))
        col = w % per_band * WIN + (lane & (WIN - 1))
        own = (row >= HALF) & (row < HALF + rows) & (col >= HALF) & (col < HALF + cols)
        return term * jnp.where(own, 1.0, 0.0)

    grad_query, grad_key, grad_value, bias_sum = attend_all_back(
        query, key_t, value, probs_s, grad_mixes, size, weigh
    )
    grad_norm = (
        nt(grad_query.T, weights[0]) + nt(grad_key, weights[1]) + nt(grad_value, weights[2])
    )
    grad_surface = grad_middle.astype(F32) + norm_back(unit_one, inverse_one, grad_norm)
    xs[...] = from_windows(grad_surface, total, wide)
    grad_out[...] = to_windows(xs[HALF : HALF + rows, HALF : HALF + cols, :]).astype(BF16)
    own = own_windows(rows, cols, channels, HALF, HALF + rows)
    low = jnp.where(index == 0, 0, HALF)
    high = jnp.where(index == last, total, HALF + rows)
    normed_one = normed_one * own_windows(rows, cols, channels, low, high)
    count = lax.axis_size("cols")
    qkv = [nn(grad_query, normed_one), tn(grad_key, normed_one), tn(grad_value, normed_one)]
    blocks = joined(
        narrow_units(
            [jnp.concatenate(qkv, axis=0), nn(mix_t, grad_middle * own).T], count
        ),
        narrow_units([tn(grad_pre, normed_two * own)], count),
        wide_units(tn(grad * own, act), 2 * channels, count),
    )
    tails = [table_tail([fold_bias(bias_sum)], 2 * channels)]
    write_parts(sort_by(blocks, lax.axis_index("cols") & 1, 2), tails, (keep, send))


def third_kernel(
    grad_ref, middle_ref, act, slope, inner_w, outer_w, grad_out, keep, send
):
    count = grad_ref.shape[0]
    grad = grad_ref[...]
    unit, inverse = norm(middle_ref[...].astype(F32))
    grad_pres, grad_norms = [], []
    for at in range(0, count, 2 * TOK):
        here = slice(at, at + 2 * TOK)
        grad_pre = (slope[here] * nn(grad[here], outer_w[0])).astype(BF16)
        grad_pres.append(grad_pre)
        grad_norms.append(nt(grad_pre, inner_w[0]))
    grad_pre = jnp.concatenate(grad_pres, axis=0)
    grad_norm = jnp.concatenate(grad_norms, axis=0)
    grad_out[...] = (grad.astype(F32) + norm_back(unit, inverse, grad_norm)).astype(BF16)
    number = lax.axis_size("cols")
    blocks = joined(
        narrow_units([tn(grad_pre, unit.astype(BF16))], number),
        wide_units(tn(grad, act[...]), 2 * grad.shape[1], number),
    )
    write_parts(sort_by(blocks, lax.axis_index("cols") & 1, 2), [], (keep, send))


def fourth_kernel(
    tokens,
    grad_ref,
    query,
    key_t,
    value,
    probs_ref,
    mix_t,
    qkv_w,
    proj_w,
    token_grad,
    keep,
    send,
):
    rows, cols, channels = tokens.shape
    width = probs_ref.shape[2]
    size = channels // (width // TOK)
    count = rows * cols
    unit_one, inverse_one = norm(to_windows(tokens[...].astype(F32)))
    normed_one = unit_one.astype(BF16)
    grad_middle = grad_ref[...]
    grad_mix = nt(grad_middle, proj_w[0]).astype(BF16)
    grad_mixes = [grad_mix[at : at + TOK] for at in range(0, count, TOK)]
    grad_query, grad_key, grad_value, bias_sum = attend_all_back(
        query, key_t, value, probs_ref, grad_mixes, size, lambda w, term: term
    )
    weights = [qkv_w[0, :, i * channels : (i + 1) * channels] for i in range(3)]
    grad_norm = (
        nt(grad_query.T, weights[0]) + nt(grad_key, weights[1]) + nt(grad_value, weights[2])
    )
    grad_surface = grad_middle.astype(F32) + norm_back(unit_one, inverse_one, grad_norm)
    token_grad[...] = from_windows(grad_surface, rows, cols).astype(BF16)
    number = lax.axis_size("cols")
    qkv = [nn(grad_query, normed_one), tn(grad_key, normed_one), tn(grad_value, normed_one)]
    blocks = narrow_units(
        [jnp.concatenate(qkv, axis=0), nn(mix_t[...], grad_middle).T], number
    )
    tails = [table_tail([fold_bias(bias_sum)], 2 * channels)]
    write_parts(sort_by(blocks, lax.axis_index("cols") & 1, 2), tails, (keep, send))


def summed(refs):
    values = [ref[...].astype(F32) for ref in refs]
    if len(values) == 4:
        values = [values[i] for i in ORDERED]
    return tree_sum(values)


def cut(values, count):
    rows = values.shape[0] // count
    return [values[i * rows : (i + 1) * rows] for i in range(count)]


def ordered(parts):
    return [parts[i] for i in ARRIVAL] if len(parts) == 4 else parts


def join_kernel(count, bit, ways, *refs):
    two, ffn, att = (summed(refs[i : i + 2]) for i in (0, 2, 4))
    tail = 2 * WIN
    blocks = joined(
        cut(att[: att.shape[0] - tail], count), cut(ffn, count), cut(two[: two.shape[0] - tail], count)
    )
    tables = [rows_table(part[part.shape[0] - tail :]) for part in (att, two)]
    place = (lax.axis_index("cols") >> bit) & (ways - 1)
    tails = [table_tail(tables, att.shape[1])]
    write_parts(ordered(sort_by(blocks, place, ways)), tails, refs[6:])


def step_kernel(axis, count, bit, before, ways, tail, *refs):
    both = summed(refs[:before])
    edge = both.shape[0] - tail
    place = (lax.axis_index(axis) >> bit) & (ways - 1)
    parts = sort_by(cut(both[:edge], count), place, ways)
    write_parts(ordered(parts), [both[edge:]], refs[before:])


def dense(block, used):
    if used * 4 != LANES * 3:
        pad = jnp.zeros((block.shape[0], LANES - used), F32)
        return jnp.concatenate([block, pad], axis=1)
    cut_at = block.shape[0] // 4
    side = jnp.concatenate(
        [block[3 * cut_at :, a : a + LANES // 4] for a in range(0, used, LANES // 4)], axis=0
    )
    return jnp.concatenate([block[: 3 * cut_at], side], axis=1)


def undense(block, used):
    if used * 4 != LANES * 3:
        return block
    cut_at = block.shape[0] // 3
    side = [block[i * cut_at : (i + 1) * cut_at, used:] for i in range(3)]
    return jnp.concatenate([block[:, :used], jnp.concatenate(side, axis=1)], axis=0)


def turn_kernel(channels, hidden, before, ways, *refs):
    both = summed(refs[:before])
    count = lax.axis_size("rows")
    edge = both.shape[0] - 2 * WIN
    used = 2 * channels // count
    pieces = [
        row_pieces(unit, n % 3 == 2, channels, hidden, count)
        for n, unit in enumerate(cut(both[:edge], 6))
    ]
    halves = [[dense(b, used) for b in joined(*pieces[n : n + 3])] for n in (0, 3)]
    parts = sort_by(joined(*halves), lax.axis_index("rows") & (ways - 1), ways)
    tables = [rows_table(both[edge + n * WIN : edge + (n + 1) * WIN]) for n in range(2)]
    write_parts(ordered(parts), [table_tail(tables, LANES)], refs[before:])


def last_kernel(sizes, scale, before, *refs):
    (qkv_cols, inner_cols, proj_cols), thin, broad = sizes
    qkv, proj, inner, outer, table = refs[before:]
    total = summed(refs[:before]) * scale
    edge = total.shape[0] - 4 * WIN
    heads = table.shape[0]
    onehot = offset_rows(table.shape[2])
    for b in range(2):
        both = undense(total[b * edge // 2 : (b + 1) * edge // 2], 2 * thin)
        low, mid, wide = cut(both, 3)
        low = jnp.concatenate([low[:, :thin], low[:, thin : 2 * thin]], axis=0)
        mid = jnp.concatenate([mid[:, :thin], mid[:, thin : 2 * thin]], axis=0)
        qkv[b] = low[:qkv_cols].T
        proj[b] = low[qkv_cols:]
        inner[b] = mid.T
        outer[b] = jnp.concatenate(
            [part[:, : 2 * thin] for part in cut(wide, broad // (2 * thin))], axis=1
        )
        sums = rows_table(total[edge + 2 * b * WIN : edge + 2 * (b + 1) * WIN])
        table[:, b] = sum(nt(part, onehot) for part in split(sums, 2))[:heads]


def call(kernel, outs, scratch, *operands, cost=0.2):
    return pl.pallas_call(
        kernel,
        out_shape=[jax.ShapeDtypeStruct(shape, kind) for shape, kind in outs],
        scratch_shapes=scratch,
        cost_estimate=pl.CostEstimate(
            flops=int(cost * 1e9), bytes_accessed=1024, transcendentals=0
        ),
        compiler_params=pltpu.CompilerParams(vmem_limit_bytes=VMEM_LIMIT),
    )(*operands)


def flip(values, axis, bit):
    count = lax.axis_size(axis)
    return lax.ppermute(values, axis, [(i, i ^ bit) for i in range(count)])


def swap(values, axis, offset, periodic):
    count = lax.axis_size(axis)
    pairs = []
    for i in range(offset, count, 2):
        j = (i + 1) % count
        if periodic or i + 1 < count:
            pairs += [(i, j), (j, i)]
    return lax.ppermute(values, axis, pairs)


def spread_parts(parts, axis, bit):
    ways = len(parts)
    order = ARRIVAL if ways == 4 else range(ways)
    return [flip(part, axis, j << bit) if j else part for j, part in zip(order, parts)]


def bit_groups(bits, size):
    return [min(size, bits - at) for at in range(0, bits, size)]


def reduce_terms(pairs, channels, hidden, units):
    got = []
    for keep, send in pairs:
        got += [keep, flip(send, "cols", 1)]
    count = lax.axis_size("cols") // 2
    tail = 2 * WIN
    bit = 1
    for size in bit_groups(count.bit_length() - 1, 2):
        ways = 1 << size
        shape = ((count // ways * units * 6 + tail, 2 * channels), BF16)
        if bit == 1:
            kernel = functools.partial(join_kernel, count, bit, ways)
        else:
            kernel = functools.partial(step_kernel, "cols", count, bit, len(got), ways, tail)
        got = spread_parts(call(kernel, [shape] * ways, [], *got), "cols", bit)
        bit += size
        count //= ways
    count = lax.axis_size("rows")
    thin = channels // count
    rows = units * 3 // 4 * 3 if 8 * thin == 3 * LANES else units * 3
    tail = 4 * WIN
    bit = 0
    for size in bit_groups(count.bit_length() - 1, 2):
        ways = 1 << size
        shape = ((count // ways * rows * 2 + tail, LANES), BF16)
        if bit == 0:
            kernel = functools.partial(turn_kernel, channels, hidden, len(got), ways)
        else:
            kernel = functools.partial(step_kernel, "rows", count, bit, len(got), ways, tail)
        got = spread_parts(call(kernel, [shape] * ways, [], *got), "rows", bit)
        bit += size
        count //= ways
    return got


def local(
    tokens,
    region_ids,
    upper_rim,
    upper_ids,
    lower_rim,
    lower_ids,
    cotangent,
    qkv_weight,
    proj_weight,
    inner_weight,
    outer_weight,
    bias_table,
):
    rows, cols, channels = tokens.shape
    hidden = inner_weight.shape[2]
    length, heads = bias_table.shape[1:]
    outer_weight = jnp.swapaxes(outer_weight, 1, 2)
    bias_table = jnp.transpose(bias_table, (2, 0, 1))
    col_count = lax.axis_size("cols")
    row_count = lax.axis_size("rows")
    count = rows * cols
    width = heads * TOK
    total = rows + 2 * HALF
    flat = ((count, channels), BF16)
    band = (HALF * cols + 2 * WIN, 2 * channels)
    pair = ((TOK, width), F32)
    bias_one, bias_two = call(bias_kernel, [pair, pair], [], bias_table, cost=6.0)
    first_out, near, far, query, key, value, probs, mix, middle, pre, act = call(
        first_kernel,
        [
            ((rows, cols, channels), BF16),
            (band, BF16),
            (band, BF16),
            flat,
            flat,
            flat,
            ((count // TOK, TOK, width), F32),
            ((channels, count), BF16),
            flat,
            ((count, hidden), F32),
            ((count, hidden), BF16),
        ],
        [pltpu.VMEM(band, F32)],
        tokens,
        region_ids,
        cotangent,
        qkv_weight,
        proj_weight,
        inner_weight,
        outer_weight,
        bias_one,
        cost=3.0,
    )
    from_near = swap(near, "rows", 0, False)
    from_far = swap(far, "rows", 1, False)
    slope, key_t = call(
        side_kernel, [((count, hidden), F32), ((channels, count), BF16)], [], pre, key, cost=1.0
    )
    strip = (total * HALF + total, 2 * channels)
    up, down, near, far, ext_ids = call(
        edge_kernel,
        [
            ((HALF * cols, 2 * channels), BF16),
            ((HALF * cols, 2 * channels), BF16),
            (strip, BF16),
            (strip, BF16),
            ((total, cols), F32),
        ],
        [pltpu.VMEM(strip, F32), pltpu.VMEM((total, cols), F32)],
        first_out,
        cotangent,
        region_ids,
        upper_rim,
        upper_ids,
        lower_rim,
        lower_ids,
        from_near,
        from_far,
    )
    near = swap(near, "cols", 0, True)
    far = swap(far, "cols", 1, True)
    units = 4 * channels // col_count // 2
    slots = col_count // 2

    def packed(number, tail):
        return ((slots * number * units + tail, 2 * channels), BF16)

    grid = (total, cols + 2 * HALF, channels)
    grad_first, keep_two, send_two = call(
        second_kernel,
        [flat, packed(3, 2 * WIN), packed(3, 2 * WIN)],
        [
            pltpu.VMEM(grid, F32),
            pltpu.VMEM(grid, F32),
            pltpu.VMEM((grid[0] * grid[1] // TOK, TOK, width), F32),
        ],
        first_out,
        cotangent,
        up,
        down,
        near,
        far,
        ext_ids,
        bias_two,
        qkv_weight,
        proj_weight,
        inner_weight,
        outer_weight,
        cost=12.0,
    )
    grad_middle, keep_ffn, send_ffn = call(
        third_kernel,
        [flat, packed(2, 0), packed(2, 0)],
        [],
        grad_first,
        middle,
        act,
        slope,
        inner_weight,
        outer_weight,
        cost=1.0,
    )
    token_grad, keep_one, send_one = call(
        fourth_kernel,
        [((rows, cols, channels), BF16), packed(1, 2 * WIN), packed(1, 2 * WIN)],
        [],
        tokens,
        grad_middle,
        query,
        key_t,
        value,
        probs,
        mix,
        qkv_weight,
        proj_weight,
        cost=4.0,
    )
    pairs = [(keep_two, send_two), (keep_ffn, send_ffn), (keep_one, send_one)]
    got = reduce_terms(pairs, channels, hidden, units)
    thin = channels // row_count
    broad = hidden // row_count
    sizes = (
        (3 * channels // col_count, hidden // col_count, channels // col_count),
        thin,
        broad,
    )
    qkv_grad, proj_grad, inner_grad, outer_grad, table_grad = call(
        functools.partial(last_kernel, sizes, 1.0 / (row_count * col_count), len(got)),
        [
            ((2, thin, sizes[0][0]), F32),
            ((2, sizes[0][2], thin), F32),
            ((2, thin, sizes[0][1]), F32),
            ((2, sizes[0][2], broad), F32),
            ((heads, 2, length), F32),
        ],
        [],
        *got,
    )
    proj_grad = jnp.swapaxes(proj_grad, 1, 2)
    outer_grad = jnp.swapaxes(outer_grad, 1, 2)
    table_grad = jnp.transpose(table_grad, (1, 2, 0))
    return token_grad, qkv_grad, proj_grad, inner_grad, outer_grad, table_grad


def solution(mesh):
    return jax.shard_map(
        local,
        mesh=mesh,
        in_specs=(
            P("rows", "cols", None),
            P("rows", "cols"),
            P(None, "cols", None),
            P(None, "cols"),
            P(None, "cols", None),
            P(None, "cols"),
            P("rows", "cols", None),
            P(),
            P(),
            P(),
            P(),
            P(),
        ),
        out_specs=(
            P("rows", "cols", None),
            P(None, "rows", "cols"),
            P(None, "rows", "cols"),
            P(None, "rows", "cols"),
            P(None, "rows", "cols"),
            P(),
        ),
        check_vma=False,
    )
```

time: 72.1 us -> 57.1 us (0.79)
  starting transfers between devices: 22.6 us -> 17.7 us
  Pallas kernels: 22 us -> 17.7 us
  local copies, waits for them, and re-layouts: 4.46 us -> 0.98 us
  waiting for transfers between devices: 21.9 us -> 19.7 us
    ppermute x14 -> x13, starting transfers between devices: 22.6 us -> 17.7 us  [the longest x9 11 us: flip(): return lax.ppermute(values, axis, [(i, i ^ bit) for i in range(count)])]
    pallas_call x14 -> x10, Pallas kernels: 22 us -> 17.7 us  [call(): pl.pallas_call(kernel, out_shape=[jax.ShapeDtypeStruct(shape, kind) for s...]
    unnamed x27 -> x24, local copies, waits for them, and re-layouts: 4.46 us -> 0.98 us
    ppermute x14 -> x13, waiting for transfers between devices: 21.9 us -> 19.7 us  [the longest x9 15.9 us: flip(): return lax.ppermute(values, axis, [(i, i ^ bit) for i in range(count)])]
  transfers between devices with their start and end apart: 14 -> 13, of which waited for: 9 -> 8; matrix products, arithmetic and copies ran while one was open for 0% -> 0% of each run, Pallas kernels for 9% -> 6%
where the time goes in v1:
time: 57.1 us; the launch traced here: 56.9 us
  waiting for transfers between devices  19.7 us (35%)
  Pallas kernels  17.7 us (31%)
  starting transfers between devices  17.7 us (31%)
  local copies, waits for them, and re-layouts  0.98 us (2%)
  between operations  0.8 us (1%)
    pallas_call x10, Pallas kernels, call(): pl.pallas_call(kernel, out_shape=[jax.ShapeDtypeStruct(shape, kind) for s...  17.7 us
    ppermute x9, waiting for transfers between devices, flip(): return lax.ppermute(values, axis, [(i, i ^ bit) for i in range(count)])  15.9 us
    ppermute x9, starting transfers between devices, flip(): return lax.ppermute(values, axis, [(i, i ^ bit) for i in range(count)])  11 us
    ppermute x4, starting transfers between devices, swap(): return lax.ppermute(values, axis, pairs)  6.7 us
    ppermute x4, waiting for transfers between devices, swap(): return lax.ppermute(values, axis, pairs)  3.77 us
  transfers between devices with their start and end apart: 13, of which 8 were waited for; matrix products, arithmetic and copies ran while one was open for 0% of the time, Pallas kernels for 6%

profile of v1, /device:TPU:0, one launch (start us, length us, event | category | flops | bytes accessed | tf_op | source)
XLA Modules:
  0.0 56.9 jit_solution(3855545825123586317)
XLA Ops:
  0.6 0.7 %copy-done.8 = f32[2,225,6]{1,0,2:T(2,128)S(1)} copy-done((f32[2,225,6]{1,0,2:T(2,128)S(1)}, f32[2,225,6]{1,0,2:T(2,128)}, u32[]{:S(2)}) %copy-start.8) | copy-done | bytes 10824
  1.4 1.2 %shard_map.163 = (f32[64,384]{1,0:T(8,128)S(1)}, f32[64,384]{1,0:T(8,128)S(1)}) custom-call(f32[6,2,225]{2,1,0:T(2,128)S(1)} %bitcast.8), custom_call_target="tpu_custom_call" | custom-call | flops 6000000000 | bytes 1024 | tf_op jit(solution)/shard_map/pallas_call | solution.py:829
  2.6 0.1 copy-done.2
  2.9 1.9 %shard_map.164 = (bf16[8,32,192]{2,1,0:T(8,128)(2,1)S(1)}, bf16[144,384]{1,0:T(8,128)(2,1)S(1)}, bf16[144,384]{1,0:T(8,128)(2,1)S(1)}, bf16[256,192]{1,0:T(8,128...) custom-call(bf16[8,32,192]{2,1,0:T(8,128)(2,1)S(1)} %copy-done.5, ...), custom_call_target="tpu_custom_call" | custom-call | flops 3000000000 | bytes 1024 | tf_op jit(solution)/shard_map/pallas_call | solution.py:829
  4.8 3.1 %collective-permute-start = (bf16[144,384]{1,0:T(8,128)(2,1)S(1)}, bf16[144,384]{1,0:T(8,128)(2,1)S(1)}, u32[]{:S(2)}, u32[]{:S(2)}) collective-permute-start(bf16[144,384]{1,0:T(8,128)(2,1)S(1)} %get-tuple-element.50), channel_id=1, source_target_pairs={{0,8},{8,0},{16,24},{24,16},{1,9},{9,1},{17,25},{25,17},{2,10},{10... | collective-permute-start | bytes 331784 | tf_op jit(solution)/shard_map/ppermute | solution.py:852
  7.9 0.8 %collective-permute-start.1 = (bf16[144,384]{1,0:T(8,128)(2,1)S(1)}, bf16[144,384]{1,0:T(8,128)(2,1)S(1)}, u32[]{:S(2)}, u32[]{:S(2)}) collective-permute-start(bf16[144,384]{1,0:T(8,128)(2,1)S(1)} %get-tuple-element.51), channel_id=1, source_target_pairs={{8,16},{16,8},{9,17},{17,9},{10,18},{18,10},{11,19},{19,11},{12,20... | collective-permute-start | bytes 331784 | tf_op jit(solution)/shard_map/ppermute | solution.py:852
  8.7 2.2 %collective-permute-done.from_near = bf16[144,384]{1,0:T(8,128)(2,1)S(1)} collective-permute-done((bf16[144,384]{1,0:T(8,128)(2,1)S(1)}, bf16[144,384]{1,0:T(8,128)(2,1)S(1)}, u32[]{:S(2)}, u32[]{:S(2)}) %collective-permute-start) | collective-permute-done | bytes 110624 | tf_op jit(solution)/shard_map/ppermute | solution.py:852
  10.9 0.2 shard_map.165
  11.1 0.1 collective-permute-start.2
  11.2 2.7 %collective-permute-start.3 = (bf16[80,384]{1,0:T(8,128)(2,1)S(1)}, bf16[80,384]{1,0:T(8,128)(2,1)S(1)}, u32[]{:S(2)}, u32[]{:S(2)}) collective-permute-start(bf16[80,384]{1,0:T(8,128)(2,1)S(1)} %get-tuple-element.55), channel_id=1, source_target_pairs={{1,2},{2,1},{3,4},{4,3},{5,6},{6,5},{7,0},{0,7},{9,10},{10,9},{11,... | collective-permute-start | bytes 184328 | tf_op jit(solution)/shard_map/ppermute | solution.py:852
  13.9 0.3 shard_map.167
  14.3 1.6 %collective-permute-done.3.far = bf16[80,384]{1,0:T(8,128)(2,1)S(1)} collective-permute-done((bf16[80,384]{1,0:T(8,128)(2,1)S(1)}, bf16[80,384]{1,0:T(8,128)(2,1)S(1)}, u32[]{:S(2)}, u32[]{:S(2)}) %collective-permute-start.3) | collective-permute-done | bytes 61472 | tf_op jit(solution)/shard_map/ppermute | solution.py:852
  15.8 8.9 %shard_map.166 = (bf16[256,192]{1,0:T(8,128)(2,1)S(1)}, bf16[592,384]{1,0:T(8,128)(2,1)S(1)}, bf16[592,384]{1,0:T(8,128)(2,1)S(1)}) custom-call(bf16[8,32,192]{2,1,0:T(8,128)(2,1)S(1)} %get-tuple-element.49.first_out, bf16[8,32,192]{2,1,0:T(8,128)(2,1)S(1)} %copy-done.4, bf16[128,384]{1,0:T(8,128)(2,1)S(1)} %get-tuple-element.52.up, ...), custom_call_target="tpu_custom_call" | custom-call | flops 12000000000 | bytes 1024 | tf_op jit(solution)/shard_map/pallas_call | solution.py:829
  24.8 0.1 collective-permute-start.4
  24.9 0.7 %shard_map.168 = (bf16[256,192]{1,0:T(8,128)(2,1)S(1)}, bf16[384,384]{1,0:T(8,128)(2,1)S(1)}, bf16[384,384]{1,0:T(8,128)(2,1)S(1)}) custom-call(bf16[256,192]{1,0:T(8,128)(2,1)S(1)} %get-tuple-element.58.grad_ref, bf16[256,192]{1,0:T(8,128)(2,1)S(1)} %get-tuple-element.59.middle_ref, bf16[256,768]{1,0:T(8,128)(2,1)S(1)} %get-tuple-element.60.act, ...), custom_call_target="tpu_custom_call" | custom-call | flops 1000000000 | bytes 1024 | tf_op jit(solution)/shard_map/pallas_call | solution.py:829
  25.7 0.5 collective-permute-start.5
  26.2 2.3 %shard_map.169 = (bf16[8,32,192]{2,1,0:T(8,128)(2,1)}, bf16[208,384]{1,0:T(8,128)(2,1)S(1)}, bf16[208,384]{1,0:T(8,128)(2,1)S(1)}) custom-call(bf16[8,32,192]{2,1,0:T(8,128)(2,1)S(1)} %copy-done.5, bf16[256,192]{1,0:T(8,128)(2,1)S(1)} %get-tuple-element.64.grad_ref, bf16[256,192]{1,0:T(8,128)(2,1)S(1)} %get-tuple-element.65.query, ...), custom_call_target="tpu_custom_call" | custom-call | flops 4000000000 | bytes 1024 | tf_op jit(solution)/shard_map/pallas_call | solution.py:829
  28.5 1.3 %collective-permute-done.6.refs_5_ = bf16[208,384]{1,0:T(8,128)(2,1)S(1)} collective-permute-done((bf16[208,384]{1,0:T(8,128)(2,1)S(1)}, bf16[208,384]{1,0:T(8,128)(2,1)S(1)}, u32[]{:S(2)}, u32[]{:S(2)}) %collective-permute-start.6) | collective-permute-done | bytes 159776 | tf_op jit(solution)/shard_map/ppermute | solution.py:842
  29.9 0.4 shard_map.170
  30.3 2.8 %collective-permute-start.7 = (bf16[304,384]{1,0:T(8,128)(2,1)S(1)}, bf16[304,384]{1,0:T(8,128)(2,1)S(1)}, u32[]{:S(2)}, u32[]{:S(2)}) collective-permute-start(bf16[304,384]{1,0:T(8,128)(2,1)S(1)} %get-tuple-element.78), channel_id=1, source_target_pairs={{0,6},{1,7},{2,4},{3,5},{4,2},{5,3},{6,0},{7,1},{8,14},{9,15},{10,... | collective-permute-start | bytes 700424 | tf_op jit(solution)/shard_map/ppermute | solution.py:842
  33.0 0.6 %collective-permute-start.8 = (bf16[304,384]{1,0:T(8,128)(2,1)S(1)}, bf16[304,384]{1,0:T(8,128)(2,1)S(1)}, u32[]{:S(2)}, u32[]{:S(2)}) collective-permute-start(bf16[304,384]{1,0:T(8,128)(2,1)S(1)} %get-tuple-element.79), channel_id=1, source_target_pairs={{0,4},{1,5},{2,6},{3,7},{4,0},{5,1},{6,2},{7,3},{8,12},{9,13},{10,... | collective-permute-start | bytes 700424 | tf_op jit(solution)/shard_map/ppermute | solution.py:842
  33.6 0.2 collective-permute-start.9
  33.8 6.0 %collective-permute-done.7.refs_1_ = bf16[304,384]{1,0:T(8,128)(2,1)S(1)} collective-permute-done((bf16[304,384]{1,0:T(8,128)(2,1)S(1)}, bf16[304,384]{1,0:T(8,128)(2,1)S(1)}, u32[]{:S(2)}, u32[]{:S(2)}) %collective-permute-start.7) | collective-permute-done | bytes 233504 | tf_op jit(solution)/shard_map/ppermute | solution.py:842
  39.8 4.4 %collective-permute-done.8.refs_2_ = bf16[304,384]{1,0:T(8,128)(2,1)S(1)} collective-permute-done((bf16[304,384]{1,0:T(8,128)(2,1)S(1)}, bf16[304,384]{1,0:T(8,128)(2,1)S(1)}, u32[]{:S(2)}, u32[]{:S(2)}) %collective-permute-start.8) | collective-permute-done | bytes 233504 | tf_op jit(solution)/shard_map/ppermute | solution.py:842
  44.2 0.2 collective-permute-done.9.refs_3_
  44.4 0.8 %shard_map.171 = (bf16[248,128]{1,0:T(8,128)(2,1)S(1)}, bf16[248,128]{1,0:T(8,128)(2,1)S(1)}, bf16[248,128]{1,0:T(8,128)(2,1)S(1)}, bf16[248,128]{1,0:T(8,128)(2,1)S(1)}) custom-call(bf16[304,384]{1,0:T(8,128)(2,1)S(1)} %get-tuple-element.77.refs_0_, bf16[304,384]{1,0:T(8,128)(2,1)S(1)} %collective-permute-done.7.refs_1_, ...), custom_call_target="tpu_custom_call" | custom-call | flops 200000000 | bytes 1024 | tf_op jit(solution)/shard_map/pallas_call | solution.py:829
  45.2 3.8 %collective-permute-start.10 = (bf16[248,128]{1,0:T(8,128)(2,1)S(1)}, bf16[248,128]{1,0:T(8,128)(2,1)S(1)}, u32[]{:S(2)}, u32[]{:S(2)}) collective-permute-start(bf16[248,128]{1,0:T(8,128)(2,1)S(1)} %get-tuple-element.82), channel_id=1, source_target_pairs={{0,24},{8,16},{16,8},{24,0},{1,25},{9,17},{17,9},{25,1},{2,26},{10... | collective-permute-start | bytes 190472 | tf_op jit(solution)/shard_map/ppermute | solution.py:842
  49.0 2.5 %collective-permute-start.11 = (bf16[248,128]{1,0:T(8,128)(2,1)S(1)}, bf16[248,128]{1,0:T(8,128)(2,1)S(1)}, u32[]{:S(2)}, u32[]{:S(2)}) collective-permute-start(bf16[248,128]{1,0:T(8,128)(2,1)S(1)} %get-tuple-element.83), channel_id=1, source_target_pairs={{0,16},{8,24},{16,0},{24,8},{1,17},{9,25},{17,1},{25,9},{2,18},{10... | collective-permute-start | bytes 190472 | tf_op jit(solution)/shard_map/ppermute | solution.py:842
  51.5 0.5 collective-permute-start.12
  52.0 3.5 %collective-permute-done.11.refs_2_ = bf16[248,128]{1,0:T(8,128)(2,1)S(1)} collective-permute-done((bf16[248,128]{1,0:T(8,128)(2,1)S(1)}, bf16[248,128]{1,0:T(8,128)(2,1)S(1)}, u32[]{:S(2)}, u32[]{:S(2)}) %collective-permute-start.11) | collective-permute-done | bytes 63520 | tf_op jit(solution)/shard_map/ppermute | solution.py:842
  55.5 0.5 collective-permute-done.12.refs_3_
  56.0 0.9 %shard_map.172 = (f32[2,48,72]{2,1,0:T(8,128)}, f32[2,24,48]{2,1,0:T(8,128)}, f32[2,48,96]{2,1,0:T(8,128)}, f32[2,24,192]{2,1,0:T(8,128)}, f32[6,2,225]{2,1,0:T(2,128)}) custom-call(bf16[248,128]{1,0:T(8,128)(2,1)S(1)} %get-tuple-element.81.refs_0_, bf16[248,128]{1,0:T(8,128)(2,1)S(1)} %collective-permute-done.10.refs_1_, ...), custom_call_target="tpu_custom_call" | custom-call | flops 200000000 | bytes 1024 | tf_op jit(solution)/shard_map/pallas_call | solution.py:829
  (28 shorter events, 0.2 us)
Async XLA Ops:
  0.6 0.7 %copy-start.8 = (f32[2,225,6]{1,0,2:T(2,128)S(1)}, f32[2,225,6]{1,0,2:T(2,128)}, u32[]{:S(2)}) copy-start(f32[2,225,6]{1,0,2:T(2,128)} %param.23) | copy-start | bytes 32404
  1.3 1.2 %copy-start = (bf16[2,192,768]{2,1,0:T(8,128)(2,1)S(1)}, bf16[2,192,768]{2,1,0:T(8,128)(2,1)}, u32[]{:S(2)}) copy-start(bf16[2,192,768]{2,1,0:T(8,128)(2,1)} %inner_w.5) | copy-start | bytes 1769476
  1.3 1.3 %copy-start.1 = (bf16[2,768,192]{1,2,0:T(8,128)(2,1)S(1)}, bf16[2,768,192]{1,2,0:T(8,128)(2,1)}, u32[]{:S(2)}) copy-start(bf16[2,768,192]{1,2,0:T(8,128)(2,1)} %param.22) | copy-start | bytes 1769476
  1.3 1.4 %copy-start.2 = (bf16[2,192,576]{2,1,0:T(8,128)(2,1)S(1)}, bf16[2,192,576]{2,1,0:T(8,128)(2,1)}, u32[]{:S(2)}) copy-start(bf16[2,192,576]{2,1,0:T(8,128)(2,1)} %qkv_w.5) | copy-start | bytes 1327108
  1.3 1.4 %copy-start.3 = (bf16[2,192,192]{2,1,0:T(8,128)(2,1)S(1)}, bf16[2,192,192]{2,1,0:T(8,128)(2,1)}, u32[]{:S(2)}) copy-start(bf16[2,192,192]{2,1,0:T(8,128)(2,1)} %proj_w.5) | copy-start | bytes 442372
  1.4 1.5 %copy-start.4 = (bf16[8,32,192]{2,1,0:T(8,128)(2,1)S(1)}, bf16[8,32,192]{2,1,0:T(8,128)(2,1)}, u32[]{:S(2)}) copy-start(bf16[8,32,192]{2,1,0:T(8,128)(2,1)} %cotangent.5) | copy-start | bytes 294916
  1.4 1.5 %copy-start.5 = (bf16[8,32,192]{2,1,0:T(8,128)(2,1)S(1)}, bf16[8,32,192]{2,1,0:T(8,128)(2,1)}, u32[]{:S(2)}) copy-start(bf16[8,32,192]{2,1,0:T(8,128)(2,1)} %tokens.3) | copy-start | bytes 294916
  1.4 1.5 %copy-start.9 = (s32[8,32]{1,0:T(8,128)S(1)}, s32[8,32]{1,0:T(8,128)}, u32[]{:S(2)}) copy-start(s32[8,32]{1,0:T(8,128)} %ids.3) | copy-start | bytes 3076
  2.9 8.1 %copy-start.6 = (bf16[4,32,192]{2,1,0:T(8,128)(2,1)S(1)}, bf16[4,32,192]{2,1,0:T(8,128)(2,1)}, u32[]{:S(2)}) copy-start(bf16[4,32,192]{2,1,0:T(8,128)(2,1)} %upper_rim.1) | copy-start | bytes 147460
  2.9 8.1 %copy-start.7 = (bf16[4,32,192]{2,1,0:T(8,128)(2,1)S(1)}, bf16[4,32,192]{2,1,0:T(8,128)(2,1)}, u32[]{:S(2)}) copy-start(bf16[4,32,192]{2,1,0:T(8,128)(2,1)} %lower_rim.1) | copy-start | bytes 147460
  4.7 6.2 %copy-start.11 = (s32[4,32]{1,0:T(4,128)S(1)}, s32[4,32]{1,0:T(4,128)}, u32[]{:S(2)}) copy-start(s32[4,32]{1,0:T(4,128)} %lower_ids.1) | copy-start | bytes 1540
  4.8 6.2 %copy-start.10 = (s32[4,32]{1,0:T(4,128)S(1)}, s32[4,32]{1,0:T(4,128)}, u32[]{:S(2)}) copy-start(s32[4,32]{1,0:T(4,128)} %upper_ids.1) | copy-start | bytes 1540
  4.8 6.1 %collective-permute-start = (bf16[144,384]{1,0:T(8,128)(2,1)S(1)}, bf16[144,384]{1,0:T(8,128)(2,1)S(1)}, u32[]{:S(2)}, u32[]{:S(2)}) collective-permute-start(bf16[144,384]{1,0:T(8,128)(2,1)S(1)} %get-tuple-element.50), channel_id=1, source_target_pairs={{0,8},{8,0},{16,24},{24,16},{1,9},{9,1},{17,25},{25,17},{2,10},{10... | collective-permute-start | bytes 331784 | tf_op jit(solution)/shard_map/ppermute | solution.py:852
  7.9 3.1 %collective-permute-start.1 = (bf16[144,384]{1,0:T(8,128)(2,1)S(1)}, bf16[144,384]{1,0:T(8,128)(2,1)S(1)}, u32[]{:S(2)}, u32[]{:S(2)}) collective-permute-start(bf16[144,384]{1,0:T(8,128)(2,1)S(1)} %get-tuple-element.51), channel_id=1, source_target_pairs={{8,16},{16,8},{9,17},{17,9},{10,18},{18,10},{11,19},{19,11},{12,20... | collective-permute-start | bytes 331784 | tf_op jit(solution)/shard_map/ppermute | solution.py:852
  11.1 3.1 %collective-permute-start.2 = (bf16[80,384]{1,0:T(8,128)(2,1)S(1)}, bf16[80,384]{1,0:T(8,128)(2,1)S(1)}, u32[]{:S(2)}, u32[]{:S(2)}) collective-permute-start(bf16[80,384]{1,0:T(8,128)(2,1)S(1)} %get-tuple-element.54), channel_id=1, source_target_pairs={{0,1},{1,0},{2,3},{3,2},{4,5},{5,4},{6,7},{7,6},{8,9},{9,8},{10,11... | collective-permute-start | bytes 184328 | tf_op jit(solution)/shard_map/ppermute | solution.py:852
  11.2 4.6 %collective-permute-start.3 = (bf16[80,384]{1,0:T(8,128)(2,1)S(1)}, bf16[80,384]{1,0:T(8,128)(2,1)S(1)}, u32[]{:S(2)}, u32[]{:S(2)}) collective-permute-start(bf16[80,384]{1,0:T(8,128)(2,1)S(1)} %get-tuple-element.55), channel_id=1, source_target_pairs={{1,2},{2,1},{3,4},{4,3},{5,6},{6,5},{7,0},{0,7},{9,10},{10,9},{11,... | collective-permute-start | bytes 184328 | tf_op jit(solution)/shard_map/ppermute | solution.py:852
  24.8 5.1 %collective-permute-start.4 = (bf16[592,384]{1,0:T(8,128)(2,1)S(1)}, bf16[592,384]{1,0:T(8,128)(2,1)S(1)}, u32[]{:S(2)}, u32[]{:S(2)}) collective-permute-start(bf16[592,384]{1,0:T(8,128)(2,1)S(1)} %get-tuple-element.72), channel_id=1, source_target_pairs={{0,1},{1,0},{2,3},{3,2},{4,5},{5,4},{6,7},{7,6},{8,9},{9,8},{10,11... | collective-permute-start | bytes 1363976 | tf_op jit(solution)/shard_map/ppermute | solution.py:842
  25.7 4.2 %collective-permute-start.5 = (bf16[384,384]{1,0:T(8,128)(2,1)S(1)}, bf16[384,384]{1,0:T(8,128)(2,1)S(1)}, u32[]{:S(2)}, u32[]{:S(2)}) collective-permute-start(bf16[384,384]{1,0:T(8,128)(2,1)S(1)} %get-tuple-element.74), channel_id=1, source_target_pairs={{0,1},{1,0},{2,3},{3,2},{4,5},{5,4},{6,7},{7,6},{8,9},{9,8},{10,11... | collective-permute-start | bytes 884744 | tf_op jit(solution)/shard_map/ppermute | solution.py:842
  28.5 1.4 %collective-permute-start.6 = (bf16[208,384]{1,0:T(8,128)(2,1)S(1)}, bf16[208,384]{1,0:T(8,128)(2,1)S(1)}, u32[]{:S(2)}, u32[]{:S(2)}) collective-permute-start(bf16[208,384]{1,0:T(8,128)(2,1)S(1)} %get-tuple-element.76), channel_id=1, source_target_pairs={{0,1},{1,0},{2,3},{3,2},{4,5},{5,4},{6,7},{7,6},{8,9},{9,8},{10,11... | collective-permute-start | bytes 479240 | tf_op jit(solution)/shard_map/ppermute | solution.py:842
  30.3 9.5 %collective-permute-start.7 = (bf16[304,384]{1,0:T(8,128)(2,1)S(1)}, bf16[304,384]{1,0:T(8,128)(2,1)S(1)}, u32[]{:S(2)}, u32[]{:S(2)}) collective-permute-start(bf16[304,384]{1,0:T(8,128)(2,1)S(1)} %get-tuple-element.78), channel_id=1, source_target_pairs={{0,6},{1,7},{2,4},{3,5},{4,2},{5,3},{6,0},{7,1},{8,14},{9,15},{10,... | collective-permute-start | bytes 700424 | tf_op jit(solution)/shard_map/ppermute | solution.py:842
  33.0 11.2 %collective-permute-start.8 = (bf16[304,384]{1,0:T(8,128)(2,1)S(1)}, bf16[304,384]{1,0:T(8,128)(2,1)S(1)}, u32[]{:S(2)}, u32[]{:S(2)}) collective-permute-start(bf16[304,384]{1,0:T(8,128)(2,1)S(1)} %get-tuple-element.79), channel_id=1, source_target_pairs={{0,4},{1,5},{2,6},{3,7},{4,0},{5,1},{6,2},{7,3},{8,12},{9,13},{10,... | collective-permute-start | bytes 700424 | tf_op jit(solution)/shard_map/ppermute | solution.py:842
  33.6 10.8 %collective-permute-start.9 = (bf16[304,384]{1,0:T(8,128)(2,1)S(1)}, bf16[304,384]{1,0:T(8,128)(2,1)S(1)}, u32[]{:S(2)}, u32[]{:S(2)}) collective-permute-start(bf16[304,384]{1,0:T(8,128)(2,1)S(1)} %get-tuple-element.80), channel_id=1, source_target_pairs={{0,2},{1,3},{2,0},{3,1},{4,6},{5,7},{6,4},{7,5},{8,10},{9,11},{10,... | collective-permute-start | bytes 700424 | tf_op jit(solution)/shard_map/ppermute | solution.py:842
  45.2 6.8 %collective-permute-start.10 = (bf16[248,128]{1,0:T(8,128)(2,1)S(1)}, bf16[248,128]{1,0:T(8,128)(2,1)S(1)}, u32[]{:S(2)}, u32[]{:S(2)}) collective-permute-start(bf16[248,128]{1,0:T(8,128)(2,1)S(1)} %get-tuple-element.82), channel_id=1, source_target_pairs={{0,24},{8,16},{16,8},{24,0},{1,25},{9,17},{17,9},{25,1},{2,26},{10... | collective-permute-start | bytes 190472 | tf_op jit(solution)/shard_map/ppermute | solution.py:842
  49.0 6.5 %collective-permute-start.11 = (bf16[248,128]{1,0:T(8,128)(2,1)S(1)}, bf16[248,128]{1,0:T(8,128)(2,1)S(1)}, u32[]{:S(2)}, u32[]{:S(2)}) collective-permute-start(bf16[248,128]{1,0:T(8,128)(2,1)S(1)} %get-tuple-element.83), channel_id=1, source_target_pairs={{0,16},{8,24},{16,0},{24,8},{1,17},{9,25},{17,1},{25,9},{2,18},{10... | collective-permute-start | bytes 190472 | tf_op jit(solution)/shard_map/ppermute | solution.py:842
  51.5 4.5 %collective-permute-start.12 = (bf16[248,128]{1,0:T(8,128)(2,1)S(1)}, bf16[248,128]{1,0:T(8,128)(2,1)S(1)}, u32[]{:S(2)}, u32[]{:S(2)}) collective-permute-start(bf16[248,128]{1,0:T(8,128)(2,1)S(1)} %get-tuple-element.84), channel_id=1, source_target_pairs={{0,8},{8,0},{16,24},{24,16},{1,9},{9,1},{17,25},{25,17},{2,10},{10... | collective-permute-start | bytes 190472 | tf_op jit(solution)/shard_map/ppermute | solution.py:842

commit v2 on v1

--- a/solution.py
+++ b/solution.py
@@ -19,6 +19,8 @@
 BF16 = jnp.bfloat16
 ARRIVAL = (0, 3, 2, 1)
 ORDERED = (0, 3, 2, 1)
+TURN_COST = 20.0
+FILL = 1
 VMEM_LIMIT = 40 * 1024 * 1024
 
 
@@ -236,9 +238,18 @@
 
 
 def offset_places():
-    lane = iota((2 * LANES, WIN * LANES), 1)
-    row = ((lane >> 3) & (WIN - 1)) - (lane >> 7) + WIN - 1
-    return ones_where(iota((2 * LANES, WIN * LANES), 0) == 2 * WIN * row + (lane & (WIN - 1)))
+    lane = iota((2 * LANES, LANES), 1)
+    return ones_where(iota((2 * LANES, LANES), 0) == 2 * WIN * (lane >> 3) + (lane & (WIN - 1)))
+
+
+def shifted(values, first, last):
+    place = iota(values.shape, 0) & (WIN - 1)
+    result = values
+    for c in range(WIN):
+        shift = (first + (last - first) // (WIN - 1) * c) % values.shape[1]
+        if shift:
+            result = jnp.where(place == c, pltpu.roll(values, shift, 1), result)
+    return result
 
 
 def expand_bias(table):
@@ -248,28 +259,54 @@
     base = jnp.concatenate(
         [jnp.broadcast_to(rows[h : h + 1], (WIN, 2 * LANES)) for h in range(heads)], axis=0
     )
-    place = iota(base.shape, 0) & (WIN - 1)
-    rolled = base
-    for c in range(WIN - 1):
-        rolled = jnp.where(place == c, pltpu.roll(base, c + 2 * LANES - WIN + 1, 1), rolled)
     places = offset_places()
-    spreaded = sum(nn(part, places) for part in split(rolled, 3))
+    spreaded = sum(nn(part, places) for part in split(shifted(base, 1 - WIN, 0), 3))
     left = iota((WIN, LANES), 1) < TOK
     columns = []
     for h in range(0, heads, 2):
-        pieces = [
-            jnp.where(
-                left,
-                spreaded[h * WIN : (h + 1) * WIN, r * LANES : (r + 1) * LANES],
-                spreaded[(h + 1) * WIN : (h + 2) * WIN, r * LANES : (r + 1) * LANES],
-            )
-            for r in range(WIN)
-        ]
+        first = spreaded[h * WIN : (h + 1) * WIN]
+        second = spreaded[(h + 1) * WIN : (h + 2) * WIN]
+        pieces = []
+        for r in range(WIN):
+            back = LANES - WIN * (WIN - 1 - r)
+            one = pltpu.roll(first, back % LANES, 1) if back % LANES else first
+            two = pltpu.roll(second, (back + TOK) % LANES, 1)
+            pieces.append(jnp.where(left, one, two))
         columns.append(jnp.concatenate(pieces, axis=0))
     return jnp.concatenate(columns, axis=1)
 
 
 def fold_bias(grad):
+    heads = grad.shape[1] // TOK
+    left = iota((WIN, LANES), 1) < TOK
+    rows = []
+    for h in range(heads):
+        at = h // 2 * LANES
+        total = None
+        for r in range(WIN):
+            piece = grad[r * WIN : (r + 1) * WIN, at : at + LANES]
+            piece = jnp.where(left, piece, 0.0) if h % 2 == 0 else jnp.where(left, 0.0, piece)
+            shift = (WIN * (WIN - 1 - r) + h % 2 * TOK) % LANES
+            piece = pltpu.roll(piece, shift, 1) if shift else piece
+            total = piece if total is None else total + piece
+        rows.append(total)
+    places = offset_places()
+    stacked = jnp.concatenate(rows, axis=0)
+    folded = shifted(sum(nt(part, places) for part in split(stacked, 2)), WIN - 1, 0)
+    sums = [
+        jnp.sum(folded[h * WIN : (h + 1) * WIN], axis=0, keepdims=True) for h in range(heads)
+    ]
+    sums.append(jnp.zeros((WIN - heads, 2 * LANES), F32))
+    return jnp.concatenate(sums, axis=0)
+
+
+def wide_places():
+    lane = iota((2 * LANES, WIN * LANES), 1)
+    row = ((lane >> 3) & (WIN - 1)) - (lane >> 7) + WIN - 1
+    return ones_where(iota((2 * LANES, WIN * LANES), 0) == 2 * WIN * row + (lane & (WIN - 1)))
+
+
+def fold_wide(grad):
     heads = grad.shape[1] // TOK
     left = iota((WIN, LANES), 1) < TOK
     rows = []
@@ -281,8 +318,8 @@
             pieces.append(jnp.where(left, piece, 0.0) if h % 2 == 0 else jnp.where(left, 0.0, piece))
         rows.append(jnp.concatenate(pieces, axis=1))
     stacked = jnp.concatenate(rows, axis=0)
-    places = offset_places()
-    folded = sum(nt(part, places) for part in split(stacked, 3))
+    places = wide_places()
+    folded = sum(nt(part, places) for part in split(stacked, 2))
     place = iota(folded.shape, 0) & (WIN - 1)
     rolled = folded
     for c in range(WIN - 1):
@@ -558,6 +595,7 @@
     proj_w,
     inner_w,
     outer_w,
+    after,
     grad_out,
     keep,
     send,
@@ -702,6 +740,7 @@
     mix_t,
     qkv_w,
     proj_w,
+    after,
     token_grad,
     keep,
     send,
@@ -729,7 +768,7 @@
     blocks = narrow_units(
         [jnp.concatenate(qkv, axis=0), nn(mix_t[...], grad_middle).T], number
     )
-    tails = [table_tail([fold_bias(bias_sum)], 2 * channels)]
+    tails = [table_tail([fold_wide(bias_sum)], 2 * channels)]
     write_parts(sort_by(blocks, lax.axis_index("cols") & 1, 2), tails, (keep, send))
 
 
@@ -749,16 +788,18 @@
     return [parts[i] for i in ARRIVAL] if len(parts) == 4 else parts
 
 
-def join_kernel(count, bit, ways, *refs):
-    two, ffn, att = (summed(refs[i : i + 2]) for i in (0, 2, 4))
-    tail = 2 * WIN
-    blocks = joined(
-        cut(att[: att.shape[0] - tail], count), cut(ffn, count), cut(two[: two.shape[0] - tail], count)
-    )
-    tables = [rows_table(part[part.shape[0] - tail :]) for part in (att, two)]
+def join_kernel(count, bit, ways, tails, *refs):
+    blocks = []
+    table = None
+    for n, tail in enumerate(tails):
+        part = summed(refs[2 * n : 2 * n + 2])
+        edge = part.shape[0] - tail
+        blocks.append(cut(part[:edge], count))
+        table = rows_table(part[edge:]) if tail else table
     place = (lax.axis_index("cols") >> bit) & (ways - 1)
-    tails = [table_tail(tables, att.shape[1])]
-    write_parts(ordered(sort_by(blocks, place, ways)), tails, refs[6:])
+    tail = [table_tail([table], part.shape[1])]
+    parts = ordered(sort_by(joined(*blocks), place, ways))
+    write_parts(parts, tail, refs[len(refs) - ways :])
 
 
 def step_kernel(axis, count, bit, before, ways, tail, *refs):
@@ -769,10 +810,14 @@
     write_parts(ordered(parts), [both[edge:]], refs[before:])
 
 
+def padded(block):
+    pad = jnp.zeros((block.shape[0], LANES - block.shape[1]), F32)
+    return jnp.concatenate([block, pad], axis=1)
+
+
 def dense(block, used):
     if used * 4 != LANES * 3:
-        pad = jnp.zeros((block.shape[0], LANES - used), F32)
-        return jnp.concatenate([block, pad], axis=1)
+        return padded(block)
     cut_at = block.shape[0] // 4
     side = jnp.concatenate(
         [block[3 * cut_at :, a : a + LANES // 4] for a in range(0, used, LANES // 4)], axis=0
@@ -788,19 +833,34 @@
     return jnp.concatenate([block[:, :used], jnp.concatenate(side, axis=1)], axis=0)
 
 
-def turn_kernel(channels, hidden, before, ways, *refs):
+def first_turn_kernel(channels, hidden, before, *refs):
     both = summed(refs[:before])
+    two, ffn, table = refs[before:]
     count = lax.axis_size("rows")
     edge = both.shape[0] - 2 * WIN
     used = 2 * channels // count
     pieces = [
-        row_pieces(unit, n % 3 == 2, channels, hidden, count)
-        for n, unit in enumerate(cut(both[:edge], 6))
+        row_pieces(unit, n in (1, 4), channels, hidden, count)
+        for n, unit in enumerate(cut(both[:edge], 5))
     ]
-    halves = [[dense(b, used) for b in joined(*pieces[n : n + 3])] for n in (0, 3)]
-    parts = sort_by(joined(*halves), lax.axis_index("rows") & (ways - 1), ways)
-    tables = [rows_table(both[edge + n * WIN : edge + (n + 1) * WIN]) for n in range(2)]
-    write_parts(ordered(parts), [table_tail(tables, LANES)], refs[before:])
+    ffn[...] = padded(jnp.concatenate(joined(*pieces[:2]), axis=0))
+    two[...] = jnp.concatenate([dense(b, used) for b in joined(*pieces[2:])], axis=0)
+    table[...] = rows_table(both[edge:])
+
+
+def merge_kernel(channels, hidden, before, ways, *refs):
+    both = summed(refs[:before])
+    two, ffn, table = refs[before : before + 3]
+    count = lax.axis_size("rows")
+    edge = both.shape[0] - 2 * WIN
+    used = 2 * channels // count
+    att = row_pieces(both[:edge], False, channels, hidden, count)
+    one = [dense(b, used) for b in joined(att, cut(ffn[...][:, :used], count))]
+    parts = sort_by(
+        joined(one, cut(two[...], count)), lax.axis_index("rows") & (ways - 1), ways
+    )
+    tails = [table_tail([rows_table(both[edge:]), table[...]], LANES)]
+    write_parts(ordered(parts), tails, refs[before + 3 :])
 
 
 def last_kernel(sizes, scale, before, *refs):
@@ -842,14 +902,27 @@
     return lax.ppermute(values, axis, [(i, i ^ bit) for i in range(count)])
 
 
-def swap(values, axis, offset, periodic):
-    count = lax.axis_size(axis)
+def swap_cols(values, offset):
+    count = lax.axis_size("cols")
     pairs = []
     for i in range(offset, count, 2):
         j = (i + 1) % count
-        if periodic or i + 1 < count:
-            pairs += [(i, j), (j, i)]
-    return lax.ppermute(values, axis, pairs)
+        pairs += [(i, j), (j, i)]
+    return lax.ppermute(values, "cols", pairs)
+
+
+def swap_rows(values, offset):
+    count = lax.axis_size("rows")
+    cols = lax.axis_size("cols")
+    partner = {}
+    for i in range(offset, count - 1, 2):
+        partner[i], partner[i + 1] = i + 1, i
+    pairs = []
+    for r in range(count):
+        for c in range(cols):
+            target = (partner[r], c) if r in partner else (r, c ^ FILL)
+            pairs.append((r * cols + c, target[0] * cols + target[1]))
+    return lax.ppermute(values, ("rows", "cols"), pairs)
 
 
 def spread_parts(parts, axis, bit):
@@ -862,33 +935,40 @@
     return [min(size, bits - at) for at in range(0, bits, size)]
 
 
-def reduce_terms(pairs, channels, hidden, units):
+def reduce_cols(pairs, tails, width, units, after=()):
     got = []
     for keep, send in pairs:
         got += [keep, flip(send, "cols", 1)]
     count = lax.axis_size("cols") // 2
     tail = 2 * WIN
     bit = 1
+    kept = None
     for size in bit_groups(count.bit_length() - 1, 2):
         ways = 1 << size
-        shape = ((count // ways * units * 6 + tail, 2 * channels), BF16)
+        shape = ((count // ways * units + tail, width), BF16)
         if bit == 1:
-            kernel = functools.partial(join_kernel, count, bit, ways)
+            kernel = functools.partial(join_kernel, count, bit, ways, tails)
+            got = got + list(after)
         else:
             kernel = functools.partial(step_kernel, "cols", count, bit, len(got), ways, tail)
-        got = spread_parts(call(kernel, [shape] * ways, [], *got), "cols", bit)
+        parts = call(kernel, [shape] * ways, [], *got)
+        kept = parts[0] if kept is None else kept
+        got = spread_parts(parts, "cols", bit)
         bit += size
         count //= ways
+    return got, kept
+
+
+def reduce_rows(got, others, channels, hidden, rows):
     count = lax.axis_size("rows")
-    thin = channels // count
-    rows = units * 3 // 4 * 3 if 8 * thin == 3 * LANES else units * 3
     tail = 4 * WIN
     bit = 0
     for size in bit_groups(count.bit_length() - 1, 2):
         ways = 1 << size
         shape = ((count // ways * rows * 2 + tail, LANES), BF16)
         if bit == 0:
-            kernel = functools.partial(turn_kernel, channels, hidden, len(got), ways)
+            kernel = functools.partial(merge_kernel, channels, hidden, len(got), ways)
+            got = [*got, *others]
         else:
             kernel = functools.partial(step_kernel, "rows", count, bit, len(got), ways, tail)
         got = spread_parts(call(kernel, [shape] * ways, [], *got), "rows", bit)
@@ -951,8 +1031,8 @@
         bias_one,
         cost=3.0,
     )
-    from_near = swap(near, "rows", 0, False)
-    from_far = swap(far, "rows", 1, False)
+    from_near = swap_rows(near, 0)
+    from_far = swap_rows(far, 1)
     slope, key_t = call(
         side_kernel, [((count, hidden), F32), ((channels, count), BF16)], [], pre, key, cost=1.0
     )
@@ -977,8 +1057,8 @@
         from_near,
         from_far,
     )
-    near = swap(near, "cols", 0, True)
-    far = swap(far, "cols", 1, True)
+    near = swap_cols(near, 0)
+    far = swap_cols(far, 1)
     units = 4 * channels // col_count // 2
     slots = col_count // 2
 
@@ -1006,6 +1086,7 @@
         proj_weight,
         inner_weight,
         outer_weight,
+        key_t,
         cost=12.0,
     )
     grad_middle, keep_ffn, send_ffn = call(
@@ -1019,6 +1100,22 @@
         inner_weight,
         outer_weight,
         cost=1.0,
+    )
+    got, kept = reduce_cols(
+        [(keep_ffn, send_ffn), (keep_two, send_two)], (0, 2 * WIN), 2 * channels, 5 * units
+    )
+    thin = channels // row_count
+    piece = units * 3 // 4 * 3 if 8 * thin == 3 * LANES else units * 3
+    others = call(
+        functools.partial(first_turn_kernel, channels, hidden, len(got)),
+        [
+            ((row_count * piece, LANES), F32),
+            ((row_count * 2 * units, LANES), F32),
+            ((WIN, 2 * LANES), F32),
+        ],
+        [],
+        *got,
+        cost=TURN_COST,
     )
     token_grad, keep_one, send_one = call(
         fourth_kernel,
@@ -1033,11 +1130,11 @@
         mix,
         qkv_weight,
         proj_weight,
+        kept,
         cost=4.0,
     )
-    pairs = [(keep_two, send_two), (keep_ffn, send_ffn), (keep_one, send_one)]
-    got = reduce_terms(pairs, channels, hidden, units)
-    thin = channels // row_count
+    got, _ = reduce_cols([(keep_one, send_one)], (2 * WIN,), 2 * channels, units)
+    got = reduce_rows(got, others, channels, hidden, piece)
     broad = hidden // row_count
     sizes = (
         (3 * channels // col_count, hidden // col_count, channels // col_count),

time: 57.1 us -> 52.9 us (0.926)
  waiting for transfers between devices: 19.7 us -> 15.5 us
  Pallas kernels: 17.7 us -> 16.9 us
  starting transfers between devices: 17.7 us -> 18.4 us
    ppermute x9 -> x12, waiting for transfers between devices: 15.9 us -> 10.9 us  [flip(): return lax.ppermute(values, axis, [(i, i ^ bit) for i in range(count)])]
    ppermute x9 -> x12, starting transfers between devices: 11 us -> 12.5 us  [flip(): return lax.ppermute(values, axis, [(i, i ^ bit) for i in range(count)])]
    ppermute x4, waiting for transfers between devices: 3.77 us -> 4.61 us  [the longest x2 3.06 us: swap_rows(): return lax.ppermute(values, ('rows', 'cols'), pairs)]
    pallas_call x10 -> x12, Pallas kernels: 17.7 us -> 16.9 us  [call(): pl.pallas_call(kernel, out_shape=[jax.ShapeDtypeStruct(shape, kind) for s...]
    ppermute x4, starting transfers between devices: 6.7 us -> 5.87 us  [the longest x2 3.09 us: swap_rows(): return lax.ppermute(values, ('rows', 'cols'), pairs)]
  transfers between devices with their start and end apart: 13 -> 16, of which waited for: 8 -> 10; matrix products, arithmetic and copies ran while one was open for 0% -> 0% of each run, Pallas kernels for 6% -> 8%
where the time goes in v2:
time: 52.9 us; the launch traced here: 52.7 us
  starting transfers between devices  18.4 us (35%)
  Pallas kernels  16.9 us (32%)
  waiting for transfers between devices  15.5 us (29%)
  local copies, waits for them, and re-layouts  1.11 us (2%)
  between operations  0.81 us (2%)
    pallas_call x12, Pallas kernels, call(): pl.pallas_call(kernel, out_shape=[jax.ShapeDtypeStruct(shape, kind) for s...  16.9 us
    ppermute x12, starting transfers between devices, flip(): return lax.ppermute(values, axis, [(i, i ^ bit) for i in range(count)])  12.5 us
    ppermute x12, waiting for transfers between devices, flip(): return lax.ppermute(values, axis, [(i, i ^ bit) for i in range(count)])  10.9 us
    ppermute x2, starting transfers between devices, swap_rows(): return lax.ppermute(values, ('rows', 'cols'), pairs)  3.09 us
    ppermute x2, waiting for transfers between devices, swap_rows(): return lax.ppermute(values, ('rows', 'cols'), pairs)  3.06 us
    ppermute x2, starting transfers between devices, swap_cols(): return lax.ppermute(values, 'cols', pairs)  2.78 us
    ppermute x2, waiting for transfers between devices, swap_cols(): return lax.ppermute(values, 'cols', pairs)  1.56 us
    unnamed x24, local copies, waits for them, and re-layouts  1.11 us
  transfers between devices with their start and end apart: 16, of which 10 were waited for; matrix products, arithmetic and copies ran while one was open for 0% of the time, Pallas kernels for 8%

profile of v2, /device:TPU:0, one launch (start us, length us, event | category | flops | bytes accessed | tf_op | source)
XLA Modules:
  0.0 52.7 jit_solution(11771984616958755268)
XLA Ops:
  0.6 0.7 %copy-done.8 = f32[2,225,6]{1,0,2:T(2,128)S(1)} copy-done((f32[2,225,6]{1,0,2:T(2,128)S(1)}, f32[2,225,6]{1,0,2:T(2,128)}, u32[]{:S(2)}) %copy-start.8) | copy-done | bytes 10824
  1.4 1.1 %shard_map.163 = (f32[64,384]{1,0:T(8,128)S(1)}, f32[64,384]{1,0:T(8,128)S(1)}) custom-call(f32[6,2,225]{2,1,0:T(2,128)S(1)} %bitcast.8), custom_call_target="tpu_custom_call" | custom-call | flops 6000000000 | bytes 1024 | tf_op jit(solution)/shard_map/pallas_call | solution.py:889
  2.9 1.9 %shard_map.164 = (bf16[8,32,192]{2,1,0:T(8,128)(2,1)S(1)}, bf16[144,384]{1,0:T(8,128)(2,1)S(1)}, bf16[144,384]{1,0:T(8,128)(2,1)S(1)}, bf16[256,192]{1,0:T(8,128...) custom-call(bf16[8,32,192]{2,1,0:T(8,128)(2,1)S(1)} %copy-done.5, ...), custom_call_target="tpu_custom_call" | custom-call | flops 3000000000 | bytes 1024 | tf_op jit(solution)/shard_map/pallas_call | solution.py:889
  4.8 3.1 %collective-permute-start = (bf16[144,384]{1,0:T(8,128)(2,1)S(1)}, bf16[144,384]{1,0:T(8,128)(2,1)S(1)}, u32[]{:S(2)}, u32[]{:S(2)}) collective-permute-start(bf16[144,384]{1,0:T(8,128)(2,1)S(1)} %get-tuple-element.57), channel_id=1, source_target_pairs={{0,8},{1,9},{2,10},{3,11},{4,12},{5,13},{6,14},{7,15},{8,0},{9,1},... | collective-permute-start | bytes 331784 | tf_op jit(solution)/shard_map/ppermute | solution.py:925
  7.9 3.1 %collective-permute-done.from_near = bf16[144,384]{1,0:T(8,128)(2,1)S(1)} collective-permute-done((bf16[144,384]{1,0:T(8,128)(2,1)S(1)}, bf16[144,384]{1,0:T(8,128)(2,1)S(1)}, u32[]{:S(2)}, u32[]{:S(2)}) %collective-permute-start) | collective-permute-done | bytes 110624 | tf_op jit(solution)/shard_map/ppermute | solution.py:925
  10.9 0.2 shard_map.165
  11.2 2.7 %collective-permute-start.3 = (bf16[80,384]{1,0:T(8,128)(2,1)S(1)}, bf16[80,384]{1,0:T(8,128)(2,1)S(1)}, u32[]{:S(2)}, u32[]{:S(2)}) collective-permute-start(bf16[80,384]{1,0:T(8,128)(2,1)S(1)} %get-tuple-element.62), channel_id=1, source_target_pairs={{1,2},{2,1},{3,4},{4,3},{5,6},{6,5},{7,0},{0,7},{9,10},{10,9},{11,... | collective-permute-start | bytes 184328 | tf_op jit(solution)/shard_map/ppermute | solution.py:911
  13.9 0.3 shard_map.166
  14.3 1.6 %collective-permute-done.3.far = bf16[80,384]{1,0:T(8,128)(2,1)S(1)} collective-permute-done((bf16[80,384]{1,0:T(8,128)(2,1)S(1)}, bf16[80,384]{1,0:T(8,128)(2,1)S(1)}, u32[]{:S(2)}, u32[]{:S(2)}) %collective-permute-start.3) | collective-permute-done | bytes 61472 | tf_op jit(solution)/shard_map/ppermute | solution.py:911
  15.8 8.1 %shard_map.167 = (bf16[256,192]{1,0:T(8,128)(2,1)S(1)}, bf16[592,384]{1,0:T(8,128)(2,1)S(1)}, bf16[592,384]{1,0:T(8,128)(2,1)S(1)}) custom-call(bf16[8,32,192]{2,1,0:T(8,128)(2,1)S(1)} %get-tuple-element.56.first_out, bf16[8,32,192]{2,1,0:T(8,128)(2,1)S(1)} %copy-done.4, bf16[128,384]{1,0:T(8,128)(2,1)S(1)} %get-tuple-element.59.up, ...), custom_call_target="tpu_custom_call" | custom-call | flops 12000000000 | bytes 1024 | tf_op jit(solution)/shard_map/pallas_call | solution.py:889
  24.1 0.7 %shard_map.168 = (bf16[256,192]{1,0:T(8,128)(2,1)S(1)}, bf16[384,384]{1,0:T(8,128)(2,1)S(1)}, bf16[384,384]{1,0:T(8,128)(2,1)S(1)}) custom-call(bf16[256,192]{1,0:T(8,128)(2,1)S(1)} %get-tuple-element.68.grad_ref, bf16[256,192]{1,0:T(8,128)(2,1)S(1)} %get-tuple-element.69.middle_ref, bf16[256,768]{1,0:T(8,128)(2,1)S(1)} %get-tuple-element.70.act, ...), custom_call_target="tpu_custom_call" | custom-call | flops 1000000000 | bytes 1024 | tf_op jit(solution)/shard_map/pallas_call | solution.py:889
  24.8 0.5 %collective-permute-start.4 = (bf16[384,384]{1,0:T(8,128)(2,1)S(1)}, bf16[384,384]{1,0:T(8,128)(2,1)S(1)}, u32[]{:S(2)}, u32[]{:S(2)}) collective-permute-start(bf16[384,384]{1,0:T(8,128)(2,1)S(1)} %get-tuple-element.78), channel_id=1, source_target_pairs={{0,1},{1,0},{2,3},{3,2},{4,5},{5,4},{6,7},{7,6},{8,9},{9,8},{10,11... | collective-permute-start | bytes 884744 | tf_op jit(solution)/shard_map/ppermute | solution.py:902
  25.3 1.2 %collective-permute-done.4.refs_1_ = bf16[384,384]{1,0:T(8,128)(2,1)S(1)} collective-permute-done((bf16[384,384]{1,0:T(8,128)(2,1)S(1)}, bf16[384,384]{1,0:T(8,128)(2,1)S(1)}, u32[]{:S(2)}, u32[]{:S(2)}) %collective-permute-start.4) | collective-permute-done | bytes 294944 | tf_op jit(solution)/shard_map/ppermute | solution.py:902
  26.5 0.3 shard_map.169
  26.9 3.0 %collective-permute-start.10 = (bf16[256,384]{1,0:T(8,128)(2,1)S(1)}, bf16[256,384]{1,0:T(8,128)(2,1)S(1)}, u32[]{:S(2)}, u32[]{:S(2)}) collective-permute-start(bf16[256,384]{1,0:T(8,128)(2,1)S(1)} %get-tuple-element.89), channel_id=1, source_target_pairs={{0,6},{1,7},{2,4},{3,5},{4,2},{5,3},{6,0},{7,1},{8,14},{9,15},{10,... | collective-permute-start | bytes 589832 | tf_op jit(solution)/shard_map/ppermute | solution.py:902
  29.8 0.6 %collective-permute-start.11 = (bf16[256,384]{1,0:T(8,128)(2,1)S(1)}, bf16[256,384]{1,0:T(8,128)(2,1)S(1)}, u32[]{:S(2)}, u32[]{:S(2)}) collective-permute-start(bf16[256,384]{1,0:T(8,128)(2,1)S(1)} %get-tuple-element.90), channel_id=1, source_target_pairs={{0,4},{1,5},{2,6},{3,7},{4,0},{5,1},{6,2},{7,3},{8,12},{9,13},{10,... | collective-permute-start | bytes 589832 | tf_op jit(solution)/shard_map/ppermute | solution.py:902
  30.5 2.5 %shard_map.170 = (bf16[8,32,192]{2,1,0:T(8,128)(2,1)}, bf16[208,384]{1,0:T(8,128)(2,1)S(1)}, bf16[208,384]{1,0:T(8,128)(2,1)S(1)}) custom-call(bf16[8,32,192]{2,1,0:T(8,128)(2,1)S(1)} %copy-done.5, bf16[256,192]{1,0:T(8,128)(2,1)S(1)} %get-tuple-element.72.grad_ref, bf16[256,192]{1,0:T(8,128)(2,1)S(1)} %get-tuple-element.73.query, ...), custom_call_target="tpu_custom_call" | custom-call | flops 4000000000 | bytes 1024 | tf_op jit(solution)/shard_map/pallas_call | solution.py:889
  33.0 1.4 %collective-permute-done.6.refs_1_ = bf16[208,384]{1,0:T(8,128)(2,1)S(1)} collective-permute-done((bf16[208,384]{1,0:T(8,128)(2,1)S(1)}, bf16[208,384]{1,0:T(8,128)(2,1)S(1)}, u32[]{:S(2)}, u32[]{:S(2)}) %collective-permute-start.6) | collective-permute-done | bytes 159776 | tf_op jit(solution)/shard_map/ppermute | solution.py:902
  34.4 2.9 %collective-permute-start.7 = (bf16[64,384]{1,0:T(8,128)(2,1)S(1)}, bf16[64,384]{1,0:T(8,128)(2,1)S(1)}, u32[]{:S(2)}, u32[]{:S(2)}) collective-permute-start(bf16[64,384]{1,0:T(8,128)(2,1)S(1)} %get-tuple-element.86), channel_id=1, source_target_pairs={{0,6},{1,7},{2,4},{3,5},{4,2},{5,3},{6,0},{7,1},{8,14},{9,15},{10,... | collective-permute-start | bytes 147464 | tf_op jit(solution)/shard_map/ppermute | solution.py:902
  37.3 0.6 %collective-permute-start.8 = (bf16[64,384]{1,0:T(8,128)(2,1)S(1)}, bf16[64,384]{1,0:T(8,128)(2,1)S(1)}, u32[]{:S(2)}, u32[]{:S(2)}) collective-permute-start(bf16[64,384]{1,0:T(8,128)(2,1)S(1)} %get-tuple-element.87), channel_id=1, source_target_pairs={{0,4},{1,5},{2,6},{3,7},{4,0},{5,1},{6,2},{7,3},{8,12},{9,13},{10,... | collective-permute-start | bytes 147464 | tf_op jit(solution)/shard_map/ppermute | solution.py:902
  38.0 1.8 %collective-permute-done.11.refs_2_ = bf16[256,384]{1,0:T(8,128)(2,1)S(1)} collective-permute-done((bf16[256,384]{1,0:T(8,128)(2,1)S(1)}, bf16[256,384]{1,0:T(8,128)(2,1)S(1)}, u32[]{:S(2)}, u32[]{:S(2)}) %collective-permute-start.11) | collective-permute-done | bytes 196640 | tf_op jit(solution)/shard_map/ppermute | solution.py:902
  39.7 0.5 collective-permute-done.12.refs_3_
  40.2 0.5 shard_map.172
  40.7 0.7 %collective-permute-done.8.refs_2_ = bf16[64,384]{1,0:T(8,128)(2,1)S(1)} collective-permute-done((bf16[64,384]{1,0:T(8,128)(2,1)S(1)}, bf16[64,384]{1,0:T(8,128)(2,1)S(1)}, u32[]{:S(2)}, u32[]{:S(2)}) %collective-permute-start.8) | collective-permute-done | bytes 49184 | tf_op jit(solution)/shard_map/ppermute | solution.py:902
  41.4 0.6 %collective-permute-done.9.refs_3_ = bf16[64,384]{1,0:T(8,128)(2,1)S(1)} collective-permute-done((bf16[64,384]{1,0:T(8,128)(2,1)S(1)}, bf16[64,384]{1,0:T(8,128)(2,1)S(1)}, u32[]{:S(2)}, u32[]{:S(2)}) %collective-permute-start.9) | collective-permute-done | bytes 49184 | tf_op jit(solution)/shard_map/ppermute | solution.py:902
  42.0 0.3 shard_map.173
  42.3 3.7 %collective-permute-start.13 = (bf16[248,128]{1,0:T(8,128)(2,1)S(1)}, bf16[248,128]{1,0:T(8,128)(2,1)S(1)}, u32[]{:S(2)}, u32[]{:S(2)}) collective-permute-start(bf16[248,128]{1,0:T(8,128)(2,1)S(1)} %get-tuple-element.96), channel_id=1, source_target_pairs={{0,24},{8,16},{16,8},{24,0},{1,25},{9,17},{17,9},{25,1},{2,26},{10... | collective-permute-start | bytes 190472 | tf_op jit(solution)/shard_map/ppermute | solution.py:902
  46.0 0.6 %collective-permute-start.14 = (bf16[248,128]{1,0:T(8,128)(2,1)S(1)}, bf16[248,128]{1,0:T(8,128)(2,1)S(1)}, u32[]{:S(2)}, u32[]{:S(2)}) collective-permute-start(bf16[248,128]{1,0:T(8,128)(2,1)S(1)} %get-tuple-element.97), channel_id=1, source_target_pairs={{0,16},{8,24},{16,0},{24,8},{1,17},{9,25},{17,1},{25,9},{2,18},{10... | collective-permute-start | bytes 190472 | tf_op jit(solution)/shard_map/ppermute | solution.py:902
  46.6 0.5 collective-permute-start.15
  47.1 1.4 %collective-permute-done.13.refs_1_ = bf16[248,128]{1,0:T(8,128)(2,1)S(1)} collective-permute-done((bf16[248,128]{1,0:T(8,128)(2,1)S(1)}, bf16[248,128]{1,0:T(8,128)(2,1)S(1)}, u32[]{:S(2)}, u32[]{:S(2)}) %collective-permute-start.13) | collective-permute-done | bytes 63520 | tf_op jit(solution)/shard_map/ppermute | solution.py:902
  48.5 3.4 %collective-permute-done.14.refs_2_ = bf16[248,128]{1,0:T(8,128)(2,1)S(1)} collective-permute-done((bf16[248,128]{1,0:T(8,128)(2,1)S(1)}, bf16[248,128]{1,0:T(8,128)(2,1)S(1)}, u32[]{:S(2)}, u32[]{:S(2)}) %collective-permute-start.14) | collective-permute-done | bytes 63520 | tf_op jit(solution)/shard_map/ppermute | solution.py:902
  51.8 0.9 %shard_map.174 = (f32[2,48,72]{2,1,0:T(8,128)}, f32[2,24,48]{2,1,0:T(8,128)}, f32[2,48,96]{2,1,0:T(8,128)}, f32[2,24,192]{2,1,0:T(8,128)}, f32[6,2,225]{2,1,0:T(2,128)}) custom-call(bf16[248,128]{1,0:T(8,128)(2,1)S(1)} %get-tuple-element.95.refs_0_, bf16[248,128]{1,0:T(8,128)(2,1)S(1)} %collective-permute-done.13.refs_1_, ...), custom_call_target="tpu_custom_call" | custom-call | flops 200000000 | bytes 1024 | tf_op jit(solution)/shard_map/pallas_call | solution.py:889
  (36 shorter events, 0.7 us)
Async XLA Ops:
  0.6 0.7 %copy-start.8 = (f32[2,225,6]{1,0,2:T(2,128)S(1)}, f32[2,225,6]{1,0,2:T(2,128)}, u32[]{:S(2)}) copy-start(f32[2,225,6]{1,0,2:T(2,128)} %param.23) | copy-start | bytes 32404
  1.3 1.1 %copy-start = (bf16[2,192,768]{2,1,0:T(8,128)(2,1)S(1)}, bf16[2,192,768]{2,1,0:T(8,128)(2,1)}, u32[]{:S(2)}) copy-start(bf16[2,192,768]{2,1,0:T(8,128)(2,1)} %inner_w.5) | copy-start | bytes 1769476
  1.3 1.2 %copy-start.1 = (bf16[2,768,192]{1,2,0:T(8,128)(2,1)S(1)}, bf16[2,768,192]{1,2,0:T(8,128)(2,1)}, u32[]{:S(2)}) copy-start(bf16[2,768,192]{1,2,0:T(8,128)(2,1)} %param.22) | copy-start | bytes 1769476
  1.3 1.4 %copy-start.2 = (bf16[2,192,576]{2,1,0:T(8,128)(2,1)S(1)}, bf16[2,192,576]{2,1,0:T(8,128)(2,1)}, u32[]{:S(2)}) copy-start(bf16[2,192,576]{2,1,0:T(8,128)(2,1)} %qkv_w.5) | copy-start | bytes 1327108
  1.3 1.4 %copy-start.3 = (bf16[2,192,192]{2,1,0:T(8,128)(2,1)S(1)}, bf16[2,192,192]{2,1,0:T(8,128)(2,1)}, u32[]{:S(2)}) copy-start(bf16[2,192,192]{2,1,0:T(8,128)(2,1)} %proj_w.5) | copy-start | bytes 442372
  1.4 1.5 %copy-start.4 = (bf16[8,32,192]{2,1,0:T(8,128)(2,1)S(1)}, bf16[8,32,192]{2,1,0:T(8,128)(2,1)}, u32[]{:S(2)}) copy-start(bf16[8,32,192]{2,1,0:T(8,128)(2,1)} %cotangent.5) | copy-start | bytes 294916
  1.4 1.5 %copy-start.5 = (bf16[8,32,192]{2,1,0:T(8,128)(2,1)S(1)}, bf16[8,32,192]{2,1,0:T(8,128)(2,1)}, u32[]{:S(2)}) copy-start(bf16[8,32,192]{2,1,0:T(8,128)(2,1)} %tokens.3) | copy-start | bytes 294916
  1.4 1.5 %copy-start.9 = (s32[8,32]{1,0:T(8,128)S(1)}, s32[8,32]{1,0:T(8,128)}, u32[]{:S(2)}) copy-start(s32[8,32]{1,0:T(8,128)} %ids.3) | copy-start | bytes 3076
  2.9 8.1 %copy-start.6 = (bf16[4,32,192]{2,1,0:T(8,128)(2,1)S(1)}, bf16[4,32,192]{2,1,0:T(8,128)(2,1)}, u32[]{:S(2)}) copy-start(bf16[4,32,192]{2,1,0:T(8,128)(2,1)} %upper_rim.1) | copy-start | bytes 147460
  2.9 8.1 %copy-start.7 = (bf16[4,32,192]{2,1,0:T(8,128)(2,1)S(1)}, bf16[4,32,192]{2,1,0:T(8,128)(2,1)}, u32[]{:S(2)}) copy-start(bf16[4,32,192]{2,1,0:T(8,128)(2,1)} %lower_rim.1) | copy-start | bytes 147460
  4.7 6.2 %copy-start.11 = (s32[4,32]{1,0:T(4,128)S(1)}, s32[4,32]{1,0:T(4,128)}, u32[]{:S(2)}) copy-start(s32[4,32]{1,0:T(4,128)} %lower_ids.1) | copy-start | bytes 1540
  4.8 6.2 %copy-start.10 = (s32[4,32]{1,0:T(4,128)S(1)}, s32[4,32]{1,0:T(4,128)}, u32[]{:S(2)}) copy-start(s32[4,32]{1,0:T(4,128)} %upper_ids.1) | copy-start | bytes 1540
  4.8 6.1 %collective-permute-start = (bf16[144,384]{1,0:T(8,128)(2,1)S(1)}, bf16[144,384]{1,0:T(8,128)(2,1)S(1)}, u32[]{:S(2)}, u32[]{:S(2)}) collective-permute-start(bf16[144,384]{1,0:T(8,128)(2,1)S(1)} %get-tuple-element.57), channel_id=1, source_target_pairs={{0,8},{1,9},{2,10},{3,11},{4,12},{5,13},{6,14},{7,15},{8,0},{9,1},... | collective-permute-start | bytes 331784 | tf_op jit(solution)/shard_map/ppermute | solution.py:925
  7.9 3.1 %collective-permute-start.1 = (bf16[144,384]{1,0:T(8,128)(2,1)S(1)}, bf16[144,384]{1,0:T(8,128)(2,1)S(1)}, u32[]{:S(2)}, u32[]{:S(2)}) collective-permute-start(bf16[144,384]{1,0:T(8,128)(2,1)S(1)} %get-tuple-element.58), channel_id=1, source_target_pairs={{0,1},{1,0},{2,3},{3,2},{4,5},{5,4},{6,7},{7,6},{8,16},{9,17},{10,... | collective-permute-start | bytes 331784 | tf_op jit(solution)/shard_map/ppermute | solution.py:925
  11.1 3.1 %collective-permute-start.2 = (bf16[80,384]{1,0:T(8,128)(2,1)S(1)}, bf16[80,384]{1,0:T(8,128)(2,1)S(1)}, u32[]{:S(2)}, u32[]{:S(2)}) collective-permute-start(bf16[80,384]{1,0:T(8,128)(2,1)S(1)} %get-tuple-element.61), channel_id=1, source_target_pairs={{0,1},{1,0},{2,3},{3,2},{4,5},{5,4},{6,7},{7,6},{8,9},{9,8},{10,11... | collective-permute-start | bytes 184328 | tf_op jit(solution)/shard_map/ppermute | solution.py:911
  11.2 4.6 %collective-permute-start.3 = (bf16[80,384]{1,0:T(8,128)(2,1)S(1)}, bf16[80,384]{1,0:T(8,128)(2,1)S(1)}, u32[]{:S(2)}, u32[]{:S(2)}) collective-permute-start(bf16[80,384]{1,0:T(8,128)(2,1)S(1)} %get-tuple-element.62), channel_id=1, source_target_pairs={{1,2},{2,1},{3,4},{4,3},{5,6},{6,5},{7,0},{0,7},{9,10},{10,9},{11,... | collective-permute-start | bytes 184328 | tf_op jit(solution)/shard_map/ppermute | solution.py:911
  23.9 2.6 %collective-permute-start.5 = (bf16[592,384]{1,0:T(8,128)(2,1)S(1)}, bf16[592,384]{1,0:T(8,128)(2,1)S(1)}, u32[]{:S(2)}, u32[]{:S(2)}) collective-permute-start(bf16[592,384]{1,0:T(8,128)(2,1)S(1)} %get-tuple-element.80), channel_id=1, source_target_pairs={{0,1},{1,0},{2,3},{3,2},{4,5},{5,4},{6,7},{7,6},{8,9},{9,8},{10,11... | collective-permute-start | bytes 1363976 | tf_op jit(solution)/shard_map/ppermute | solution.py:902
  24.8 1.7 %collective-permute-start.4 = (bf16[384,384]{1,0:T(8,128)(2,1)S(1)}, bf16[384,384]{1,0:T(8,128)(2,1)S(1)}, u32[]{:S(2)}, u32[]{:S(2)}) collective-permute-start(bf16[384,384]{1,0:T(8,128)(2,1)S(1)} %get-tuple-element.78), channel_id=1, source_target_pairs={{0,1},{1,0},{2,3},{3,2},{4,5},{5,4},{6,7},{7,6},{8,9},{9,8},{10,11... | collective-permute-start | bytes 884744 | tf_op jit(solution)/shard_map/ppermute | solution.py:902
  26.9 11.1 %collective-permute-start.10 = (bf16[256,384]{1,0:T(8,128)(2,1)S(1)}, bf16[256,384]{1,0:T(8,128)(2,1)S(1)}, u32[]{:S(2)}, u32[]{:S(2)}) collective-permute-start(bf16[256,384]{1,0:T(8,128)(2,1)S(1)} %get-tuple-element.89), channel_id=1, source_target_pairs={{0,6},{1,7},{2,4},{3,5},{4,2},{5,3},{6,0},{7,1},{8,14},{9,15},{10,... | collective-permute-start | bytes 589832 | tf_op jit(solution)/shard_map/ppermute | solution.py:902
  29.8 9.9 %collective-permute-start.11 = (bf16[256,384]{1,0:T(8,128)(2,1)S(1)}, bf16[256,384]{1,0:T(8,128)(2,1)S(1)}, u32[]{:S(2)}, u32[]{:S(2)}) collective-permute-start(bf16[256,384]{1,0:T(8,128)(2,1)S(1)} %get-tuple-element.90), channel_id=1, source_target_pairs={{0,4},{1,5},{2,6},{3,7},{4,0},{5,1},{6,2},{7,3},{8,12},{9,13},{10,... | collective-permute-start | bytes 589832 | tf_op jit(solution)/shard_map/ppermute | solution.py:902
  30.5 9.7 %collective-permute-start.12 = (bf16[256,384]{1,0:T(8,128)(2,1)S(1)}, bf16[256,384]{1,0:T(8,128)(2,1)S(1)}, u32[]{:S(2)}, u32[]{:S(2)}) collective-permute-start(bf16[256,384]{1,0:T(8,128)(2,1)S(1)} %get-tuple-element.91), channel_id=1, source_target_pairs={{0,2},{1,3},{2,0},{3,1},{4,6},{5,7},{6,4},{7,5},{8,10},{9,11},{10,... | collective-permute-start | bytes 589832 | tf_op jit(solution)/shard_map/ppermute | solution.py:902
  33.0 1.4 %collective-permute-start.6 = (bf16[208,384]{1,0:T(8,128)(2,1)S(1)}, bf16[208,384]{1,0:T(8,128)(2,1)S(1)}, u32[]{:S(2)}, u32[]{:S(2)}) collective-permute-start(bf16[208,384]{1,0:T(8,128)(2,1)S(1)} %get-tuple-element.84), channel_id=1, source_target_pairs={{0,1},{1,0},{2,3},{3,2},{4,5},{5,4},{6,7},{7,6},{8,9},{9,8},{10,11... | collective-permute-start | bytes 479240 | tf_op jit(solution)/shard_map/ppermute | solution.py:902
  34.4 6.3 %collective-permute-start.7 = (bf16[64,384]{1,0:T(8,128)(2,1)S(1)}, bf16[64,384]{1,0:T(8,128)(2,1)S(1)}, u32[]{:S(2)}, u32[]{:S(2)}) collective-permute-start(bf16[64,384]{1,0:T(8,128)(2,1)S(1)} %get-tuple-element.86), channel_id=1, source_target_pairs={{0,6},{1,7},{2,4},{3,5},{4,2},{5,3},{6,0},{7,1},{8,14},{9,15},{10,... | collective-permute-start | bytes 147464 | tf_op jit(solution)/shard_map/ppermute | solution.py:902
  37.3 4.1 %collective-permute-start.8 = (bf16[64,384]{1,0:T(8,128)(2,1)S(1)}, bf16[64,384]{1,0:T(8,128)(2,1)S(1)}, u32[]{:S(2)}, u32[]{:S(2)}) collective-permute-start(bf16[64,384]{1,0:T(8,128)(2,1)S(1)} %get-tuple-element.87), channel_id=1, source_target_pairs={{0,4},{1,5},{2,6},{3,7},{4,0},{5,1},{6,2},{7,3},{8,12},{9,13},{10,... | collective-permute-start | bytes 147464 | tf_op jit(solution)/shard_map/ppermute | solution.py:902
  37.9 4.1 %collective-permute-start.9 = (bf16[64,384]{1,0:T(8,128)(2,1)S(1)}, bf16[64,384]{1,0:T(8,128)(2,1)S(1)}, u32[]{:S(2)}, u32[]{:S(2)}) collective-permute-start(bf16[64,384]{1,0:T(8,128)(2,1)S(1)} %get-tuple-element.88), channel_id=1, source_target_pairs={{0,2},{1,3},{2,0},{3,1},{4,6},{5,7},{6,4},{7,5},{8,10},{9,11},{10,... | collective-permute-start | bytes 147464 | tf_op jit(solution)/shard_map/ppermute | solution.py:902
  42.3 6.1 %collective-permute-start.13 = (bf16[248,128]{1,0:T(8,128)(2,1)S(1)}, bf16[248,128]{1,0:T(8,128)(2,1)S(1)}, u32[]{:S(2)}, u32[]{:S(2)}) collective-permute-start(bf16[248,128]{1,0:T(8,128)(2,1)S(1)} %get-tuple-element.96), channel_id=1, source_target_pairs={{0,24},{8,16},{16,8},{24,0},{1,25},{9,17},{17,9},{25,1},{2,26},{10... | collective-permute-start | bytes 190472 | tf_op jit(solution)/shard_map/ppermute | solution.py:902
  46.0 5.8 %collective-permute-start.14 = (bf16[248,128]{1,0:T(8,128)(2,1)S(1)}, bf16[248,128]{1,0:T(8,128)(2,1)S(1)}, u32[]{:S(2)}, u32[]{:S(2)}) collective-permute-start(bf16[248,128]{1,0:T(8,128)(2,1)S(1)} %get-tuple-element.97), channel_id=1, source_target_pairs={{0,16},{8,24},{16,0},{24,8},{1,17},{9,25},{17,1},{25,9},{2,18},{10... | collective-permute-start | bytes 190472 | tf_op jit(solution)/shard_map/ppermute | solution.py:902
  46.6 5.3 %collective-permute-start.15 = (bf16[248,128]{1,0:T(8,128)(2,1)S(1)}, bf16[248,128]{1,0:T(8,128)(2,1)S(1)}, u32[]{:S(2)}, u32[]{:S(2)}) collective-permute-start(bf16[248,128]{1,0:T(8,128)(2,1)S(1)} %get-tuple-element.98), channel_id=1, source_target_pairs={{0,8},{8,0},{16,24},{24,16},{1,9},{9,1},{17,25},{25,17},{2,10},{10... | collective-permute-start | bytes 190472 | tf_op jit(solution)/shard_map/ppermute | solution.py:902

commit v3 on v2

--- a/solution.py
+++ b/solution.py
@@ -119,11 +119,15 @@
 
 
 def pair_up(stacks, sides, size):
-    channels = sides.shape[0]
+    wide = stacks[0].shape[1]
     return jnp.concatenate(
         [
-            paired([stack[:, first:last] for stack in stacks], sides[start : start + width], size)
-            for start, width, first, last in lane_tiles(channels, size)
+            paired(
+                [stack[:, at : at + LANES] for stack in stacks],
+                sides[at // TOK * size : (at + LANES) // TOK * size],
+                size,
+            )
+            for at in range(0, wide, LANES)
         ],
         axis=0,
     )
@@ -428,9 +432,8 @@
     ]
 
 
-def bias_kernel(table, first, second):
+def bias_kernel(table, first):
     first[...] = expand_bias(table[:, 0])
-    second[...] = expand_bias(table[:, 1])
 
 
 def first_kernel(
@@ -561,7 +564,9 @@
         ref[...] = edge[...].astype(BF16)
 
 
-def side_kernel(pre, key, slope, key_t):
+def side_kernel(pre, key, table, slope, key_t, bias, onehot):
+    onehot[...] = offset_rows(onehot.shape[0])
+    bias[...] = expand_bias(table[:, 1])
     key_t[...] = key[...].T
     for at in range(0, pre.shape[0], TOK):
         x = pre[at : at + TOK]
@@ -587,8 +592,8 @@
     cotangent,
     up,
     down,
+    far,
     near,
-    far,
     ext_ids,
     bias_ref,
     qkv_w,
@@ -597,6 +602,7 @@
     outer_w,
     after,
     grad_out,
+    table_out,
     keep,
     send,
     xs,
@@ -700,11 +706,11 @@
         narrow_units(
             [jnp.concatenate(qkv, axis=0), nn(mix_t, grad_middle * own).T], count
         ),
-        narrow_units([tn(grad_pre, normed_two * own)], count),
+        narrow_units([tn(normed_two * own, grad_pre).T], count),
         wide_units(tn(grad * own, act), 2 * channels, count),
     )
-    tails = [table_tail([fold_bias(bias_sum)], 2 * channels)]
-    write_parts(sort_by(blocks, lax.axis_index("cols") & 1, 2), tails, (keep, send))
+    table_out[...] = fold_bias(bias_sum)
+    write_parts(sort_by(blocks, lax.axis_index("cols") & 1, 2), [], (keep, send))
 
 
 def third_kernel(
@@ -731,45 +737,55 @@
 
 
 def fourth_kernel(
+    grad_ref, query, key_t, value, probs_ref, proj_w, query_out, key_out, value_out, bias_out
+):
+    count, channels = grad_ref.shape
+    width = probs_ref.shape[2]
+    grad_mix = nt(grad_ref[...], proj_w[0]).astype(BF16)
+    grad_mixes = [grad_mix[at : at + TOK] for at in range(0, count, TOK)]
+    query_out[...], key_out[...], value_out[...], bias_out[...] = attend_all_back(
+        query,
+        key_t,
+        value,
+        probs_ref,
+        grad_mixes,
+        channels // (width // TOK),
+        lambda w, term: term,
+    )
+
+
+def fifth_kernel(
     tokens,
     grad_ref,
-    query,
-    key_t,
-    value,
-    probs_ref,
     mix_t,
+    grad_query,
+    grad_key,
+    grad_value,
+    bias_sum,
+    table_two,
     qkv_w,
-    proj_w,
     after,
     token_grad,
     keep,
     send,
 ):
     rows, cols, channels = tokens.shape
-    width = probs_ref.shape[2]
-    size = channels // (width // TOK)
-    count = rows * cols
-    unit_one, inverse_one = norm(to_windows(tokens[...].astype(F32)))
-    normed_one = unit_one.astype(BF16)
+    unit, inverse = norm(to_windows(tokens[...].astype(F32)))
+    normed = unit.astype(BF16)
     grad_middle = grad_ref[...]
-    grad_mix = nt(grad_middle, proj_w[0]).astype(BF16)
-    grad_mixes = [grad_mix[at : at + TOK] for at in range(0, count, TOK)]
-    grad_query, grad_key, grad_value, bias_sum = attend_all_back(
-        query, key_t, value, probs_ref, grad_mixes, size, lambda w, term: term
-    )
-    weights = [qkv_w[0, :, i * channels : (i + 1) * channels] for i in range(3)]
-    grad_norm = (
-        nt(grad_query.T, weights[0]) + nt(grad_key, weights[1]) + nt(grad_value, weights[2])
-    )
-    grad_surface = grad_middle.astype(F32) + norm_back(unit_one, inverse_one, grad_norm)
-    token_grad[...] = from_windows(grad_surface, rows, cols).astype(BF16)
+    grads = [grad_query[...].T, grad_key[...], grad_value[...]]
     number = lax.axis_size("cols")
-    qkv = [nn(grad_query, normed_one), tn(grad_key, normed_one), tn(grad_value, normed_one)]
+    qkv = [nn(grad_query[...], normed), tn(grads[1], normed), tn(grads[2], normed)]
     blocks = narrow_units(
         [jnp.concatenate(qkv, axis=0), nn(mix_t[...], grad_middle).T], number
     )
-    tails = [table_tail([fold_wide(bias_sum)], 2 * channels)]
+    tails = [table_tail([fold_wide(bias_sum[...]), table_two[...]], 2 * channels)]
     write_parts(sort_by(blocks, lax.axis_index("cols") & 1, 2), tails, (keep, send))
+    grad_norm = sum(
+        nt(grad, qkv_w[0, :, i * channels : (i + 1) * channels]) for i, grad in enumerate(grads)
+    )
+    grad_surface = grad_middle.astype(F32) + norm_back(unit, inverse, grad_norm)
+    token_grad[...] = from_windows(grad_surface, rows, cols).astype(BF16)
 
 
 def summed(refs):
@@ -788,18 +804,18 @@
     return [parts[i] for i in ARRIVAL] if len(parts) == 4 else parts
 
 
-def join_kernel(count, bit, ways, tails, *refs):
+def join_kernel(count, bit, ways, tail, *refs):
+    sources = refs[: len(refs) - ways]
     blocks = []
-    table = None
-    for n, tail in enumerate(tails):
-        part = summed(refs[2 * n : 2 * n + 2])
+    rest = []
+    for n in range(0, len(sources), 2):
+        part = summed(sources[n : n + 2])
         edge = part.shape[0] - tail
         blocks.append(cut(part[:edge], count))
-        table = rows_table(part[edge:]) if tail else table
+        rest += [part[edge:]] if tail else []
     place = (lax.axis_index("cols") >> bit) & (ways - 1)
-    tail = [table_tail([table], part.shape[1])]
     parts = ordered(sort_by(joined(*blocks), place, ways))
-    write_parts(parts, tail, refs[len(refs) - ways :])
+    write_parts(parts, rest, refs[len(refs) - ways :])
 
 
 def step_kernel(axis, count, bit, before, ways, tail, *refs):
@@ -807,7 +823,7 @@
     edge = both.shape[0] - tail
     place = (lax.axis_index(axis) >> bit) & (ways - 1)
     parts = sort_by(cut(both[:edge], count), place, ways)
-    write_parts(ordered(parts), [both[edge:]], refs[before:])
+    write_parts(ordered(parts), [both[edge:]] if tail else [], refs[before:])
 
 
 def padded(block):
@@ -835,22 +851,20 @@
 
 def first_turn_kernel(channels, hidden, before, *refs):
     both = summed(refs[:before])
-    two, ffn, table = refs[before:]
+    two, ffn = refs[before:]
     count = lax.axis_size("rows")
-    edge = both.shape[0] - 2 * WIN
     used = 2 * channels // count
     pieces = [
         row_pieces(unit, n in (1, 4), channels, hidden, count)
-        for n, unit in enumerate(cut(both[:edge], 5))
+        for n, unit in enumerate(cut(both, 5))
     ]
     ffn[...] = padded(jnp.concatenate(joined(*pieces[:2]), axis=0))
     two[...] = jnp.concatenate([dense(b, used) for b in joined(*pieces[2:])], axis=0)
-    table[...] = rows_table(both[edge:])
 
 
 def merge_kernel(channels, hidden, before, ways, *refs):
     both = summed(refs[:before])
-    two, ffn, table = refs[before : before + 3]
+    two, ffn = refs[before : before + 2]
     count = lax.axis_size("rows")
     edge = both.shape[0] - 2 * WIN
     used = 2 * channels // count
@@ -859,17 +873,17 @@
     parts = sort_by(
         joined(one, cut(two[...], count)), lax.axis_index("rows") & (ways - 1), ways
     )
-    tails = [table_tail([rows_table(both[edge:]), table[...]], LANES)]
-    write_parts(ordered(parts), tails, refs[before + 3 :])
-
-
-def last_kernel(sizes, scale, before, *refs):
+    tables = [rows_table(both[edge + n * WIN : edge + (n + 1) * WIN]) for n in range(2)]
+    write_parts(ordered(parts), [table_tail(tables, LANES)], refs[before + 2 :])
+
+
+def last_kernel(sizes, scale, before, onehot_ref, *refs):
     (qkv_cols, inner_cols, proj_cols), thin, broad = sizes
     qkv, proj, inner, outer, table = refs[before:]
     total = summed(refs[:before]) * scale
     edge = total.shape[0] - 4 * WIN
     heads = table.shape[0]
-    onehot = offset_rows(table.shape[2])
+    onehot = onehot_ref[...]
     for b in range(2):
         both = undense(total[b * edge // 2 : (b + 1) * edge // 2], 2 * thin)
         low, mid, wide = cut(both, 3)
@@ -935,20 +949,18 @@
     return [min(size, bits - at) for at in range(0, bits, size)]
 
 
-def reduce_cols(pairs, tails, width, units, after=()):
+def reduce_cols(pairs, tail, width, units):
     got = []
     for keep, send in pairs:
         got += [keep, flip(send, "cols", 1)]
     count = lax.axis_size("cols") // 2
-    tail = 2 * WIN
     bit = 1
     kept = None
     for size in bit_groups(count.bit_length() - 1, 2):
         ways = 1 << size
         shape = ((count // ways * units + tail, width), BF16)
         if bit == 1:
-            kernel = functools.partial(join_kernel, count, bit, ways, tails)
-            got = got + list(after)
+            kernel = functools.partial(join_kernel, count, bit, ways, tail)
         else:
             kernel = functools.partial(step_kernel, "cols", count, bit, len(got), ways, tail)
         parts = call(kernel, [shape] * ways, [], *got)
@@ -1004,7 +1016,7 @@
     flat = ((count, channels), BF16)
     band = (HALF * cols + 2 * WIN, 2 * channels)
     pair = ((TOK, width), F32)
-    bias_one, bias_two = call(bias_kernel, [pair, pair], [], bias_table, cost=6.0)
+    (bias_one,) = call(bias_kernel, [pair], [], bias_table, cost=6.0)
     first_out, near, far, query, key, value, probs, mix, middle, pre, act = call(
         first_kernel,
         [
@@ -1033,8 +1045,14 @@
     )
     from_near = swap_rows(near, 0)
     from_far = swap_rows(far, 1)
-    slope, key_t = call(
-        side_kernel, [((count, hidden), F32), ((channels, count), BF16)], [], pre, key, cost=1.0
+    slope, key_t, bias_two, onehot = call(
+        side_kernel,
+        [((count, hidden), F32), ((channels, count), BF16), pair, ((length, 2 * LANES), BF16)],
+        [],
+        pre,
+        key,
+        bias_table,
+        cost=1.0,
     )
     strip = (total * HALF + total, 2 * channels)
     up, down, near, far, ext_ids = call(
@@ -1057,8 +1075,8 @@
         from_near,
         from_far,
     )
+    far = swap_cols(far, 1)
     near = swap_cols(near, 0)
-    far = swap_cols(far, 1)
     units = 4 * channels // col_count // 2
     slots = col_count // 2
 
@@ -1066,9 +1084,9 @@
         return ((slots * number * units + tail, 2 * channels), BF16)
 
     grid = (total, cols + 2 * HALF, channels)
-    grad_first, keep_two, send_two = call(
+    grad_first, table_two, keep_two, send_two = call(
         second_kernel,
-        [flat, packed(3, 2 * WIN), packed(3, 2 * WIN)],
+        [flat, ((WIN, 2 * LANES), F32), packed(3, 0), packed(3, 0)],
         [
             pltpu.VMEM(grid, F32),
             pltpu.VMEM(grid, F32),
@@ -1078,8 +1096,8 @@
         cotangent,
         up,
         down,
+        far,
         near,
-        far,
         ext_ids,
         bias_two,
         qkv_weight,
@@ -1102,7 +1120,7 @@
         cost=1.0,
     )
     got, kept = reduce_cols(
-        [(keep_ffn, send_ffn), (keep_two, send_two)], (0, 2 * WIN), 2 * channels, 5 * units
+        [(keep_ffn, send_ffn), (keep_two, send_two)], 0, 2 * channels, 5 * units
     )
     thin = channels // row_count
     piece = units * 3 // 4 * 3 if 8 * thin == 3 * LANES else units * 3
@@ -1111,29 +1129,40 @@
         [
             ((row_count * piece, LANES), F32),
             ((row_count * 2 * units, LANES), F32),
-            ((WIN, 2 * LANES), F32),
         ],
         [],
         *got,
         cost=TURN_COST,
     )
-    token_grad, keep_one, send_one = call(
+    grad_query, grad_key, grad_value, bias_sum = call(
         fourth_kernel,
-        [((rows, cols, channels), BF16), packed(1, 2 * WIN), packed(1, 2 * WIN)],
+        [((channels, count), BF16), flat, flat, pair],
         [],
-        tokens,
         grad_middle,
         query,
         key_t,
         value,
         probs,
+        proj_weight,
+        cost=2.0,
+    )
+    token_grad, keep_one, send_one = call(
+        fifth_kernel,
+        [((rows, cols, channels), BF16), packed(1, 2 * WIN), packed(1, 2 * WIN)],
+        [],
+        tokens,
+        grad_middle,
         mix,
+        grad_query,
+        grad_key,
+        grad_value,
+        bias_sum,
+        table_two,
         qkv_weight,
-        proj_weight,
         kept,
         cost=4.0,
     )
-    got, _ = reduce_cols([(keep_one, send_one)], (2 * WIN,), 2 * channels, units)
+    got, _ = reduce_cols([(keep_one, send_one)], 2 * WIN, 2 * channels, units)
     got = reduce_rows(got, others, channels, hidden, piece)
     broad = hidden // row_count
     sizes = (
@@ -1151,6 +1180,7 @@
             ((heads, 2, length), F32),
         ],
         [],
+        onehot,
         *got,
     )
     proj_grad = jnp.swapaxes(proj_grad, 1, 2)

time: 52.9 us -> 52.6 us (level)
  starting transfers between devices: 18.4 us -> 17.6 us
    ppermute x12, waiting for transfers between devices: 10.9 us -> 9.74 us  [flip(): return lax.ppermute(values, axis, [(i, i ^ bit) for i in range(count)])]
    ppermute x2, starting transfers between devices: 2.78 us -> 1.84 us  [swap_cols(): return lax.ppermute(values, 'cols', pairs)]
    ppermute x2, waiting for transfers between devices: 1.56 us -> 2.26 us  [swap_cols(): return lax.ppermute(values, 'cols', pairs)]
    unnamed x24 -> x26, local copies, waits for them, and re-layouts: 1.11 us -> 1.59 us
    pallas_call x12 -> x13, Pallas kernels: 16.9 us -> 17.3 us  [call(): pl.pallas_call(kernel, out_shape=[jax.ShapeDtypeStruct(shape, kind) for s...]
  transfers between devices with their start and end apart: 16 -> 16, of which waited for: 10 -> 8; matrix products, arithmetic and copies ran while one was open for 0% -> 0% of each run, Pallas kernels for 8% -> 10%
where the time goes in v3:
time: 52.6 us; the launch traced here: 52.3 us
  starting transfers between devices  17.6 us (33%)
  Pallas kernels  17.3 us (33%)
  waiting for transfers between devices  15.1 us (29%)
  local copies, waits for them, and re-layouts  1.59 us (3%)
  between operations  0.83 us (2%)
    pallas_call x13, Pallas kernels, call(): pl.pallas_call(kernel, out_shape=[jax.ShapeDtypeStruct(shape, kind) for s...  17.3 us
    ppermute x12, starting transfers between devices, flip(): return lax.ppermute(values, axis, [(i, i ^ bit) for i in range(count)])  12.6 us
    ppermute x12, waiting for transfers between devices, flip(): return lax.ppermute(values, axis, [(i, i ^ bit) for i in range(count)])  9.74 us
    ppermute x2, starting transfers between devices, swap_rows(): return lax.ppermute(values, ('rows', 'cols'), pairs)  3.09 us
    ppermute x2, waiting for transfers between devices, swap_rows(): return lax.ppermute(values, ('rows', 'cols'), pairs)  3.06 us
    ppermute x2, waiting for transfers between devices, swap_cols(): return lax.ppermute(values, 'cols', pairs)  2.26 us
    ppermute x2, starting transfers between devices, swap_cols(): return lax.ppermute(values, 'cols', pairs)  1.84 us
    unnamed x26, local copies, waits for them, and re-layouts  1.59 us
  transfers between devices with their start and end apart: 16, of which 8 were waited for; matrix products, arithmetic and copies ran while one was open for 0% of the time, Pallas kernels for 10%

profile of v3, /device:TPU:0, one launch (start us, length us, event | category | flops | bytes accessed | tf_op | source)
XLA Modules:
  0.0 52.3 jit_solution(3960333123498938764)
XLA Ops:
  0.6 0.7 %copy-done.8 = f32[2,225,6]{1,0,2:T(2,128)S(1)} copy-done((f32[2,225,6]{1,0,2:T(2,128)S(1)}, f32[2,225,6]{1,0,2:T(2,128)}, u32[]{:S(2)}) %copy-start.8) | copy-done | bytes 10824
  1.4 0.6 %shard_map.163.bias_ref = f32[64,384]{1,0:T(8,128)S(1)} custom-call(f32[6,2,225]{2,1,0:T(2,128)S(1)} %bitcast.8), custom_call_target="tpu_custom_call" | custom-call | flops 6000000000 | bytes 1024 | tf_op jit(solution)/shard_map/pallas_call | solution.py:903
  2.0 0.4 copy-done
  2.9 1.9 %shard_map.164 = (bf16[8,32,192]{2,1,0:T(8,128)(2,1)S(1)}, bf16[144,384]{1,0:T(8,128)(2,1)S(1)}, bf16[144,384]{1,0:T(8,128)(2,1)S(1)}, bf16[256,192]{1,0:T(8,128...) custom-call(bf16[8,32,192]{2,1,0:T(8,128)(2,1)S(1)} %copy-done.5, ...), custom_call_target="tpu_custom_call" | custom-call | flops 3000000000 | bytes 1024 | tf_op jit(solution)/shard_map/pallas_call | solution.py:903
  4.8 3.1 %collective-permute-start = (bf16[144,384]{1,0:T(8,128)(2,1)S(1)}, bf16[144,384]{1,0:T(8,128)(2,1)S(1)}, u32[]{:S(2)}, u32[]{:S(2)}) collective-permute-start(bf16[144,384]{1,0:T(8,128)(2,1)S(1)} %get-tuple-element.60), channel_id=1, source_target_pairs={{0,8},{1,9},{2,10},{3,11},{4,12},{5,13},{6,14},{7,15},{8,0},{9,1},... | collective-permute-start | bytes 331784 | tf_op jit(solution)/shard_map/ppermute | solution.py:939
  7.9 3.1 %collective-permute-done.from_near = bf16[144,384]{1,0:T(8,128)(2,1)S(1)} collective-permute-done((bf16[144,384]{1,0:T(8,128)(2,1)S(1)}, bf16[144,384]{1,0:T(8,128)(2,1)S(1)}, u32[]{:S(2)}, u32[]{:S(2)}) %collective-permute-start) | collective-permute-done | bytes 110624 | tf_op jit(solution)/shard_map/ppermute | solution.py:939
  11.2 1.2 %collective-permute-start.2 = (bf16[80,384]{1,0:T(8,128)(2,1)S(1)}, bf16[80,384]{1,0:T(8,128)(2,1)S(1)}, u32[]{:S(2)}, u32[]{:S(2)}) collective-permute-start(bf16[80,384]{1,0:T(8,128)(2,1)S(1)} %get-tuple-element.64), channel_id=1, source_target_pairs={{1,2},{2,1},{3,4},{4,3},{5,6},{6,5},{7,0},{0,7},{9,10},{10,9},{11,... | collective-permute-start | bytes 184328 | tf_op jit(solution)/shard_map/ppermute | solution.py:925
  12.4 0.6 %collective-permute-start.3 = (bf16[80,384]{1,0:T(8,128)(2,1)S(1)}, bf16[80,384]{1,0:T(8,128)(2,1)S(1)}, u32[]{:S(2)}, u32[]{:S(2)}) collective-permute-start(bf16[80,384]{1,0:T(8,128)(2,1)S(1)} %get-tuple-element.65), channel_id=1, source_target_pairs={{0,1},{1,0},{2,3},{3,2},{4,5},{5,4},{6,7},{7,6},{8,9},{9,8},{10,11... | collective-permute-start | bytes 184328 | tf_op jit(solution)/shard_map/ppermute | solution.py:925
  13.0 0.9 %shard_map.166 = (f32[256,768]{1,0:T(8,128)S(1)}, bf16[192,256]{1,0:T(8,128)(2,1)S(1)}, f32[64,384]{1,0:T(8,128)S(1)}, bf16[225,256]{1,0:T(8,128)(2,1)S(1)}) custom-call(f32[256,768]{1,0:T(8,128)S(1)} %get-tuple-element.67.pre, bf16[256,192]{1,0:T(8,128)(2,1)S(1)} %get-tuple-element.68.key, f32[6,2,225]{2,1,0:T(2,128)S(1)} %bitcast.9), custom_call_target="tpu_custom_call" | custom-call | flops 1000000000 | bytes 1024 | tf_op jit(solution)/shard_map/pallas_call | solution.py:903
  13.9 2.3 %collective-permute-done.2.far = bf16[80,384]{1,0:T(8,128)(2,1)S(1)} collective-permute-done((bf16[80,384]{1,0:T(8,128)(2,1)S(1)}, bf16[80,384]{1,0:T(8,128)(2,1)S(1)}, u32[]{:S(2)}, u32[]{:S(2)}) %collective-permute-start.2) | collective-permute-done | bytes 61472 | tf_op jit(solution)/shard_map/ppermute | solution.py:925
  16.2 7.8 %shard_map.167 = (bf16[256,192]{1,0:T(8,128)(2,1)S(1)}, f32[8,256]{1,0:T(8,128)S(1)}, bf16[576,384]{1,0:T(8,128)(2,1)S(1)}, bf16[576,384]{1,0:T(8,128)(2,1)S(1)}) custom-call(bf16[8,32,192]{2,1,0:T(8,128)(2,1)S(1)} %get-tuple-element.59.first_out, bf16[8,32,192]{2,1,0:T(8,128)(2,1)S(1)} %copy-done.4, bf16[128,384]{1,0:T(8,128)(2,1)S(1)} %get-tuple-element.62.up, ...), custom_call_target="tpu_custom_call" | custom-call | flops 12000000000 | bytes 1024 | tf_op jit(solution)/shard_map/pallas_call | solution.py:903
  24.1 0.7 %shard_map.168 = (bf16[256,192]{1,0:T(8,128)(2,1)S(1)}, bf16[384,384]{1,0:T(8,128)(2,1)S(1)}, bf16[384,384]{1,0:T(8,128)(2,1)S(1)}) custom-call(bf16[256,192]{1,0:T(8,128)(2,1)S(1)} %get-tuple-element.71.grad_ref, bf16[256,192]{1,0:T(8,128)(2,1)S(1)} %get-tuple-element.72.middle_ref, bf16[256,768]{1,0:T(8,128)(2,1)S(1)} %get-tuple-element.73.act, ...), custom_call_target="tpu_custom_call" | custom-call | flops 1000000000 | bytes 1024 | tf_op jit(solution)/shard_map/pallas_call | solution.py:903
  24.8 0.6 %collective-permute-start.4 = (bf16[384,384]{1,0:T(8,128)(2,1)S(1)}, bf16[384,384]{1,0:T(8,128)(2,1)S(1)}, u32[]{:S(2)}, u32[]{:S(2)}) collective-permute-start(bf16[384,384]{1,0:T(8,128)(2,1)S(1)} %get-tuple-element.86), channel_id=1, source_target_pairs={{0,1},{1,0},{2,3},{3,2},{4,5},{5,4},{6,7},{7,6},{8,9},{9,8},{10,11... | collective-permute-start | bytes 884744 | tf_op jit(solution)/shard_map/ppermute | solution.py:916
  25.4 1.3 %shard_map.169 = (bf16[192,256]{1,0:T(8,128)(2,1)S(1)}, bf16[256,192]{1,0:T(8,128)(2,1)S(1)}, bf16[256,192]{1,0:T(8,128)(2,1)S(1)}, f32[64,384]{1,0:T(8,128)S(1)}) custom-call(bf16[256,192]{1,0:T(8,128)(2,1)S(1)} %get-tuple-element.75.grad_ref, bf16[256,192]{1,0:T(8,128)(2,1)S(1)} %get-tuple-element.77.query, ...), custom_call_target="tpu_custom_call" | custom-call | flops 2000000000 | bytes 1024 | tf_op jit(solution)/shard_map/pallas_call | solution.py:903
  27.1 1.5 %collective-permute-start.10 = (bf16[240,384]{1,0:T(8,128)(2,1)S(1)}, bf16[240,384]{1,0:T(8,128)(2,1)S(1)}, u32[]{:S(2)}, u32[]{:S(2)}) collective-permute-start(bf16[240,384]{1,0:T(8,128)(2,1)S(1)} %get-tuple-element.98), channel_id=1, source_target_pairs={{0,6},{1,7},{2,4},{3,5},{4,2},{5,3},{6,0},{7,1},{8,14},{9,15},{10,... | collective-permute-start | bytes 552968 | tf_op jit(solution)/shard_map/ppermute | solution.py:916
  28.6 0.9 %collective-permute-start.11 = (bf16[240,384]{1,0:T(8,128)(2,1)S(1)}, bf16[240,384]{1,0:T(8,128)(2,1)S(1)}, u32[]{:S(2)}, u32[]{:S(2)}) collective-permute-start(bf16[240,384]{1,0:T(8,128)(2,1)S(1)} %get-tuple-element.99), channel_id=1, source_target_pairs={{0,4},{1,5},{2,6},{3,7},{4,0},{5,1},{6,2},{7,3},{8,12},{9,13},{10,... | collective-permute-start | bytes 552968 | tf_op jit(solution)/shard_map/ppermute | solution.py:916
  29.5 1.1 %collective-permute-start.12 = (bf16[240,384]{1,0:T(8,128)(2,1)S(1)}, bf16[240,384]{1,0:T(8,128)(2,1)S(1)}, u32[]{:S(2)}, u32[]{:S(2)}) collective-permute-start(bf16[240,384]{1,0:T(8,128)(2,1)S(1)} %get-tuple-element.100), channel_id=1, source_target_pairs={{0,2},{1,3},{2,0},{3,1},{4,6},{5,7},{6,4},{7,5},{8,10},{9,11},{10,... | collective-permute-start | bytes 552968 | tf_op jit(solution)/shard_map/ppermute | solution.py:916
  30.6 1.8 %shard_map.171 = (bf16[8,32,192]{2,1,0:T(8,128)(2,1)}, bf16[208,384]{1,0:T(8,128)(2,1)S(1)}, bf16[208,384]{1,0:T(8,128)(2,1)S(1)}) custom-call(bf16[8,32,192]{2,1,0:T(8,128)(2,1)S(1)} %copy-done.5, bf16[256,192]{1,0:T(8,128)(2,1)S(1)} %get-tuple-element.75.grad_ref, bf16[192,256]{1,0:T(8,128)(2,1)S(1)} %get-tuple-element.76.mix_t, ...), custom_call_target="tpu_custom_call" | custom-call | flops 4000000000 | bytes 1024 | tf_op jit(solution)/shard_map/pallas_call | solution.py:903
  32.4 1.4 %collective-permute-done.6.refs_1_ = bf16[208,384]{1,0:T(8,128)(2,1)S(1)} collective-permute-done((bf16[208,384]{1,0:T(8,128)(2,1)S(1)}, bf16[208,384]{1,0:T(8,128)(2,1)S(1)}, u32[]{:S(2)}, u32[]{:S(2)}) %collective-permute-start.6) | collective-permute-done | bytes 159776 | tf_op jit(solution)/shard_map/ppermute | solution.py:916
  33.8 1.5 %collective-permute-start.7 = (bf16[64,384]{1,0:T(8,128)(2,1)S(1)}, bf16[64,384]{1,0:T(8,128)(2,1)S(1)}, u32[]{:S(2)}, u32[]{:S(2)}) collective-permute-start(bf16[64,384]{1,0:T(8,128)(2,1)S(1)} %get-tuple-element.95), channel_id=1, source_target_pairs={{0,6},{1,7},{2,4},{3,5},{4,2},{5,3},{6,0},{7,1},{8,14},{9,15},{10,... | collective-permute-start | bytes 147464 | tf_op jit(solution)/shard_map/ppermute | solution.py:916
  35.4 0.9 %collective-permute-start.8 = (bf16[64,384]{1,0:T(8,128)(2,1)S(1)}, bf16[64,384]{1,0:T(8,128)(2,1)S(1)}, u32[]{:S(2)}, u32[]{:S(2)}) collective-permute-start(bf16[64,384]{1,0:T(8,128)(2,1)S(1)} %get-tuple-element.96), channel_id=1, source_target_pairs={{0,4},{1,5},{2,6},{3,7},{4,0},{5,1},{6,2},{7,3},{8,12},{9,13},{10,... | collective-permute-start | bytes 147464 | tf_op jit(solution)/shard_map/ppermute | solution.py:916
  36.3 1.1 %collective-permute-start.9 = (bf16[64,384]{1,0:T(8,128)(2,1)S(1)}, bf16[64,384]{1,0:T(8,128)(2,1)S(1)}, u32[]{:S(2)}, u32[]{:S(2)}) collective-permute-start(bf16[64,384]{1,0:T(8,128)(2,1)S(1)} %get-tuple-element.97), channel_id=1, source_target_pairs={{0,2},{1,3},{2,0},{3,1},{4,6},{5,7},{6,4},{7,5},{8,10},{9,11},{10,... | collective-permute-start | bytes 147464 | tf_op jit(solution)/shard_map/ppermute | solution.py:916
  37.4 1.9 %collective-permute-done.11.refs_2_ = bf16[240,384]{1,0:T(8,128)(2,1)S(1)} collective-permute-done((bf16[240,384]{1,0:T(8,128)(2,1)S(1)}, bf16[240,384]{1,0:T(8,128)(2,1)S(1)}, u32[]{:S(2)}, u32[]{:S(2)}) %collective-permute-start.11) | collective-permute-done | bytes 184352 | tf_op jit(solution)/shard_map/ppermute | solution.py:916
  39.4 0.5 shard_map.173
  39.9 0.6 %collective-permute-done.7.refs_1_ = bf16[64,384]{1,0:T(8,128)(2,1)S(1)} collective-permute-done((bf16[64,384]{1,0:T(8,128)(2,1)S(1)}, bf16[64,384]{1,0:T(8,128)(2,1)S(1)}, u32[]{:S(2)}, u32[]{:S(2)}) %collective-permute-start.7) | collective-permute-done | bytes 49184 | tf_op jit(solution)/shard_map/ppermute | solution.py:916
  40.5 0.4 collective-permute-done.8.refs_2_
  41.1 4.0 %collective-permute-start.13 = (bf16[248,128]{1,0:T(8,128)(2,1)S(1)}, bf16[248,128]{1,0:T(8,128)(2,1)S(1)}, u32[]{:S(2)}, u32[]{:S(2)}) collective-permute-start(bf16[248,128]{1,0:T(8,128)(2,1)S(1)} %get-tuple-element.104), channel_id=1, source_target_pairs={{0,24},{8,16},{16,8},{24,0},{1,25},{9,17},{17,9},{25,1},{2,26},{10... | collective-permute-start | bytes 190472 | tf_op jit(solution)/shard_map/ppermute | solution.py:916
  45.1 0.6 %collective-permute-start.14 = (bf16[248,128]{1,0:T(8,128)(2,1)S(1)}, bf16[248,128]{1,0:T(8,128)(2,1)S(1)}, u32[]{:S(2)}, u32[]{:S(2)}) collective-permute-start(bf16[248,128]{1,0:T(8,128)(2,1)S(1)} %get-tuple-element.105), channel_id=1, source_target_pairs={{0,16},{8,24},{16,0},{24,8},{1,17},{9,25},{17,1},{25,9},{2,18},{10... | collective-permute-start | bytes 190472 | tf_op jit(solution)/shard_map/ppermute | solution.py:916
  45.7 0.3 collective-permute-start.15
  46.0 1.6 %collective-permute-done.13.refs_1_ = bf16[248,128]{1,0:T(8,128)(2,1)S(1)} collective-permute-done((bf16[248,128]{1,0:T(8,128)(2,1)S(1)}, bf16[248,128]{1,0:T(8,128)(2,1)S(1)}, u32[]{:S(2)}, u32[]{:S(2)}) %collective-permute-start.13) | collective-permute-done | bytes 63520 | tf_op jit(solution)/shard_map/ppermute | solution.py:916
  47.6 3.8 %collective-permute-done.14.refs_2_ = bf16[248,128]{1,0:T(8,128)(2,1)S(1)} collective-permute-done((bf16[248,128]{1,0:T(8,128)(2,1)S(1)}, bf16[248,128]{1,0:T(8,128)(2,1)S(1)}, u32[]{:S(2)}, u32[]{:S(2)}) %collective-permute-start.14) | collective-permute-done | bytes 63520 | tf_op jit(solution)/shard_map/ppermute | solution.py:916
  51.5 0.9 %shard_map.175 = (f32[2,48,72]{2,1,0:T(8,128)}, f32[2,24,48]{2,1,0:T(8,128)}, f32[2,48,96]{2,1,0:T(8,128)}, f32[2,24,192]{2,1,0:T(8,128)}, f32[6,2,225]{2,1,0:T(2,128)}) custom-call(bf16[225,256]{1,0:T(8,128)(2,1)S(1)} %get-tuple-element.91.onehot_ref, bf16[248,128]{1,0:T(8,128)(2,1)S(1)} %get-tuple-element.103.refs_0_, ...), custom_call_target="tpu_custom_call" | custom-call | flops 200000000 | bytes 1024 | tf_op jit(solution)/shard_map/pallas_call | solution.py:903
  (39 shorter events, 1.4 us)
Async XLA Ops:
  0.6 0.7 %copy-start.8 = (f32[2,225,6]{1,0,2:T(2,128)S(1)}, f32[2,225,6]{1,0,2:T(2,128)}, u32[]{:S(2)}) copy-start(f32[2,225,6]{1,0,2:T(2,128)} %param.23) | copy-start | bytes 32404
  1.3 1.1 %copy-start = (bf16[2,192,768]{2,1,0:T(8,128)(2,1)S(1)}, bf16[2,192,768]{2,1,0:T(8,128)(2,1)}, u32[]{:S(2)}) copy-start(bf16[2,192,768]{2,1,0:T(8,128)(2,1)} %inner_w.5) | copy-start | bytes 1769476
  1.3 1.2 %copy-start.1 = (bf16[2,768,192]{1,2,0:T(8,128)(2,1)S(1)}, bf16[2,768,192]{1,2,0:T(8,128)(2,1)}, u32[]{:S(2)}) copy-start(bf16[2,768,192]{1,2,0:T(8,128)(2,1)} %param.22) | copy-start | bytes 1769476
  1.3 1.4 %copy-start.2 = (bf16[2,192,576]{2,1,0:T(8,128)(2,1)S(1)}, bf16[2,192,576]{2,1,0:T(8,128)(2,1)}, u32[]{:S(2)}) copy-start(bf16[2,192,576]{2,1,0:T(8,128)(2,1)} %qkv_w.5) | copy-start | bytes 1327108
  1.4 1.4 %copy-start.3 = (bf16[2,192,192]{2,1,0:T(8,128)(2,1)S(1)}, bf16[2,192,192]{2,1,0:T(8,128)(2,1)}, u32[]{:S(2)}) copy-start(bf16[2,192,192]{2,1,0:T(8,128)(2,1)} %proj_w.5) | copy-start | bytes 442372
  1.4 1.5 %copy-start.4 = (bf16[8,32,192]{2,1,0:T(8,128)(2,1)S(1)}, bf16[8,32,192]{2,1,0:T(8,128)(2,1)}, u32[]{:S(2)}) copy-start(bf16[8,32,192]{2,1,0:T(8,128)(2,1)} %cotangent.5) | copy-start | bytes 294916
  1.4 1.5 %copy-start.5 = (bf16[8,32,192]{2,1,0:T(8,128)(2,1)S(1)}, bf16[8,32,192]{2,1,0:T(8,128)(2,1)}, u32[]{:S(2)}) copy-start(bf16[8,32,192]{2,1,0:T(8,128)(2,1)} %tokens.3) | copy-start | bytes 294916
  1.4 1.5 %copy-start.10 = (s32[8,32]{1,0:T(8,128)S(1)}, s32[8,32]{1,0:T(8,128)}, u32[]{:S(2)}) copy-start(s32[8,32]{1,0:T(8,128)} %ids.3) | copy-start | bytes 3076
  2.9 8.1 %copy-start.6 = (bf16[4,32,192]{2,1,0:T(8,128)(2,1)S(1)}, bf16[4,32,192]{2,1,0:T(8,128)(2,1)}, u32[]{:S(2)}) copy-start(bf16[4,32,192]{2,1,0:T(8,128)(2,1)} %upper_rim.1) | copy-start | bytes 147460
  2.9 8.1 %copy-start.7 = (bf16[4,32,192]{2,1,0:T(8,128)(2,1)S(1)}, bf16[4,32,192]{2,1,0:T(8,128)(2,1)}, u32[]{:S(2)}) copy-start(bf16[4,32,192]{2,1,0:T(8,128)(2,1)} %lower_rim.1) | copy-start | bytes 147460
  4.8 6.2 %copy-start.12 = (s32[4,32]{1,0:T(4,128)S(1)}, s32[4,32]{1,0:T(4,128)}, u32[]{:S(2)}) copy-start(s32[4,32]{1,0:T(4,128)} %lower_ids.1) | copy-start | bytes 1540
  4.8 6.2 %copy-start.11 = (s32[4,32]{1,0:T(4,128)S(1)}, s32[4,32]{1,0:T(4,128)}, u32[]{:S(2)}) copy-start(s32[4,32]{1,0:T(4,128)} %upper_ids.1) | copy-start | bytes 1540
  4.8 6.1 %collective-permute-start = (bf16[144,384]{1,0:T(8,128)(2,1)S(1)}, bf16[144,384]{1,0:T(8,128)(2,1)S(1)}, u32[]{:S(2)}, u32[]{:S(2)}) collective-permute-start(bf16[144,384]{1,0:T(8,128)(2,1)S(1)} %get-tuple-element.60), channel_id=1, source_target_pairs={{0,8},{1,9},{2,10},{3,11},{4,12},{5,13},{6,14},{7,15},{8,0},{9,1},... | collective-permute-start | bytes 331784 | tf_op jit(solution)/shard_map/ppermute | solution.py:939
  7.9 3.1 %collective-permute-start.1 = (bf16[144,384]{1,0:T(8,128)(2,1)S(1)}, bf16[144,384]{1,0:T(8,128)(2,1)S(1)}, u32[]{:S(2)}, u32[]{:S(2)}) collective-permute-start(bf16[144,384]{1,0:T(8,128)(2,1)S(1)} %get-tuple-element.61), channel_id=1, source_target_pairs={{0,1},{1,0},{2,3},{3,2},{4,5},{5,4},{6,7},{7,6},{8,16},{9,17},{10,... | collective-permute-start | bytes 331784 | tf_op jit(solution)/shard_map/ppermute | solution.py:939
  11.0 2.1 %copy-start.9 = (f32[2,225,6]{1,0,2:T(2,128)S(1)}, f32[2,225,6]{1,0,2:T(2,128)}, u32[]{:S(2)}) copy-start(f32[2,225,6]{1,0,2:T(2,128)} %param.23) | copy-start | bytes 32404
  11.2 5.0 %collective-permute-start.2 = (bf16[80,384]{1,0:T(8,128)(2,1)S(1)}, bf16[80,384]{1,0:T(8,128)(2,1)S(1)}, u32[]{:S(2)}, u32[]{:S(2)}) collective-permute-start(bf16[80,384]{1,0:T(8,128)(2,1)S(1)} %get-tuple-element.64), channel_id=1, source_target_pairs={{1,2},{2,1},{3,4},{4,3},{5,6},{6,5},{7,0},{0,7},{9,10},{10,9},{11,... | collective-permute-start | bytes 184328 | tf_op jit(solution)/shard_map/ppermute | solution.py:925
  12.4 3.7 %collective-permute-start.3 = (bf16[80,384]{1,0:T(8,128)(2,1)S(1)}, bf16[80,384]{1,0:T(8,128)(2,1)S(1)}, u32[]{:S(2)}, u32[]{:S(2)}) collective-permute-start(bf16[80,384]{1,0:T(8,128)(2,1)S(1)} %get-tuple-element.65), channel_id=1, source_target_pairs={{0,1},{1,0},{2,3},{3,2},{4,5},{5,4},{6,7},{7,6},{8,9},{9,8},{10,11... | collective-permute-start | bytes 184328 | tf_op jit(solution)/shard_map/ppermute | solution.py:925
  24.0 2.7 %collective-permute-start.5 = (bf16[576,384]{1,0:T(8,128)(2,1)S(1)}, bf16[576,384]{1,0:T(8,128)(2,1)S(1)}, u32[]{:S(2)}, u32[]{:S(2)}) collective-permute-start(bf16[576,384]{1,0:T(8,128)(2,1)S(1)} %get-tuple-element.88), channel_id=1, source_target_pairs={{0,1},{1,0},{2,3},{3,2},{4,5},{5,4},{6,7},{7,6},{8,9},{9,8},{10,11... | collective-permute-start | bytes 1327112 | tf_op jit(solution)/shard_map/ppermute | solution.py:916
  24.8 1.9 %collective-permute-start.4 = (bf16[384,384]{1,0:T(8,128)(2,1)S(1)}, bf16[384,384]{1,0:T(8,128)(2,1)S(1)}, u32[]{:S(2)}, u32[]{:S(2)}) collective-permute-start(bf16[384,384]{1,0:T(8,128)(2,1)S(1)} %get-tuple-element.86), channel_id=1, source_target_pairs={{0,1},{1,0},{2,3},{3,2},{4,5},{5,4},{6,7},{7,6},{8,9},{9,8},{10,11... | collective-permute-start | bytes 884744 | tf_op jit(solution)/shard_map/ppermute | solution.py:916
  27.1 9.2 %collective-permute-start.10 = (bf16[240,384]{1,0:T(8,128)(2,1)S(1)}, bf16[240,384]{1,0:T(8,128)(2,1)S(1)}, u32[]{:S(2)}, u32[]{:S(2)}) collective-permute-start(bf16[240,384]{1,0:T(8,128)(2,1)S(1)} %get-tuple-element.98), channel_id=1, source_target_pairs={{0,6},{1,7},{2,4},{3,5},{4,2},{5,3},{6,0},{7,1},{8,14},{9,15},{10,... | collective-permute-start | bytes 552968 | tf_op jit(solution)/shard_map/ppermute | solution.py:916
  28.6 10.8 %collective-permute-start.11 = (bf16[240,384]{1,0:T(8,128)(2,1)S(1)}, bf16[240,384]{1,0:T(8,128)(2,1)S(1)}, u32[]{:S(2)}, u32[]{:S(2)}) collective-permute-start(bf16[240,384]{1,0:T(8,128)(2,1)S(1)} %get-tuple-element.99), channel_id=1, source_target_pairs={{0,4},{1,5},{2,6},{3,7},{4,0},{5,1},{6,2},{7,3},{8,12},{9,13},{10,... | collective-permute-start | bytes 552968 | tf_op jit(solution)/shard_map/ppermute | solution.py:916
  29.5 9.8 %collective-permute-start.12 = (bf16[240,384]{1,0:T(8,128)(2,1)S(1)}, bf16[240,384]{1,0:T(8,128)(2,1)S(1)}, u32[]{:S(2)}, u32[]{:S(2)}) collective-permute-start(bf16[240,384]{1,0:T(8,128)(2,1)S(1)} %get-tuple-element.100), channel_id=1, source_target_pairs={{0,2},{1,3},{2,0},{3,1},{4,6},{5,7},{6,4},{7,5},{8,10},{9,11},{10,... | collective-permute-start | bytes 552968 | tf_op jit(solution)/shard_map/ppermute | solution.py:916
  32.4 1.4 %collective-permute-start.6 = (bf16[208,384]{1,0:T(8,128)(2,1)S(1)}, bf16[208,384]{1,0:T(8,128)(2,1)S(1)}, u32[]{:S(2)}, u32[]{:S(2)}) collective-permute-start(bf16[208,384]{1,0:T(8,128)(2,1)S(1)} %get-tuple-element.93), channel_id=1, source_target_pairs={{0,1},{1,0},{2,3},{3,2},{4,5},{5,4},{6,7},{7,6},{8,9},{9,8},{10,11... | collective-permute-start | bytes 479240 | tf_op jit(solution)/shard_map/ppermute | solution.py:916
  33.8 6.6 %collective-permute-start.7 = (bf16[64,384]{1,0:T(8,128)(2,1)S(1)}, bf16[64,384]{1,0:T(8,128)(2,1)S(1)}, u32[]{:S(2)}, u32[]{:S(2)}) collective-permute-start(bf16[64,384]{1,0:T(8,128)(2,1)S(1)} %get-tuple-element.95), channel_id=1, source_target_pairs={{0,6},{1,7},{2,4},{3,5},{4,2},{5,3},{6,0},{7,1},{8,14},{9,15},{10,... | collective-permute-start | bytes 147464 | tf_op jit(solution)/shard_map/ppermute | solution.py:916
  35.4 5.5 %collective-permute-start.8 = (bf16[64,384]{1,0:T(8,128)(2,1)S(1)}, bf16[64,384]{1,0:T(8,128)(2,1)S(1)}, u32[]{:S(2)}, u32[]{:S(2)}) collective-permute-start(bf16[64,384]{1,0:T(8,128)(2,1)S(1)} %get-tuple-element.96), channel_id=1, source_target_pairs={{0,4},{1,5},{2,6},{3,7},{4,0},{5,1},{6,2},{7,3},{8,12},{9,13},{10,... | collective-permute-start | bytes 147464 | tf_op jit(solution)/shard_map/ppermute | solution.py:916
  36.3 4.5 %collective-permute-start.9 = (bf16[64,384]{1,0:T(8,128)(2,1)S(1)}, bf16[64,384]{1,0:T(8,128)(2,1)S(1)}, u32[]{:S(2)}, u32[]{:S(2)}) collective-permute-start(bf16[64,384]{1,0:T(8,128)(2,1)S(1)} %get-tuple-element.97), channel_id=1, source_target_pairs={{0,2},{1,3},{2,0},{3,1},{4,6},{5,7},{6,4},{7,5},{8,10},{9,11},{10,... | collective-permute-start | bytes 147464 | tf_op jit(solution)/shard_map/ppermute | solution.py:916
  41.1 6.5 %collective-permute-start.13 = (bf16[248,128]{1,0:T(8,128)(2,1)S(1)}, bf16[248,128]{1,0:T(8,128)(2,1)S(1)}, u32[]{:S(2)}, u32[]{:S(2)}) collective-permute-start(bf16[248,128]{1,0:T(8,128)(2,1)S(1)} %get-tuple-element.104), channel_id=1, source_target_pairs={{0,24},{8,16},{16,8},{24,0},{1,25},{9,17},{17,9},{25,1},{2,26},{10... | collective-permute-start | bytes 190472 | tf_op jit(solution)/shard_map/ppermute | solution.py:916
  45.1 6.3 %collective-permute-start.14 = (bf16[248,128]{1,0:T(8,128)(2,1)S(1)}, bf16[248,128]{1,0:T(8,128)(2,1)S(1)}, u32[]{:S(2)}, u32[]{:S(2)}) collective-permute-start(bf16[248,128]{1,0:T(8,128)(2,1)S(1)} %get-tuple-element.105), channel_id=1, source_target_pairs={{0,16},{8,24},{16,0},{24,8},{1,17},{9,25},{17,1},{25,9},{2,18},{10... | collective-permute-start | bytes 190472 | tf_op jit(solution)/shard_map/ppermute | solution.py:916
  45.7 5.8 %collective-permute-start.15 = (bf16[248,128]{1,0:T(8,128)(2,1)S(1)}, bf16[248,128]{1,0:T(8,128)(2,1)S(1)}, u32[]{:S(2)}, u32[]{:S(2)}) collective-permute-start(bf16[248,128]{1,0:T(8,128)(2,1)S(1)} %get-tuple-element.106), channel_id=1, source_target_pairs={{0,8},{8,0},{16,24},{24,16},{1,9},{9,1},{17,25},{25,17},{2,10},{10... | collective-permute-start | bytes 190472 | tf_op jit(solution)/shard_map/ppermute | solution.py:916

commit v4 on v3

--- a/solution.py
+++ b/solution.py
@@ -439,24 +439,15 @@
 def first_kernel(
     tokens,
     ids,
-    cotangent,
     qkv_w,
     proj_w,
-    inner_w,
-    outer_w,
     bias_ref,
-    first_out,
-    near,
-    far,
     query_out,
     key_out,
     value_out,
     probs_out,
     mix_out,
     middle_out,
-    pre_out,
-    act_out,
-    edge,
 ):
     rows, cols, channels = tokens.shape
     size = channels // (bias_ref.shape[1] // TOK)
@@ -475,6 +466,14 @@
     mix_out[...] = mix_t
     middle = (surface + tn(mix_t, proj_w[0])).astype(BF16)
     middle_out[...] = middle
+
+
+def feed_kernel(
+    middle_ref, ids, cotangent, inner_w, outer_w, first_out, near, far, pre_out, act_out, edge
+):
+    rows, cols, channels = first_out.shape
+    count = rows * cols
+    middle = middle_ref[...]
     normed = norm(middle.astype(F32))[0].astype(BF16)
     outs = []
     for at in range(0, count, 2 * TOK):
@@ -1017,31 +1016,33 @@
     band = (HALF * cols + 2 * WIN, 2 * channels)
     pair = ((TOK, width), F32)
     (bias_one,) = call(bias_kernel, [pair], [], bias_table, cost=6.0)
-    first_out, near, far, query, key, value, probs, mix, middle, pre, act = call(
+    query, key, value, probs, mix, middle = call(
         first_kernel,
+        [flat, flat, flat, ((count // TOK, TOK, width), F32), ((channels, count), BF16), flat],
+        [],
+        tokens,
+        region_ids,
+        qkv_weight,
+        proj_weight,
+        bias_one,
+        cost=2.0,
+    )
+    first_out, near, far, pre, act = call(
+        feed_kernel,
         [
             ((rows, cols, channels), BF16),
             (band, BF16),
             (band, BF16),
-            flat,
-            flat,
-            flat,
-            ((count // TOK, TOK, width), F32),
-            ((channels, count), BF16),
-            flat,
             ((count, hidden), F32),
             ((count, hidden), BF16),
         ],
         [pltpu.VMEM(band, F32)],
-        tokens,
+        middle,
         region_ids,
         cotangent,
-        qkv_weight,
-        proj_weight,
         inner_weight,
         outer_weight,
-        bias_one,
-        cost=3.0,
+        cost=1.0,
     )
     from_near = swap_rows(near, 0)
     from_far = swap_rows(far, 1)

time: 52.6 us -> 52.5 us (level)
    pallas_call x13 -> x14, Pallas kernels: 17.3 us -> 17.5 us  [call(): pl.pallas_call(kernel, out_shape=[jax.ShapeDtypeStruct(shape, kind) for s...]
where the time goes in v4:
time: 52.5 us; the launch traced here: 52.3 us
  starting transfers between devices  17.6 us (34%)
  Pallas kernels  17.5 us (33%)
  waiting for transfers between devices  15.1 us (29%)
  local copies, waits for them, and re-layouts  1.28 us (2%)
  between operations  0.85 us (2%)
    pallas_call x14, Pallas kernels, call(): pl.pallas_call(kernel, out_shape=[jax.ShapeDtypeStruct(shape, kind) for s...  17.5 us
    ppermute x12, starting transfers between devices, flip(): return lax.ppermute(values, axis, [(i, i ^ bit) for i in range(count)])  12.6 us
    ppermute x12, waiting for transfers between devices, flip(): return lax.ppermute(values, axis, [(i, i ^ bit) for i in range(count)])  9.75 us
    ppermute x2, starting transfers between devices, swap_rows(): return lax.ppermute(values, ('rows', 'cols'), pairs)  3.09 us
    ppermute x2, waiting for transfers between devices, swap_rows(): return lax.ppermute(values, ('rows', 'cols'), pairs)  3.05 us
    ppermute x2, waiting for transfers between devices, swap_cols(): return lax.ppermute(values, 'cols', pairs)  2.27 us
    ppermute x2, starting transfers between devices, swap_cols(): return lax.ppermute(values, 'cols', pairs)  1.84 us
    unnamed x26, local copies, waits for them, and re-layouts  1.28 us
  transfers between devices with their start and end apart: 16, of which 8 were waited for; matrix products, arithmetic and copies ran while one was open for 0% of the time, Pallas kernels for 10%

profile of v4, /device:TPU:0, one launch (start us, length us, event | category | flops | bytes accessed | tf_op | source)
XLA Modules:
  0.0 52.3 jit_solution(7930806433331352041)
XLA Ops:
  0.6 0.7 %copy-done.8 = f32[2,225,6]{1,0,2:T(2,128)S(1)} copy-done((f32[2,225,6]{1,0,2:T(2,128)S(1)}, f32[2,225,6]{1,0,2:T(2,128)}, u32[]{:S(2)}) %copy-start.8) | copy-done | bytes 10824
  1.4 0.6 %shard_map.163.bias_ref = f32[64,384]{1,0:T(8,128)S(1)} custom-call(f32[6,2,225]{2,1,0:T(2,128)S(1)} %bitcast.8), custom_call_target="tpu_custom_call" | custom-call | flops 6000000000 | bytes 1024 | tf_op jit(solution)/shard_map/pallas_call | solution.py:902
  2.0 0.4 copy-done.2
  2.5 1.3 %shard_map.164 = (bf16[256,192]{1,0:T(8,128)(2,1)S(1)}, bf16[256,192]{1,0:T(8,128)(2,1)S(1)}, bf16[256,192]{1,0:T(8,128)(2,1)S(1)}, f32[4,64,384]{2,1,0:T(8,128)...) custom-call(bf16[8,32,192]{2,1,0:T(8,128)(2,1)S(1)} %copy-done.5, s32[8,32]{1,0:T(8,128)S(1)} %copy-done.10, ...), custom_call_target="tpu_custom_call" | custom-call | flops 2000000000 | bytes 1024 | tf_op jit(solution)/shard_map/pallas_call | solution.py:902
  3.9 0.7 %shard_map.165 = (bf16[8,32,192]{2,1,0:T(8,128)(2,1)S(1)}, bf16[144,384]{1,0:T(8,128)(2,1)S(1)}, bf16[144,384]{1,0:T(8,128)(2,1)S(1)}, f32[256,768]{1,0:T(8,128)S(1)}, bf16[256,768]{1,0:T(8,128)(2,1)S(1)}) custom-call(bf16[256,192]{1,0:T(8,128)(2,1)S(1)} %get-tuple-element.59.middle_ref, s32[8,32]{1,0:T(8,128)S(1)} %copy-done.10, ...), custom_call_target="tpu_custom_call" | custom-call | flops 1000000000 | bytes 1024 | tf_op jit(solution)/shard_map/pallas_call | solution.py:902
  4.7 3.1 %collective-permute-start = (bf16[144,384]{1,0:T(8,128)(2,1)S(1)}, bf16[144,384]{1,0:T(8,128)(2,1)S(1)}, u32[]{:S(2)}, u32[]{:S(2)}) collective-permute-start(bf16[144,384]{1,0:T(8,128)(2,1)S(1)} %get-tuple-element.61), channel_id=1, source_target_pairs={{0,8},{1,9},{2,10},{3,11},{4,12},{5,13},{6,14},{7,15},{8,0},{9,1},... | collective-permute-start | bytes 331784 | tf_op jit(solution)/shard_map/ppermute | solution.py:938
  7.8 3.1 %collective-permute-done.from_near = bf16[144,384]{1,0:T(8,128)(2,1)S(1)} collective-permute-done((bf16[144,384]{1,0:T(8,128)(2,1)S(1)}, bf16[144,384]{1,0:T(8,128)(2,1)S(1)}, u32[]{:S(2)}, u32[]{:S(2)}) %collective-permute-start) | collective-permute-done | bytes 110624 | tf_op jit(solution)/shard_map/ppermute | solution.py:938
  11.1 1.2 %collective-permute-start.2 = (bf16[80,384]{1,0:T(8,128)(2,1)S(1)}, bf16[80,384]{1,0:T(8,128)(2,1)S(1)}, u32[]{:S(2)}, u32[]{:S(2)}) collective-permute-start(bf16[80,384]{1,0:T(8,128)(2,1)S(1)} %get-tuple-element.65), channel_id=1, source_target_pairs={{1,2},{2,1},{3,4},{4,3},{5,6},{6,5},{7,0},{0,7},{9,10},{10,9},{11,... | collective-permute-start | bytes 184328 | tf_op jit(solution)/shard_map/ppermute | solution.py:924
  12.3 0.6 %collective-permute-start.3 = (bf16[80,384]{1,0:T(8,128)(2,1)S(1)}, bf16[80,384]{1,0:T(8,128)(2,1)S(1)}, u32[]{:S(2)}, u32[]{:S(2)}) collective-permute-start(bf16[80,384]{1,0:T(8,128)(2,1)S(1)} %get-tuple-element.66), channel_id=1, source_target_pairs={{0,1},{1,0},{2,3},{3,2},{4,5},{5,4},{6,7},{7,6},{8,9},{9,8},{10,11... | collective-permute-start | bytes 184328 | tf_op jit(solution)/shard_map/ppermute | solution.py:924
  12.9 0.9 %shard_map.167 = (f32[256,768]{1,0:T(8,128)S(1)}, bf16[192,256]{1,0:T(8,128)(2,1)S(1)}, f32[64,384]{1,0:T(8,128)S(1)}, bf16[225,256]{1,0:T(8,128)(2,1)S(1)}) custom-call(f32[256,768]{1,0:T(8,128)S(1)} %get-tuple-element.68.pre, bf16[256,192]{1,0:T(8,128)(2,1)S(1)} %get-tuple-element.69.key, f32[6,2,225]{2,1,0:T(2,128)S(1)} %bitcast.9), custom_call_target="tpu_custom_call" | custom-call | flops 1000000000 | bytes 1024 | tf_op jit(solution)/shard_map/pallas_call | solution.py:902
  13.8 2.3 %collective-permute-done.2.far = bf16[80,384]{1,0:T(8,128)(2,1)S(1)} collective-permute-done((bf16[80,384]{1,0:T(8,128)(2,1)S(1)}, bf16[80,384]{1,0:T(8,128)(2,1)S(1)}, u32[]{:S(2)}, u32[]{:S(2)}) %collective-permute-start.2) | collective-permute-done | bytes 61472 | tf_op jit(solution)/shard_map/ppermute | solution.py:924
  16.1 7.9 %shard_map.168 = (bf16[256,192]{1,0:T(8,128)(2,1)S(1)}, f32[8,256]{1,0:T(8,128)S(1)}, bf16[576,384]{1,0:T(8,128)(2,1)S(1)}, bf16[576,384]{1,0:T(8,128)(2,1)S(1)}) custom-call(bf16[8,32,192]{2,1,0:T(8,128)(2,1)S(1)} %get-tuple-element.60.first_out, bf16[8,32,192]{2,1,0:T(8,128)(2,1)S(1)} %copy-done.4, bf16[128,384]{1,0:T(8,128)(2,1)S(1)} %get-tuple-element.63.up, ...), custom_call_target="tpu_custom_call" | custom-call | flops 12000000000 | bytes 1024 | tf_op jit(solution)/shard_map/pallas_call | solution.py:902
  24.0 0.8 %shard_map.169 = (bf16[256,192]{1,0:T(8,128)(2,1)S(1)}, bf16[384,384]{1,0:T(8,128)(2,1)S(1)}, bf16[384,384]{1,0:T(8,128)(2,1)S(1)}) custom-call(bf16[256,192]{1,0:T(8,128)(2,1)S(1)} %get-tuple-element.72.grad_ref, bf16[256,192]{1,0:T(8,128)(2,1)S(1)} %get-tuple-element.59.middle_ref, bf16[256,768]{1,0:T(8,128)(2,1)S(1)} %get-tuple-element.73.act, ...), custom_call_target="tpu_custom_call" | custom-call | flops 1000000000 | bytes 1024 | tf_op jit(solution)/shard_map/pallas_call | solution.py:902
  24.8 0.6 %collective-permute-start.4 = (bf16[384,384]{1,0:T(8,128)(2,1)S(1)}, bf16[384,384]{1,0:T(8,128)(2,1)S(1)}, u32[]{:S(2)}, u32[]{:S(2)}) collective-permute-start(bf16[384,384]{1,0:T(8,128)(2,1)S(1)} %get-tuple-element.86), channel_id=1, source_target_pairs={{0,1},{1,0},{2,3},{3,2},{4,5},{5,4},{6,7},{7,6},{8,9},{9,8},{10,11... | collective-permute-start | bytes 884744 | tf_op jit(solution)/shard_map/ppermute | solution.py:915
  25.3 1.3 %shard_map.170 = (bf16[192,256]{1,0:T(8,128)(2,1)S(1)}, bf16[256,192]{1,0:T(8,128)(2,1)S(1)}, bf16[256,192]{1,0:T(8,128)(2,1)S(1)}, f32[64,384]{1,0:T(8,128)S(1)}) custom-call(bf16[256,192]{1,0:T(8,128)(2,1)S(1)} %get-tuple-element.75.grad_ref, bf16[256,192]{1,0:T(8,128)(2,1)S(1)} %get-tuple-element.77.query, ...), custom_call_target="tpu_custom_call" | custom-call | flops 2000000000 | bytes 1024 | tf_op jit(solution)/shard_map/pallas_call | solution.py:902
  27.0 1.5 %collective-permute-start.10 = (bf16[240,384]{1,0:T(8,128)(2,1)S(1)}, bf16[240,384]{1,0:T(8,128)(2,1)S(1)}, u32[]{:S(2)}, u32[]{:S(2)}) collective-permute-start(bf16[240,384]{1,0:T(8,128)(2,1)S(1)} %get-tuple-element.98), channel_id=1, source_target_pairs={{0,6},{1,7},{2,4},{3,5},{4,2},{5,3},{6,0},{7,1},{8,14},{9,15},{10,... | collective-permute-start | bytes 552968 | tf_op jit(solution)/shard_map/ppermute | solution.py:915
  28.5 0.9 %collective-permute-start.11 = (bf16[240,384]{1,0:T(8,128)(2,1)S(1)}, bf16[240,384]{1,0:T(8,128)(2,1)S(1)}, u32[]{:S(2)}, u32[]{:S(2)}) collective-permute-start(bf16[240,384]{1,0:T(8,128)(2,1)S(1)} %get-tuple-element.99), channel_id=1, source_target_pairs={{0,4},{1,5},{2,6},{3,7},{4,0},{5,1},{6,2},{7,3},{8,12},{9,13},{10,... | collective-permute-start | bytes 552968 | tf_op jit(solution)/shard_map/ppermute | solution.py:915
  29.5 1.1 %collective-permute-start.12 = (bf16[240,384]{1,0:T(8,128)(2,1)S(1)}, bf16[240,384]{1,0:T(8,128)(2,1)S(1)}, u32[]{:S(2)}, u32[]{:S(2)}) collective-permute-start(bf16[240,384]{1,0:T(8,128)(2,1)S(1)} %get-tuple-element.100), channel_id=1, source_target_pairs={{0,2},{1,3},{2,0},{3,1},{4,6},{5,7},{6,4},{7,5},{8,10},{9,11},{10,... | collective-permute-start | bytes 552968 | tf_op jit(solution)/shard_map/ppermute | solution.py:915
  30.6 1.8 %shard_map.172 = (bf16[8,32,192]{2,1,0:T(8,128)(2,1)}, bf16[208,384]{1,0:T(8,128)(2,1)S(1)}, bf16[208,384]{1,0:T(8,128)(2,1)S(1)}) custom-call(bf16[8,32,192]{2,1,0:T(8,128)(2,1)S(1)} %copy-done.5, bf16[256,192]{1,0:T(8,128)(2,1)S(1)} %get-tuple-element.75.grad_ref, bf16[192,256]{1,0:T(8,128)(2,1)S(1)} %get-tuple-element.76.mix_t, ...), custom_call_target="tpu_custom_call" | custom-call | flops 4000000000 | bytes 1024 | tf_op jit(solution)/shard_map/pallas_call | solution.py:902
  32.3 1.4 %collective-permute-done.6.refs_1_ = bf16[208,384]{1,0:T(8,128)(2,1)S(1)} collective-permute-done((bf16[208,384]{1,0:T(8,128)(2,1)S(1)}, bf16[208,384]{1,0:T(8,128)(2,1)S(1)}, u32[]{:S(2)}, u32[]{:S(2)}) %collective-permute-start.6) | collective-permute-done | bytes 159776 | tf_op jit(solution)/shard_map/ppermute | solution.py:915
  33.8 1.5 %collective-permute-start.7 = (bf16[64,384]{1,0:T(8,128)(2,1)S(1)}, bf16[64,384]{1,0:T(8,128)(2,1)S(1)}, u32[]{:S(2)}, u32[]{:S(2)}) collective-permute-start(bf16[64,384]{1,0:T(8,128)(2,1)S(1)} %get-tuple-element.95), channel_id=1, source_target_pairs={{0,6},{1,7},{2,4},{3,5},{4,2},{5,3},{6,0},{7,1},{8,14},{9,15},{10,... | collective-permute-start | bytes 147464 | tf_op jit(solution)/shard_map/ppermute | solution.py:915
  35.3 0.9 %collective-permute-start.8 = (bf16[64,384]{1,0:T(8,128)(2,1)S(1)}, bf16[64,384]{1,0:T(8,128)(2,1)S(1)}, u32[]{:S(2)}, u32[]{:S(2)}) collective-permute-start(bf16[64,384]{1,0:T(8,128)(2,1)S(1)} %get-tuple-element.96), channel_id=1, source_target_pairs={{0,4},{1,5},{2,6},{3,7},{4,0},{5,1},{6,2},{7,3},{8,12},{9,13},{10,... | collective-permute-start | bytes 147464 | tf_op jit(solution)/shard_map/ppermute | solution.py:915
  36.2 1.1 %collective-permute-start.9 = (bf16[64,384]{1,0:T(8,128)(2,1)S(1)}, bf16[64,384]{1,0:T(8,128)(2,1)S(1)}, u32[]{:S(2)}, u32[]{:S(2)}) collective-permute-start(bf16[64,384]{1,0:T(8,128)(2,1)S(1)} %get-tuple-element.97), channel_id=1, source_target_pairs={{0,2},{1,3},{2,0},{3,1},{4,6},{5,7},{6,4},{7,5},{8,10},{9,11},{10,... | collective-permute-start | bytes 147464 | tf_op jit(solution)/shard_map/ppermute | solution.py:915
  37.3 2.0 %collective-permute-done.11.refs_2_ = bf16[240,384]{1,0:T(8,128)(2,1)S(1)} collective-permute-done((bf16[240,384]{1,0:T(8,128)(2,1)S(1)}, bf16[240,384]{1,0:T(8,128)(2,1)S(1)}, u32[]{:S(2)}, u32[]{:S(2)}) %collective-permute-start.11) | collective-permute-done | bytes 184352 | tf_op jit(solution)/shard_map/ppermute | solution.py:915
  39.3 0.5 shard_map.174
  39.8 0.6 %collective-permute-done.7.refs_1_ = bf16[64,384]{1,0:T(8,128)(2,1)S(1)} collective-permute-done((bf16[64,384]{1,0:T(8,128)(2,1)S(1)}, bf16[64,384]{1,0:T(8,128)(2,1)S(1)}, u32[]{:S(2)}, u32[]{:S(2)}) %collective-permute-start.7) | collective-permute-done | bytes 49184 | tf_op jit(solution)/shard_map/ppermute | solution.py:915
  40.4 0.4 collective-permute-done.8.refs_2_
  41.1 4.0 %collective-permute-start.13 = (bf16[248,128]{1,0:T(8,128)(2,1)S(1)}, bf16[248,128]{1,0:T(8,128)(2,1)S(1)}, u32[]{:S(2)}, u32[]{:S(2)}) collective-permute-start(bf16[248,128]{1,0:T(8,128)(2,1)S(1)} %get-tuple-element.104), channel_id=1, source_target_pairs={{0,24},{8,16},{16,8},{24,0},{1,25},{9,17},{17,9},{25,1},{2,26},{10... | collective-permute-start | bytes 190472 | tf_op jit(solution)/shard_map/ppermute | solution.py:915
  45.1 0.6 %collective-permute-start.14 = (bf16[248,128]{1,0:T(8,128)(2,1)S(1)}, bf16[248,128]{1,0:T(8,128)(2,1)S(1)}, u32[]{:S(2)}, u32[]{:S(2)}) collective-permute-start(bf16[248,128]{1,0:T(8,128)(2,1)S(1)} %get-tuple-element.105), channel_id=1, source_target_pairs={{0,16},{8,24},{16,0},{24,8},{1,17},{9,25},{17,1},{25,9},{2,18},{10... | collective-permute-start | bytes 190472 | tf_op jit(solution)/shard_map/ppermute | solution.py:915
  46.0 1.6 %collective-permute-done.13.refs_1_ = bf16[248,128]{1,0:T(8,128)(2,1)S(1)} collective-permute-done((bf16[248,128]{1,0:T(8,128)(2,1)S(1)}, bf16[248,128]{1,0:T(8,128)(2,1)S(1)}, u32[]{:S(2)}, u32[]{:S(2)}) %collective-permute-start.13) | collective-permute-done | bytes 63520 | tf_op jit(solution)/shard_map/ppermute | solution.py:915
  47.6 3.8 %collective-permute-done.14.refs_2_ = bf16[248,128]{1,0:T(8,128)(2,1)S(1)} collective-permute-done((bf16[248,128]{1,0:T(8,128)(2,1)S(1)}, bf16[248,128]{1,0:T(8,128)(2,1)S(1)}, u32[]{:S(2)}, u32[]{:S(2)}) %collective-permute-start.14) | collective-permute-done | bytes 63520 | tf_op jit(solution)/shard_map/ppermute | solution.py:915
  51.4 0.9 %shard_map.176 = (f32[2,48,72]{2,1,0:T(8,128)}, f32[2,24,48]{2,1,0:T(8,128)}, f32[2,48,96]{2,1,0:T(8,128)}, f32[2,24,192]{2,1,0:T(8,128)}, f32[6,2,225]{2,1,0:T(2,128)}) custom-call(bf16[225,256]{1,0:T(8,128)(2,1)S(1)} %get-tuple-element.91.onehot_ref, bf16[248,128]{1,0:T(8,128)(2,1)S(1)} %get-tuple-element.103.refs_0_, ...), custom_call_target="tpu_custom_call" | custom-call | flops 200000000 | bytes 1024 | tf_op jit(solution)/shard_map/pallas_call | solution.py:902
  (40 shorter events, 1.5 us)
Async XLA Ops:
  0.6 0.7 %copy-start.8 = (f32[2,225,6]{1,0,2:T(2,128)S(1)}, f32[2,225,6]{1,0,2:T(2,128)}, u32[]{:S(2)}) copy-start(f32[2,225,6]{1,0,2:T(2,128)} %param.23) | copy-start | bytes 32404
  1.3 1.0 %copy-start.2 = (bf16[2,192,576]{2,1,0:T(8,128)(2,1)S(1)}, bf16[2,192,576]{2,1,0:T(8,128)(2,1)}, u32[]{:S(2)}) copy-start(bf16[2,192,576]{2,1,0:T(8,128)(2,1)} %qkv_w.5) | copy-start | bytes 1327108
  1.3 1.1 %copy-start.3 = (bf16[2,192,192]{2,1,0:T(8,128)(2,1)S(1)}, bf16[2,192,192]{2,1,0:T(8,128)(2,1)}, u32[]{:S(2)}) copy-start(bf16[2,192,192]{2,1,0:T(8,128)(2,1)} %proj_w.5) | copy-start | bytes 442372
  1.3 1.1 %copy-start.5 = (bf16[8,32,192]{2,1,0:T(8,128)(2,1)S(1)}, bf16[8,32,192]{2,1,0:T(8,128)(2,1)}, u32[]{:S(2)}) copy-start(bf16[8,32,192]{2,1,0:T(8,128)(2,1)} %tokens.3) | copy-start | bytes 294916
  1.3 1.1 %copy-start.10 = (s32[8,32]{1,0:T(8,128)S(1)}, s32[8,32]{1,0:T(8,128)}, u32[]{:S(2)}) copy-start(s32[8,32]{1,0:T(8,128)} %ids.5) | copy-start | bytes 3076
  2.5 1.4 %copy-start = (bf16[2,192,768]{2,1,0:T(8,128)(2,1)S(1)}, bf16[2,192,768]{2,1,0:T(8,128)(2,1)}, u32[]{:S(2)}) copy-start(bf16[2,192,768]{2,1,0:T(8,128)(2,1)} %inner_w.5) | copy-start | bytes 1769476
  2.5 1.4 %copy-start.1 = (bf16[2,768,192]{1,2,0:T(8,128)(2,1)S(1)}, bf16[2,768,192]{1,2,0:T(8,128)(2,1)}, u32[]{:S(2)}) copy-start(bf16[2,768,192]{1,2,0:T(8,128)(2,1)} %param.22) | copy-start | bytes 1769476
  2.5 1.4 %copy-start.4 = (bf16[8,32,192]{2,1,0:T(8,128)(2,1)S(1)}, bf16[8,32,192]{2,1,0:T(8,128)(2,1)}, u32[]{:S(2)}) copy-start(bf16[8,32,192]{2,1,0:T(8,128)(2,1)} %cotangent.5) | copy-start | bytes 294916
  3.9 6.9 %copy-start.6 = (bf16[4,32,192]{2,1,0:T(8,128)(2,1)S(1)}, bf16[4,32,192]{2,1,0:T(8,128)(2,1)}, u32[]{:S(2)}) copy-start(bf16[4,32,192]{2,1,0:T(8,128)(2,1)} %upper_rim.1) | copy-start | bytes 147460
  3.9 6.9 %copy-start.7 = (bf16[4,32,192]{2,1,0:T(8,128)(2,1)S(1)}, bf16[4,32,192]{2,1,0:T(8,128)(2,1)}, u32[]{:S(2)}) copy-start(bf16[4,32,192]{2,1,0:T(8,128)(2,1)} %lower_rim.1) | copy-start | bytes 147460
  4.6 6.2 %copy-start.12 = (s32[4,32]{1,0:T(4,128)S(1)}, s32[4,32]{1,0:T(4,128)}, u32[]{:S(2)}) copy-start(s32[4,32]{1,0:T(4,128)} %lower_ids.1) | copy-start | bytes 1540
  4.7 6.2 %copy-start.11 = (s32[4,32]{1,0:T(4,128)S(1)}, s32[4,32]{1,0:T(4,128)}, u32[]{:S(2)}) copy-start(s32[4,32]{1,0:T(4,128)} %upper_ids.1) | copy-start | bytes 1540
  4.7 6.1 %collective-permute-start = (bf16[144,384]{1,0:T(8,128)(2,1)S(1)}, bf16[144,384]{1,0:T(8,128)(2,1)S(1)}, u32[]{:S(2)}, u32[]{:S(2)}) collective-permute-start(bf16[144,384]{1,0:T(8,128)(2,1)S(1)} %get-tuple-element.61), channel_id=1, source_target_pairs={{0,8},{1,9},{2,10},{3,11},{4,12},{5,13},{6,14},{7,15},{8,0},{9,1},... | collective-permute-start | bytes 331784 | tf_op jit(solution)/shard_map/ppermute | solution.py:938
  7.8 3.1 %collective-permute-start.1 = (bf16[144,384]{1,0:T(8,128)(2,1)S(1)}, bf16[144,384]{1,0:T(8,128)(2,1)S(1)}, u32[]{:S(2)}, u32[]{:S(2)}) collective-permute-start(bf16[144,384]{1,0:T(8,128)(2,1)S(1)} %get-tuple-element.62), channel_id=1, source_target_pairs={{0,1},{1,0},{2,3},{3,2},{4,5},{5,4},{6,7},{7,6},{8,16},{9,17},{10,... | collective-permute-start | bytes 331784 | tf_op jit(solution)/shard_map/ppermute | solution.py:938
  10.8 2.0 %copy-start.9 = (f32[2,225,6]{1,0,2:T(2,128)S(1)}, f32[2,225,6]{1,0,2:T(2,128)}, u32[]{:S(2)}) copy-start(f32[2,225,6]{1,0,2:T(2,128)} %param.23) | copy-start | bytes 32404
  11.1 5.0 %collective-permute-start.2 = (bf16[80,384]{1,0:T(8,128)(2,1)S(1)}, bf16[80,384]{1,0:T(8,128)(2,1)S(1)}, u32[]{:S(2)}, u32[]{:S(2)}) collective-permute-start(bf16[80,384]{1,0:T(8,128)(2,1)S(1)} %get-tuple-element.65), channel_id=1, source_target_pairs={{1,2},{2,1},{3,4},{4,3},{5,6},{6,5},{7,0},{0,7},{9,10},{10,9},{11,... | collective-permute-start | bytes 184328 | tf_op jit(solution)/shard_map/ppermute | solution.py:924
  12.3 3.8 %collective-permute-start.3 = (bf16[80,384]{1,0:T(8,128)(2,1)S(1)}, bf16[80,384]{1,0:T(8,128)(2,1)S(1)}, u32[]{:S(2)}, u32[]{:S(2)}) collective-permute-start(bf16[80,384]{1,0:T(8,128)(2,1)S(1)} %get-tuple-element.66), channel_id=1, source_target_pairs={{0,1},{1,0},{2,3},{3,2},{4,5},{5,4},{6,7},{7,6},{8,9},{9,8},{10,11... | collective-permute-start | bytes 184328 | tf_op jit(solution)/shard_map/ppermute | solution.py:924
  23.9 2.7 %collective-permute-start.5 = (bf16[576,384]{1,0:T(8,128)(2,1)S(1)}, bf16[576,384]{1,0:T(8,128)(2,1)S(1)}, u32[]{:S(2)}, u32[]{:S(2)}) collective-permute-start(bf16[576,384]{1,0:T(8,128)(2,1)S(1)} %get-tuple-element.88), channel_id=1, source_target_pairs={{0,1},{1,0},{2,3},{3,2},{4,5},{5,4},{6,7},{7,6},{8,9},{9,8},{10,11... | collective-permute-start | bytes 1327112 | tf_op jit(solution)/shard_map/ppermute | solution.py:915
  24.8 1.9 %collective-permute-start.4 = (bf16[384,384]{1,0:T(8,128)(2,1)S(1)}, bf16[384,384]{1,0:T(8,128)(2,1)S(1)}, u32[]{:S(2)}, u32[]{:S(2)}) collective-permute-start(bf16[384,384]{1,0:T(8,128)(2,1)S(1)} %get-tuple-element.86), channel_id=1, source_target_pairs={{0,1},{1,0},{2,3},{3,2},{4,5},{5,4},{6,7},{7,6},{8,9},{9,8},{10,11... | collective-permute-start | bytes 884744 | tf_op jit(solution)/shard_map/ppermute | solution.py:915
  27.0 9.2 %collective-permute-start.10 = (bf16[240,384]{1,0:T(8,128)(2,1)S(1)}, bf16[240,384]{1,0:T(8,128)(2,1)S(1)}, u32[]{:S(2)}, u32[]{:S(2)}) collective-permute-start(bf16[240,384]{1,0:T(8,128)(2,1)S(1)} %get-tuple-element.98), channel_id=1, source_target_pairs={{0,6},{1,7},{2,4},{3,5},{4,2},{5,3},{6,0},{7,1},{8,14},{9,15},{10,... | collective-permute-start | bytes 552968 | tf_op jit(solution)/shard_map/ppermute | solution.py:915
  28.5 10.8 %collective-permute-start.11 = (bf16[240,384]{1,0:T(8,128)(2,1)S(1)}, bf16[240,384]{1,0:T(8,128)(2,1)S(1)}, u32[]{:S(2)}, u32[]{:S(2)}) collective-permute-start(bf16[240,384]{1,0:T(8,128)(2,1)S(1)} %get-tuple-element.99), channel_id=1, source_target_pairs={{0,4},{1,5},{2,6},{3,7},{4,0},{5,1},{6,2},{7,3},{8,12},{9,13},{10,... | collective-permute-start | bytes 552968 | tf_op jit(solution)/shard_map/ppermute | solution.py:915
  29.5 9.8 %collective-permute-start.12 = (bf16[240,384]{1,0:T(8,128)(2,1)S(1)}, bf16[240,384]{1,0:T(8,128)(2,1)S(1)}, u32[]{:S(2)}, u32[]{:S(2)}) collective-permute-start(bf16[240,384]{1,0:T(8,128)(2,1)S(1)} %get-tuple-element.100), channel_id=1, source_target_pairs={{0,2},{1,3},{2,0},{3,1},{4,6},{5,7},{6,4},{7,5},{8,10},{9,11},{10,... | collective-permute-start | bytes 552968 | tf_op jit(solution)/shard_map/ppermute | solution.py:915
  32.3 1.4 %collective-permute-start.6 = (bf16[208,384]{1,0:T(8,128)(2,1)S(1)}, bf16[208,384]{1,0:T(8,128)(2,1)S(1)}, u32[]{:S(2)}, u32[]{:S(2)}) collective-permute-start(bf16[208,384]{1,0:T(8,128)(2,1)S(1)} %get-tuple-element.93), channel_id=1, source_target_pairs={{0,1},{1,0},{2,3},{3,2},{4,5},{5,4},{6,7},{7,6},{8,9},{9,8},{10,11... | collective-permute-start | bytes 479240 | tf_op jit(solution)/shard_map/ppermute | solution.py:915
  33.8 6.6 %collective-permute-start.7 = (bf16[64,384]{1,0:T(8,128)(2,1)S(1)}, bf16[64,384]{1,0:T(8,128)(2,1)S(1)}, u32[]{:S(2)}, u32[]{:S(2)}) collective-permute-start(bf16[64,384]{1,0:T(8,128)(2,1)S(1)} %get-tuple-element.95), channel_id=1, source_target_pairs={{0,6},{1,7},{2,4},{3,5},{4,2},{5,3},{6,0},{7,1},{8,14},{9,15},{10,... | collective-permute-start | bytes 147464 | tf_op jit(solution)/shard_map/ppermute | solution.py:915
  35.3 5.5 %collective-permute-start.8 = (bf16[64,384]{1,0:T(8,128)(2,1)S(1)}, bf16[64,384]{1,0:T(8,128)(2,1)S(1)}, u32[]{:S(2)}, u32[]{:S(2)}) collective-permute-start(bf16[64,384]{1,0:T(8,128)(2,1)S(1)} %get-tuple-element.96), channel_id=1, source_target_pairs={{0,4},{1,5},{2,6},{3,7},{4,0},{5,1},{6,2},{7,3},{8,12},{9,13},{10,... | collective-permute-start | bytes 147464 | tf_op jit(solution)/shard_map/ppermute | solution.py:915
  36.2 4.6 %collective-permute-start.9 = (bf16[64,384]{1,0:T(8,128)(2,1)S(1)}, bf16[64,384]{1,0:T(8,128)(2,1)S(1)}, u32[]{:S(2)}, u32[]{:S(2)}) collective-permute-start(bf16[64,384]{1,0:T(8,128)(2,1)S(1)} %get-tuple-element.97), channel_id=1, source_target_pairs={{0,2},{1,3},{2,0},{3,1},{4,6},{5,7},{6,4},{7,5},{8,10},{9,11},{10,... | collective-permute-start | bytes 147464 | tf_op jit(solution)/shard_map/ppermute | solution.py:915
  41.1 6.5 %collective-permute-start.13 = (bf16[248,128]{1,0:T(8,128)(2,1)S(1)}, bf16[248,128]{1,0:T(8,128)(2,1)S(1)}, u32[]{:S(2)}, u32[]{:S(2)}) collective-permute-start(bf16[248,128]{1,0:T(8,128)(2,1)S(1)} %get-tuple-element.104), channel_id=1, source_target_pairs={{0,24},{8,16},{16,8},{24,0},{1,25},{9,17},{17,9},{25,1},{2,26},{10... | collective-permute-start | bytes 190472 | tf_op jit(solution)/shard_map/ppermute | solution.py:915
  45.1 6.3 %collective-permute-start.14 = (bf16[248,128]{1,0:T(8,128)(2,1)S(1)}, bf16[248,128]{1,0:T(8,128)(2,1)S(1)}, u32[]{:S(2)}, u32[]{:S(2)}) collective-permute-start(bf16[248,128]{1,0:T(8,128)(2,1)S(1)} %get-tuple-element.105), channel_id=1, source_target_pairs={{0,16},{8,24},{16,0},{24,8},{1,17},{9,25},{17,1},{25,9},{2,18},{10... | collective-permute-start | bytes 190472 | tf_op jit(solution)/shard_map/ppermute | solution.py:915
  45.6 5.8 %collective-permute-start.15 = (bf16[248,128]{1,0:T(8,128)(2,1)S(1)}, bf16[248,128]{1,0:T(8,128)(2,1)S(1)}, u32[]{:S(2)}, u32[]{:S(2)}) collective-permute-start(bf16[248,128]{1,0:T(8,128)(2,1)S(1)} %get-tuple-element.106), channel_id=1, source_target_pairs={{0,8},{8,0},{16,24},{24,16},{1,9},{9,1},{17,25},{25,17},{2,10},{10... | collective-permute-start | bytes 190472 | tf_op jit(solution)/shard_map/ppermute | solution.py:915
